TPU v7x, 32 devices: a whole 2x2x4 slice. The times are simulated.
32 devices in a mesh: groups: 2 (over y), frame: 4 (over z), head: 2 (over x), rep: 2 (over core).
Axes of the slice: x: 2, y: 2, z: 4, core: 2. Of those that a mesh axis runs over, the one named last changes fastest.
Arguments:
- latents: bfloat16 [4096, 1536], P(('groups', 'frame')), parts along dimension 0, may hold values from -6 to 6
- modulation: float32 [6, 1536], P('groups'), parts along dimension 0, may hold values from -3 to 3
- key_cache: bfloat16 [4096, 1024], P(('groups', 'frame'), ('head', 'rep')), parts along dimension 0, may hold values from -310 to 310
- value_cache: bfloat16 [4096, 1024], P(('groups', 'frame'), ('head', 'rep')), parts along dimension 0, may hold values from -5 to 5
- block_worker: int32 [32], P(('groups', 'frame')), parts along dimension 0, may hold values from -1 to 3, as said below
- query_weight: bfloat16 [1536, 1024], P(None, ('head', 'rep')), may hold values from -0.3125 to 0.3125
- key_weight: bfloat16 [1536, 1024], P(None, ('head', 'rep')), may hold values from -0.15625 to 0.15625
- value_weight: bfloat16 [1536, 1024], P(None, ('head', 'rep')), may hold values from -0.15625 to 0.15625
- out_weight: bfloat16 [1024, 1536], P(('head', 'rep')), may hold values from -0.75 to 0.75
Outputs:
- update: float32 [4096, 1536], P(('groups', 'frame', 'head', 'rep')), parts along dimension 0
There are 2 independent parts, one for each index of `groups`. A program takes and returns all parts, laid end to end along the dimension named above; an argument that names none is the same for every part. Nothing has to cross between parts.
Inputs may be any that keep to these rules, and one draw needn't show every extreme that they name: `block_worker`: exactly 4 blocks hold a worker number; each number 0 to 3 is held by exactly one block, the other blocks hold -1.
All inputs are finite; a program needn't handle non-finite values.
Results may differ from a plain program's by a relative error of at most 0.0095.
The roundings to bfloat16 on the way count: a program that leaves them out, or rounds other values in their place, can miss the bound.
Values may be sent and summed in bfloat16 or wider, within the bound.
No kernel may reach another device: no remote copies, remote signals or barrier semaphores. Data moves between devices by JAX's collectives and lax.ppermute only.
A program may use at most 64 MiB of HBM per device.

v0:
```python
import math

import jax
import jax.numpy as jnp
from jax import lax
from jax.sharding import PartitionSpec as P

HD = 128


def normalize(latents, modulation):
    floats = latents.astype(jnp.float32)
    center = floats - jnp.mean(floats, axis=-1, keepdims=True)
    spread = jnp.mean(center * center, axis=-1, keepdims=True)
    return (center * lax.rsqrt(spread + 1e-06) * (1.0 + modulation[1]) + modulation[0]).astype(
        jnp.bfloat16
    )


def start_state(my_queries):
    row_count, head_count, head_size = my_queries.shape
    return (
        jnp.full((head_count, row_count), -1e30, jnp.float32),
        jnp.zeros((head_count, row_count), jnp.float32),
        jnp.zeros((head_count, row_count, head_size), jnp.float32),
    )


def fold_keys(running, shard_piece, my_queries):
    key_rows, value_rows = shard_piece
    length = key_rows.shape[0]
    block_len = math.gcd(length, 1024)
    head_count = my_queries.shape[1]
    head_size = my_queries.shape[2]
    key_blocks = key_rows.reshape(length // block_len, block_len, head_count, head_size)
    value_blocks = value_rows.reshape(length // block_len, block_len, head_count, head_size)

    def advance(carried, piece_pair):
        highest, totals, summed = carried
        key_part, value_part = piece_pair
        scores = jnp.einsum(
            "qhd,khd->hqk", my_queries, key_part, preferred_element_type=jnp.float32
        )
        new_high = jnp.maximum(highest, jnp.max(scores, axis=-1))
        rescale = jnp.exp(highest - new_high)
        weights = jnp.exp(scores - new_high[..., None])
        totals = totals * rescale + jnp.sum(weights, axis=-1)
        summed = summed * rescale[..., None] + jnp.einsum(
            "hqk,khd->hqd",
            weights.astype(jnp.bfloat16),
            value_part,
            preferred_element_type=jnp.float32,
        )
        return ((new_high, totals, summed), None)

    return lax.scan(advance, running, (key_blocks, value_blocks))[0]


def finish(carried):
    highest, totals, summed = carried
    result = summed / totals[..., None]
    head_count, row_count, head_size = result.shape
    return (
        jnp.transpose(result, (1, 0, 2))
        .reshape(row_count, head_count * head_size)
        .astype(jnp.bfloat16)
    )


def per_device(
    latents,
    modulation,
    key_cache,
    value_cache,
    block_worker,
    query_weight,
    key_weight,
    value_weight,
    out_weight,
):
    normed = normalize(latents, modulation)
    local_rows = latents.shape[0]
    block_rows = local_rows // block_worker.shape[0]
    inner_width = query_weight.shape[1]
    head_size = HD
    head_count = inner_width // head_size
    row_flags = jnp.repeat(block_worker >= 0, block_rows)[:, None]
    fresh_keys = jnp.dot(normed, key_weight, preferred_element_type=jnp.float32).astype(
        jnp.bfloat16
    )
    fresh_values = jnp.dot(normed, value_weight, preferred_element_type=jnp.float32).astype(
        jnp.bfloat16
    )
    key_rows = jnp.where(row_flags, fresh_keys, key_cache)
    value_rows = jnp.where(row_flags, fresh_values, value_cache)
    queries = (
        jnp.dot(normed, query_weight, preferred_element_type=jnp.float32) * head_size ** (-0.5)
    ).astype(jnp.bfloat16)
    my_queries = queries.reshape(local_rows, head_count, head_size)
    attended = finish(
        fold_keys(
            start_state(my_queries),
            (
                lax.all_gather(key_rows, "frame", axis=0, tiled=True),
                lax.all_gather(value_rows, "frame", axis=0, tiled=True),
            ),
            my_queries,
        )
    )
    attended = jnp.where(row_flags, attended, jnp.zeros_like(attended))
    mixed = lax.psum_scatter(
        jnp.dot(attended, out_weight, preferred_element_type=jnp.float32).astype(jnp.bfloat16),
        ("head", "rep"),
        scatter_dimension=0,
        tiled=True,
    ).astype(jnp.float32)
    return mixed * modulation[2]


def solution(mesh):
    in_specs = (
        P(("groups", "frame"), None),
        P("groups", None),
        P(("groups", "frame"), ("head", "rep")),
        P(("groups", "frame"), ("head", "rep")),
        P(("groups", "frame")),
        P(None, ("head", "rep")),
        P(None, ("head", "rep")),
        P(None, ("head", "rep")),
        P(("head", "rep"), None),
    )
    out_specs = P(("groups", "frame", "head", "rep"), None)
    return jax.shard_map(
        per_device, mesh=mesh, in_specs=in_specs, out_specs=out_specs, check_vma=False
    )
```

profile of v0, /device:TPU:0, one launch (start us, length us, event | category | flops | bytes accessed | tf_op | source)
XLA Modules:
  0.0 122.3 jit_solution(11308938002825389943)
XLA Ops:
  6.5 0.8 broadcast_compare_fusion
  7.4 0.1 broadcast_bitcast_fusion
  7.4 1.8 %convert_reduce_fusion = f32[512]{0:T(512)S(1)} fusion(bf16[512,1536]{1,0:T(8,128)(2,1)} %param.11), kind=kLoop, calls=%fused_computation.20 | loop fusion | flops 1572352 | bytes 1574912 | tf_op jit(solution)/shard_map/reduce_sum | solution.py:13
  9.2 2.0 %fusion.14 = f32[512]{0:T(512)S(1)} fusion(bf16[512,1536]{1,0:T(8,128)(2,1)} %param.11, f32[512]{0:T(512)S(1)} %broadcast_multiply_fusion), kind=kLoop, calls=%fused_computation.23 | loop fusion | flops 3145216 | bytes 1576960 | tf_op jit(solution)/shard_map/reduce_sum | solution.py:14
  11.2 0.1 slice_reduce_fusion
  11.3 0.6 fusion.17
  11.9 1.1 copy-done.2
  13.1 1.3 %fusion.20 = bf16[512,256]{1,0:T(8,128)(2,1)} fusion(bf16[512,256]{1,0:T(8,128)(2,1)S(1)} %copy-done.6, bf16[512,1536]{1,0:T(8,128)(2,1)S(1)} %fusion.17, bf16[1536,256]{1,0:T(8,128)(2,1)S(1)} %copy-done.5, pred[512]{0:T(512)(128)(4,1)S(1)} %broadcast_bitcast_fusion), kind=kOutput, calls=%fused_computation.33 | convolution fusion | flops 402915328 | bytes 2884096 | tf_op jit(solution)/shard_map/dot_general | solution.py:91
  14.4 0.0 all-gather.5.cloned.1.call-update
  14.4 0.0 all-gather.3.cloned.1.call-start
  14.5 3.0 %fusion.19 = bf16[512,256]{1,0:T(8,128)(2,1)} fusion(bf16[512,256]{1,0:T(8,128)(2,1)S(1)} %copy-done.7, bf16[512,1536]{1,0:T(8,128)(2,1)} %copy-done.2, bf16[1536,256]{1,0:T(8,128)(2,1)} %param.17, pred[512]{0:T(512)(128)(4,1)S(1)} %broadcast_bitcast_fusion), kind=kOutput, calls=%fused_computation.32 | convolution fusion | flops 402915328 | bytes 2884096 | tf_op jit(solution)/shard_map/dot_general | solution.py:88
  17.4 0.0 all-gather.3.cloned.1.call-update
  17.5 0.0 reduce-scatter.2.cloned.1.call-start
  17.6 1.8 %fusion.18 = bf16[512,256]{0,1:T(8,128)(2,1)S(1)} fusion(bf16[512,1536]{1,0:T(8,128)(2,1)S(1)} %copy-done.3, bf16[1536,256]{1,0:T(8,128)(2,1)} %param.16), kind=kOutput, calls=%fused_computation.31 | convolution fusion | flops 402915328 | bytes 2621440 | tf_op jit(solution)/shard_map/dot_general | solution.py:97
  19.3 0.8 copy.12
  20.1 25.0 %all-gather.5.cloned.1.call-done = bf16[2048,256]{1,0:T(8,128)(2,1)} async-done(((bf16[512,256]{1,0:T(8,128)(2,1)}), bf16[2048,256]{1,0:T(8,128)(2,1)}) %all-gather.5.cloned.1.call-update) | async-done | bytes 1048592 | tf_op jit(solution)/shard_map/all_gather | solution.py:105
  45.2 1.3 %reshape.29 = bf16[2,1024,2,128]{3,2,1,0:T(2,128)(2,1)S(1)} reshape(bf16[2048,256]{1,0:T(8,128)(2,1)} %all-gather.5.cloned.1.call-done) | data formatting | bytes 2097152 | tf_op jit(solution)/shard_map/reshape | solution.py:36
  46.5 27.7 %all-gather.3.cloned.1.call-done = bf16[2048,256]{1,0:T(8,128)(2,1)} async-done(((bf16[512,256]{1,0:T(8,128)(2,1)}), bf16[2048,256]{1,0:T(8,128)(2,1)}) %all-gather.3.cloned.1.call-update) | async-done | bytes 1048592 | tf_op jit(solution)/shard_map/all_gather | solution.py:104
  74.2 1.3 %reshape.27 = bf16[2,1024,2,128]{3,2,1,0:T(2,128)(2,1)S(1)} reshape(bf16[2048,256]{1,0:T(8,128)(2,1)} %all-gather.3.cloned.1.call-done) | data formatting | bytes 2097152 | tf_op jit(solution)/shard_map/reshape | solution.py:35
  75.6 8.6 %while.15 = (s32[]{:T(128)}, f32[2,512]{1,0:T(2,128)S(1)}, f32[2,512]{1,0:T(2,128)S(1)}, f32[2,512,128]{2,1,0:T(8,128)S(1)}, bf16[2,1024,2,128]{3,2,1,0:T(2,128)...) while((s32[]{:T(128)}, f32[2,512]{1,0:T(2,128)S(1)}, ...), condition=%wide.region_5.6_spmd.clone, body=%wide.region_2.5_spmd.clone.sunk | while | flops 542512128 | bytes 17105012 | solution.py:56
  75.6 0.7 constant_dynamic-slice_fusion.3
  76.3 1.7 %bitcast_reduce_fusion.2 = (f32[2,512]{1,0:T(2,128)S(1)}, f32[2,1024,512]{2,1,0:T(8,128)S(1)}) fusion(bf16[512,2,128]{2,0,1:T(8,128)(2,1)} %get-tuple-element.177, bf16[1,1024,2,128]{3,2,1,0:T(2,128)(2,1)S(1)} %get-tuple-element.148), kind=kOutput, calls=%fused_computation.1.clone.1 | convolution fusion | flops 269483008 | bytes 4984832 | tf_op jit(solution)/shard_map/while/body/eval_jaxpr/qhd,khd->hqk/dot_general | solution.py:41
  78.0 0.6 fusion.45
  78.6 1.2 %fusion.47 = f32[2,512,128]{2,1,0:T(8,128)S(1)} fusion(f32[2,1024,512]{2,1,0:T(8,128)S(1)} %get-tuple-element.150, f32[2,512]{1,0:T(2,128)S(1)} %fusion.44, bf16[1,1024,2,128]{3,2,1,0:T(2,128)(2,1)S(1)} %get-tuple-element.152, f32[2,512,128]{2,1,0:T(8,128)S(1)} %get-tuple-element.166, f32[2,512]{1,0:T(2,128)S(1)} %get-tuple-element.153, pred[]{:T(512)S(6)} %compare.3), kind=kOutput, calls=%fused_computation.7.clone.1 | convolution fusion | flops 270925824 | bytes 5775361 | tf_op jit(solution)/shard_map/while/body/eval_jaxpr/hqk,khd->hqd/dot_general | solution.py:48
  79.8 0.7 constant_dynamic-slice_fusion.3
  80.6 1.7 %bitcast_reduce_fusion.2 = (f32[2,512]{1,0:T(2,128)S(1)}, f32[2,1024,512]{2,1,0:T(8,128)S(1)}) fusion(bf16[512,2,128]{2,0,1:T(8,128)(2,1)} %get-tuple-element.177, bf16[1,1024,2,128]{3,2,1,0:T(2,128)(2,1)S(1)} %get-tuple-element.148), kind=kOutput, calls=%fused_computation.1.clone.1 | convolution fusion | flops 269483008 | bytes 4984832 | tf_op jit(solution)/shard_map/while/body/eval_jaxpr/qhd,khd->hqk/dot_general | solution.py:41
  82.3 0.6 fusion.45
  82.9 1.2 %fusion.47 = f32[2,512,128]{2,1,0:T(8,128)S(1)} fusion(f32[2,1024,512]{2,1,0:T(8,128)S(1)} %get-tuple-element.150, f32[2,512]{1,0:T(2,128)S(1)} %fusion.44, bf16[1,1024,2,128]{3,2,1,0:T(2,128)(2,1)S(1)} %get-tuple-element.152, f32[2,512,128]{2,1,0:T(8,128)S(1)} %get-tuple-element.166, f32[2,512]{1,0:T(2,128)S(1)} %get-tuple-element.153, pred[]{:T(512)S(6)} %compare.3), kind=kOutput, calls=%fused_computation.7.clone.1 | convolution fusion | flops 270925824 | bytes 5775361 | tf_op jit(solution)/shard_map/while/body/eval_jaxpr/hqk,khd->hqd/dot_general | solution.py:48
  84.1 1.9 %convolution_convert_fusion = bf16[512,1536]{1,0:T(8,128)(2,1)} fusion(bf16[256,1536]{1,0:T(8,128)(2,1)S(1)} %copy-done, pred[512]{0:T(512)(128)(4,1)S(1)} %broadcast_bitcast_fusion, f32[2,512,128]{2,1,0:T(8,128)S(1)} %get-tuple-element.43, f32[2,512]{1,0:T(2,128)S(1)} %get-tuple-element.44), kind=kOutput, calls=%fused_computation.27 | convolution fusion | flops 403832832 | bytes 2888192 | tf_op jit(solution)/shard_map/dot_general | solution.py:112
  86.0 0.0 reduce-scatter.2.cloned.1.call-update
  86.0 27.8 %reduce-scatter.2.cloned.1.call-done = bf16[128,1536]{1,0:T(8,128)(2,1)} async-done(((bf16[512,1536]{1,0:T(8,128)(2,1)}), bf16[128,1536]{1,0:T(8,128)(2,1)}) %reduce-scatter.2.cloned.1.call-update) | async-done | bytes 393232 | tf_op jit(solution)/shard_map/reduce_scatter | solution.py:111
  113.8 2.0 %convert_multiply_fusion = f32[128,1536]{1,0:T(8,128)} fusion(bf16[128,1536]{1,0:T(8,128)(2,1)} %reduce-scatter.2.cloned.1.call-done, f32[1536]{0:T(1024)S(1)} %get-tuple-element.76), kind=kLoop, calls=%fused_computation.34 | loop fusion | flops 393216 | bytes 1185792 | tf_op jit(solution)/shard_map/mul | solution.py:117
  (27 shorter events, 0.1 us)
Async XLA Ops:
  6.5 77.6 %copy-start = (bf16[256,1536]{1,0:T(8,128)(2,1)S(1)}, bf16[256,1536]{1,0:T(8,128)(2,1)}, u32[]{:S(2)}) copy-start(bf16[256,1536]{1,0:T(8,128)(2,1)} %param.19) | copy-start | bytes 2359300
  6.5 4.7 %copy-start.1 = (bf16[512,1536]{1,0:T(8,128)(2,1)S(1)}, bf16[512,1536]{1,0:T(8,128)(2,1)}, u32[]{:S(2)}) copy-start(bf16[512,1536]{1,0:T(8,128)(2,1)} %param.11) | copy-start | bytes 4718596
  6.5 4.7 %copy-start.4 = (f32[3,1536]{1,0:T(4,128)S(1)}, f32[3,1536]{1,0:T(4,128)}, u32[]{:S(2)}) copy-start(f32[3,1536]{1,0:T(4,128)} %param.12) | copy-start | bytes 55300
  6.5 38.6 %all-gather.5.cloned.1.call-start = ((), (), s32[]{:S(2)}) async-start(), calls=%async_computation.2 | async-start | bytes 1310720 | tf_op jit(solution)/shard_map/all_gather | solution.py:105
  7.4 5.6 %copy-start.5 = (bf16[1536,256]{1,0:T(8,128)(2,1)S(1)}, bf16[1536,256]{1,0:T(8,128)(2,1)}, u32[]{:S(2)}) copy-start(bf16[1536,256]{1,0:T(8,128)(2,1)} %param.18) | copy-start | bytes 2359300
  7.4 5.6 %copy-start.6 = (bf16[512,256]{1,0:T(8,128)(2,1)S(1)}, bf16[512,256]{1,0:T(8,128)(2,1)}, u32[]{:S(2)}) copy-start(bf16[512,256]{1,0:T(8,128)(2,1)} %param.14) | copy-start | bytes 786436
  11.9 1.2 copy-start.2
  13.1 1.4 %copy-start.7 = (bf16[512,256]{1,0:T(8,128)(2,1)S(1)}, bf16[512,256]{1,0:T(8,128)(2,1)}, u32[]{:S(2)}) copy-start(bf16[512,256]{1,0:T(8,128)(2,1)} %param.13) | copy-start | bytes 786436
  14.4 3.2 %copy-start.3 = (bf16[512,1536]{1,0:T(8,128)(2,1)S(1)}, bf16[512,1536]{1,0:T(8,128)(2,1)}, u32[]{:S(2)}) copy-start(bf16[512,1536]{1,0:T(8,128)(2,1)} %copy-done.2) | copy-start | bytes 4718596
  14.4 59.8 %all-gather.3.cloned.1.call-start = ((), (), s32[]{:S(2)}) async-start(), calls=%async_computation.1 | async-start | bytes 1310720 | tf_op jit(solution)/shard_map/all_gather | solution.py:104
  17.5 96.4 %reduce-scatter.2.cloned.1.call-start = ((), (), s32[]{:S(2)}) async-start(), calls=%async_computation.3 | async-start | bytes 1966080 | tf_op jit(solution)/shard_map/reduce_scatter | solution.py:111
Sparse Core Ops, SparseCore 0:
  14.5 30.6 all-gather.4
  46.7 27.4 all-gather.2
  86.1 27.6 reduce-scatter.1
where the time goes:
time: 123 us; the launch traced here: 122 us
  waiting for transfers between devices  80.6 us (66%)
  matrix products  13.7 us (11%)
  between operations  13.2 us (11%)
  other arithmetic  8.43 us (7%)
  local copies, waits for them, and re-layouts  6.21 us (5%)
    reduce_scatter x1, waiting for transfers between devices, per_device(): lax.psum_scatter(jnp.dot(attended, out_weight, preferred_element_type=jnp...  27.8 us
    all_gather x1, waiting for transfers between devices, per_device(): lax.all_gather(key_rows, 'frame', axis=0, tiled=True)  27.7 us
    all_gather x1, waiting for transfers between devices, per_device(): lax.all_gather(value_rows, 'frame', axis=0, tiled=True)  25 us
    dot_general x2, matrix products, advance(): jnp.einsum('qhd,khd->hqk', my_queries, key_part, preferred_element_type=j...  3.35 us
    dot_general x1, matrix products, per_device(): jnp.dot(normed, key_weight, preferred_element_type=jnp.float32)  2.99 us
  transfers between devices with their start and end apart: 3, of which 3 were waited for; matrix products, arithmetic and copies ran while one was open for 6% of the time, Pallas kernels for 0%

commit v1 on v0

v1 whole, which is shorter than its diff:
```python
import functools

import jax
import jax.numpy as jnp
from jax import lax
from jax.experimental import pallas as pl
from jax.experimental.pallas import tpu as pltpu
from jax.sharding import PartitionSpec as P

HD = 128
EPS = 1e-06
CHUNK = 32
TAIL = 16
MIB = 1 << 20

VMEM = pl.BlockSpec(memory_space=pltpu.VMEM)
SMEM = pl.BlockSpec(memory_space=pltpu.SMEM)


def normalize_active(worker_ref, latents_ref, modulation_ref, normed_ref, block_rows):
    gain = 1.0 + modulation_ref[1:2, :]
    shift = modulation_ref[0:1, :]

    def one_block(j, carry):
        @pl.when(worker_ref[j] >= 0)
        def _():
            def one_chunk(c, inner):
                start = pl.multiple_of(j * block_rows + c * CHUNK, CHUNK)
                floats = latents_ref[pl.ds(start, CHUNK), :].astype(jnp.float32)
                center = floats - jnp.mean(floats, axis=-1, keepdims=True)
                spread = jnp.mean(center * center, axis=-1, keepdims=True)
                normed_ref[pl.ds(start, CHUNK), :] = (
                    center * lax.rsqrt(spread + EPS) * gain + shift
                ).astype(jnp.bfloat16)
                return inner

            lax.fori_loop(0, block_rows // CHUNK, one_chunk, 0)

        return carry

    lax.fori_loop(0, worker_ref.shape[0], one_block, 0)


def query_kernel(n_frame, worker_ref, latents_ref, modulation_ref, weight_ref, *rest):
    outs, (normed_ref, queries_ref) = rest[:n_frame], rest[n_frame:]
    n_local = worker_ref.shape[0]
    block_rows = latents_ref.shape[0] // n_local
    frame = lax.axis_index("frame")
    normalize_active(worker_ref, latents_ref, modulation_ref, normed_ref, block_rows)
    queries_ref[...] = (
        jnp.dot(normed_ref[...], weight_ref[...], preferred_element_type=jnp.float32) * HD ** (-0.5)
    ).astype(jnp.bfloat16)
    for s in range(n_frame):
        outs[s][...] = jnp.zeros_like(outs[s])
    for j in range(n_local):
        worker = worker_ref[j]
        away = lax.rem(worker - frame + n_frame, n_frame)
        for s in range(n_frame):

            @pl.when((worker >= 0) & (away == s))
            def _():
                outs[s][...] = queries_ref[j * block_rows : (j + 1) * block_rows, :]


def key_value_kernel(
    worker_ref,
    latents_ref,
    modulation_ref,
    key_weight_ref,
    value_weight_ref,
    key_cache_ref,
    value_cache_ref,
    keys_ref,
    values_t_ref,
    normed_ref,
):
    n_local = worker_ref.shape[0]
    block_rows = latents_ref.shape[0] // n_local
    normalize_active(worker_ref, latents_ref, modulation_ref, normed_ref, block_rows)
    for j in range(n_local):
        rows = slice(j * block_rows, (j + 1) * block_rows)

        @pl.when(worker_ref[j] >= 0)
        def _():
            normed = normed_ref[rows, :]
            keys_ref[rows, :] = jnp.dot(
                normed, key_weight_ref[...], preferred_element_type=jnp.float32
            ).astype(jnp.bfloat16)
            values_t_ref[:, rows] = (
                jnp.dot(normed, value_weight_ref[...], preferred_element_type=jnp.float32)
                .astype(jnp.bfloat16)
                .T
            )

        @pl.when(worker_ref[j] < 0)
        def _():
            keys_ref[rows, :] = key_cache_ref[rows, :]
            values_t_ref[:, rows] = value_cache_ref[rows, :].T


def three_terms(x):
    first = x.astype(jnp.bfloat16).astype(jnp.float32)
    rest = x - first
    second = rest.astype(jnp.bfloat16).astype(jnp.float32)
    return [first, second, rest - second]


def attend_kernel(queries_ref, keys_ref, values_t_ref, out_ref):
    width = keys_ref.shape[1]
    stats = []
    for h in range(width // HD):
        cols = slice(h * HD, (h + 1) * HD)
        scores = lax.dot_general(
            keys_ref[:, cols],
            queries_ref[:, cols],
            (((1,), (1,)), ((), ())),
            preferred_element_type=jnp.float32,
        )
        highest = jnp.max(scores, axis=0, keepdims=True)
        weights = jnp.exp(scores - highest)
        total = jnp.sum(weights, axis=0, keepdims=True)
        out_ref[cols, :] = jnp.dot(
            values_t_ref[cols, :], weights.astype(jnp.bfloat16), preferred_element_type=jnp.float32
        ).astype(jnp.bfloat16)
        stats += three_terms(highest) + three_terms(total)
    shape = (out_ref.shape[0] - width, out_ref.shape[1])
    row = lax.broadcasted_iota(jnp.int32, shape, 0)
    tail = jnp.zeros(shape, jnp.float32)
    for i, stat in enumerate(stats):
        tail = jnp.where(row == i, stat, tail)
    out_ref[width:, :] = tail.astype(jnp.bfloat16)


def combine_kernel(*refs):
    parts, out_ref = refs[:-1], refs[-1]
    width = out_ref.shape[1]
    tails = [part[width:, :].astype(jnp.float32) for part in parts]
    for h in range(width // HD):
        cols = slice(h * HD, (h + 1) * HD)

        def stat(tail, at):
            at += 6 * h
            return tail[at : at + 1, :] + tail[at + 1 : at + 2, :] + tail[at + 2 : at + 3, :]

        maxima = [stat(tail, 0) for tail in tails]
        highest = functools.reduce(jnp.maximum, maxima)
        factors = [jnp.exp(m - highest) for m in maxima]
        total = sum(stat(tail, 3) * factor for tail, factor in zip(tails, factors))
        summed = sum(
            part[cols, :].astype(jnp.float32) * factor for part, factor in zip(parts, factors)
        )
        out_ref[:, cols] = (summed / total).T.astype(jnp.bfloat16)


def select_kernel(n_frame, n_head, n_rep, worker_ref, *refs):
    slots, outs = refs[:n_frame], refs[n_frame:]
    block_rows = slots[0].shape[0]
    rows = outs[0].shape[0]
    frame = lax.axis_index("frame")
    head = lax.axis_index("head")
    rep = lax.axis_index("rep")
    for d in range(n_head * n_rep):
        target_head = lax.rem(head + d // n_rep, n_head)
        target = target_head * n_rep + lax.rem(rep + d % n_rep, n_rep)
        start = target * rows
        worker = worker_ref[start // block_rows]
        offset = pl.multiple_of(lax.rem(start, block_rows), rows)
        away = lax.rem(frame - worker + n_frame, n_frame)

        @pl.when(worker < 0)
        def _():
            outs[d][...] = jnp.zeros_like(outs[d])

        for s in range(n_frame):

            @pl.when((worker >= 0) & (away == s))
            def _():
                outs[d][...] = slots[s][pl.ds(offset, rows), :]


def project_kernel(n_rep, worker_ref, modulation_ref, *refs):
    refs, out_ref = refs[:-1], refs[-1]
    parts, weights = refs[: len(refs) // 2], refs[len(refs) // 2 :]
    rows, width = out_ref.shape
    n_devices = len(parts)
    block_rows = rows * n_devices // worker_ref.shape[0]
    place = lax.axis_index("head") * n_rep + lax.axis_index("rep")
    worker = worker_ref[place * rows // block_rows]

    @pl.when(worker >= 0)
    def _():
        step = 512
        for start in range(0, width, step):
            cols = slice(start, start + step)
            total = sum(
                jnp.dot(part[...], weight[:, cols], preferred_element_type=jnp.float32)
                for part, weight in zip(parts, weights)
            )
            out_ref[:, cols] = total * modulation_ref[2:3, cols]

    @pl.when(worker < 0)
    def _():
        out_ref[...] = jnp.zeros_like(out_ref)


def params(mib):
    return pltpu.CompilerParams(vmem_limit_bytes=mib * MIB)


def cost(flops, moved, exps=0):
    return pl.CostEstimate(flops=flops, bytes_accessed=moved, transcendentals=exps)


def per_device(
    n_frame,
    n_head,
    n_rep,
    latents,
    modulation,
    key_cache,
    value_cache,
    block_worker,
    query_weight,
    key_weight,
    value_weight,
    out_weight,
):
    tokens, model = latents.shape
    n_local = block_worker.shape[0]
    block_rows = tokens // n_local
    width = query_weight.shape[1]
    n_place = n_head * n_rep
    own_rows = tokens // n_place
    tail = TAIL * -(-6 * (width // HD) // TAIL)
    half = jnp.bfloat16

    def along_frame(x, shift):
        return lax.ppermute(x, "frame", [(i, (i + shift) % n_frame) for i in range(n_frame)])

    def along_head(x, shift):
        return lax.ppermute(x, "head", [(i, (i + shift) % n_head) for i in range(n_head)])

    def along_rep(x, shift):
        return lax.ppermute(x, "rep", [(i, (i + shift) % n_rep) for i in range(n_rep)])

    def in_frame(x, d):
        pairs = []
        for h in range(n_head):
            for r in range(n_rep):
                to = ((h + d // n_rep) % n_head) * n_rep + (r + d % n_rep) % n_rep
                pairs.append((h * n_rep + r, to))
        return lax.ppermute(x, ("head", "rep"), pairs)

    slots = pl.pallas_call(
        functools.partial(query_kernel, n_frame),
        out_shape=[jax.ShapeDtypeStruct((block_rows, width), half)] * n_frame,
        in_specs=[SMEM, VMEM, VMEM, VMEM],
        out_specs=[VMEM] * n_frame,
        scratch_shapes=[pltpu.VMEM((tokens, model), half), pltpu.VMEM((tokens, width), half)],
        compiler_params=params(20),
        cost_estimate=cost(2 * tokens * model * width, 2 * tokens * model + 2 * model * width),
        name="queries",
    )(block_worker, latents, modulation, query_weight)
    mine = slots[0]
    for s in range(1, n_frame):
        mine = mine + along_frame(slots[s], s)

    keys, values_t = pl.pallas_call(
        key_value_kernel,
        out_shape=[
            jax.ShapeDtypeStruct((tokens, width), half),
            jax.ShapeDtypeStruct((width, tokens), half),
        ],
        in_specs=[SMEM] + [VMEM] * 6,
        out_specs=[VMEM, VMEM],
        scratch_shapes=[pltpu.VMEM((tokens, model), half)],
        compiler_params=params(20),
        cost_estimate=cost(4 * tokens * model * width, 2 * tokens * model + 4 * model * width),
        name="keys_values",
    )(block_worker, latents, modulation, key_weight, value_weight, key_cache, value_cache)

    attend = pl.pallas_call(
        attend_kernel,
        out_shape=jax.ShapeDtypeStruct((width + tail, block_rows), half),
        in_specs=[VMEM] * 3,
        out_specs=VMEM,
        compiler_params=params(20),
        cost_estimate=cost(
            4 * tokens * block_rows * width, 4 * tokens * width, tokens * block_rows * width // HD
        ),
        name="attend",
    )
    shared = [mine] + [along_frame(mine, s) for s in range(1, n_frame)]
    partial = [attend(queries, keys, values_t) for queries in shared]
    gathered = partial[:1] + [along_frame(partial[s], n_frame - s) for s in range(1, n_frame)]
    attended = pl.pallas_call(
        combine_kernel,
        out_shape=jax.ShapeDtypeStruct((block_rows, width), half),
        in_specs=[VMEM] * n_frame,
        out_specs=VMEM,
        compiler_params=params(20),
        cost_estimate=cost(4 * n_frame * block_rows * width, 2 * n_frame * block_rows * width),
        name="combine",
    )(*gathered)
    copies = [attended] + [along_frame(attended, s) for s in range(1, n_frame)]
    pieces = pl.pallas_call(
        functools.partial(select_kernel, n_frame, n_head, n_rep),
        out_shape=[jax.ShapeDtypeStruct((own_rows, width), half)] * n_place,
        in_specs=[SMEM] + [VMEM] * n_frame,
        out_specs=[VMEM] * n_place,
        compiler_params=params(20),
        cost_estimate=cost(0, 4 * n_frame * block_rows * width),
        name="select",
    )(block_worker, *copies)
    pieces = [pieces[0]] + [in_frame(pieces[d], d) for d in range(1, n_place)]

    weights = []
    for dh in range(n_head):
        across = along_head(out_weight, dh) if dh else out_weight
        for dr in range(n_rep):
            weights.append(along_rep(across, dr) if dr else across)
    return pl.pallas_call(
        functools.partial(project_kernel, n_rep),
        out_shape=jax.ShapeDtypeStruct((own_rows, model), jnp.float32),
        in_specs=[SMEM] + [VMEM] * (1 + 2 * n_place),
        out_specs=VMEM,
        compiler_params=params(20),
        cost_estimate=cost(2 * own_rows * model * width * n_place, 2 * model * width * n_place),
        name="project",
    )(block_worker, modulation, *pieces, *weights)


def solution(mesh):
    in_specs = (
        P(("groups", "frame"), None),
        P("groups", None),
        P(("groups", "frame"), ("head", "rep")),
        P(("groups", "frame"), ("head", "rep")),
        P(("groups", "frame")),
        P(None, ("head", "rep")),
        P(None, ("head", "rep")),
        P(None, ("head", "rep")),
        P(("head", "rep"), None),
    )
    out_specs = P(("groups", "frame", "head", "rep"), None)
    body = functools.partial(
        per_device, mesh.shape["frame"], mesh.shape["head"], mesh.shape["rep"]
    )
    return jax.shard_map(body, mesh=mesh, in_specs=in_specs, out_specs=out_specs, check_vma=False)
```

time: 123 us -> 76.3 us (0.62)
  waiting for transfers between devices: 80.6 us -> 41.7 us
  starting transfers between devices: 0.09 us -> 22.8 us
  matrix products: 13.7 us -> 0 us
  between operations: 13.2 us -> 0.14 us
  other arithmetic: 8.43 us -> 0.02 us
  Pallas kernels: 0 us -> 7.46 us
  local copies, waits for them, and re-layouts: 6.21 us -> 3.96 us
    all_gather x2 -> x0, waiting for transfers between devices: 52.7 us -> none  [the longest x1 27.7 us: per_device(): lax.all_gather(key_rows, 'frame', axis=0, tiled=True)]
    ppermute x0 -> x18, waiting for transfers between devices: none -> 41.7 us  [the longest x12 20.2 us: along_frame(): lax.ppermute(x, 'frame', [(i, (i + shift) % n_frame) for i in range(n_fra...]
    reduce_scatter x1 -> x0, waiting for transfers between devices: 27.8 us -> none  [per_device(): lax.psum_scatter(jnp.dot(attended, out_weight, preferred_element_type=jnp...]
    ppermute x0 -> x18, starting transfers between devices: none -> 22.8 us  [the longest x12 18 us: along_frame(): lax.ppermute(x, 'frame', [(i, (i + shift) % n_frame) for i in range(n_fra...]
    dot_general x8 -> x0, matrix products: 13.7 us -> none  [the longest x2 3.35 us: advance(): jnp.einsum('qhd,khd->hqk', my_queries, key_part, preferred_element_type=j...]
    pallas_call x0 -> x9, Pallas kernels: none -> 7.46 us  [the longest x4 2.93 us: per_device(): partial = [attend(queries, keys, values_t) for queries in shared]]
    reduce_sum x4 -> x0, other arithmetic: 4.87 us -> none  [the longest x1 1.95 us: normalize(): spread = jnp.mean(center * center, axis=-1, keepdims=True)]
    reshape x2 -> x0, local copies, waits for them, and re-layouts: 2.68 us -> none  [the longest x1 1.34 us: fold_keys(): value_rows.reshape(length // block_len, block_len, head_count, head_size)]
  transfers between devices with their start and end apart: 3 -> 18, of which waited for: 3 -> 10; matrix products, arithmetic and copies ran while one was open for 6% -> 0% of each run, Pallas kernels for 0% -> 8%
where the time goes in v1:
time: 76.3 us; the launch traced here: 76.1 us
  waiting for transfers between devices  41.7 us (55%)
  starting transfers between devices  22.8 us (30%)
  Pallas kernels  7.46 us (10%)
  local copies, waits for them, and re-layouts  3.96 us (5%)
    ppermute x12, waiting for transfers between devices, along_frame(): lax.ppermute(x, 'frame', [(i, (i + shift) % n_frame) for i in range(n_fra...  20.2 us
    ppermute x12, starting transfers between devices, along_frame(): lax.ppermute(x, 'frame', [(i, (i + shift) % n_frame) for i in range(n_fra...  18 us
    ppermute x1, waiting for transfers between devices, along_head(): lax.ppermute(x, 'head', [(i, (i + shift) % n_head) for i in range(n_head)])  17.7 us
    unnamed x20, local copies, waits for them, and re-layouts  3.96 us
    ppermute x3, waiting for transfers between devices, in_frame(): return lax.ppermute(x, ('head', 'rep'), pairs)  3.74 us
    ppermute x1, starting transfers between devices, along_head(): lax.ppermute(x, 'head', [(i, (i + shift) % n_head) for i in range(n_head)])  2.94 us
    pallas_call x4, Pallas kernels, per_device(): partial = [attend(queries, keys, values_t) for queries in shared]  2.93 us
    ppermute x3, starting transfers between devices, in_frame(): return lax.ppermute(x, ('head', 'rep'), pairs)  1.93 us
  transfers between devices with their start and end apart: 18, of which 10 were waited for; matrix products, arithmetic and copies ran while one was open for 0% of the time, Pallas kernels for 8%

profile of v1, /device:TPU:0, one launch (start us, length us, event | category | flops | bytes accessed | tf_op | source)
XLA Modules:
  0.0 76.1 jit_solution(3054492343993676681)
XLA Ops:
  0.0 2.9 %collective-permute-start.16 = (bf16[256,1536]{1,0:T(8,128)(2,1)}, bf16[256,1536]{1,0:T(8,128)(2,1)S(1)}, u32[]{:S(2)}, u32[]{:S(2)}) collective-permute-start(bf16[256,1536]{1,0:T(8,128)(2,1)} %refs_4_.1), channel_id=1, source_target_pairs={{0,2},{2,0},{1,3},{3,1},{4,6},{6,4},{5,7},{7,5},{8,10},{10,8},{9,1... | collective-permute-start | bytes 2359304 | tf_op jit(solution)/shard_map/ppermute | solution.py:241
  2.9 17.7 %collective-permute-done.16.refs_6_ = bf16[256,1536]{1,0:T(8,128)(2,1)S(1)} collective-permute-done((bf16[256,1536]{1,0:T(8,128)(2,1)}, bf16[256,1536]{1,0:T(8,128)(2,1)S(1)}, u32[]{:S(2)}, u32[]{:S(2)}) %collective-permute-start.16) | collective-permute-done | bytes 786464 | tf_op jit(solution)/shard_map/ppermute | solution.py:241
  20.7 1.4 %copy-done = bf16[512,1536]{1,0:T(8,128)(2,1)S(1)} copy-done((bf16[512,1536]{1,0:T(8,128)(2,1)S(1)}, bf16[512,1536]{1,0:T(8,128)(2,1)}, u32[]{:S(2)}) %copy-start) | copy-done | bytes 1572888
  22.1 1.1 %copy-done.2 = bf16[1536,256]{1,0:T(8,128)(2,1)S(1)} copy-done((bf16[1536,256]{1,0:T(8,128)(2,1)S(1)}, bf16[1536,256]{1,0:T(8,128)(2,1)}, u32[]{:S(2)}) %copy-start.2) | copy-done | bytes 786456
  23.2 0.7 copy-done.7
  24.0 0.7 copy-done.8
  24.6 1.3 %queries.1 = (bf16[128,256]{1,0:T(8,128)(2,1)S(1)}, bf16[128,256]{1,0:T(8,128)(2,1)S(1)}, bf16[128,256]{1,0:T(8,128)(2,1)S(1)}, bf16[128,256]{1,0:T(8,128)(2,1)S(1)}) custom-call(s32[4]{0:T(128)S(1)} %copy-done.8, bf16[512,1536]{1,0:T(8,128)(2,1)S(1)} %copy-done, f32[3,1536]{1,0:T(4,128)S(1)} %copy-done.7, bf16[1536,256]{1,0:T(8,128)(2,1)S(1)} %copy-done.2), custom_call_target="tpu_custom_call" | custom-call | flops 402653184 | bytes 2359296 | tf_op jit(solution)/shard_map/queries/pallas_call | solution.py:254
  25.9 5.4 %collective-permute-start = (bf16[128,256]{1,0:T(8,128)(2,1)S(1)}, bf16[128,256]{1,0:T(8,128)(2,1)S(1)}, u32[]{:S(2)}, u32[]{:S(2)}) collective-permute-start(bf16[128,256]{1,0:T(8,128)(2,1)S(1)} %get-tuple-element.16), channel_id=1, source_target_pairs={{0,4},{4,8},{8,12},{12,0},{1,5},{5,9},{9,13},{13,1},{2,6},{6,10},{... | collective-permute-start | bytes 196616 | tf_op jit(solution)/shard_map/ppermute | solution.py:238
  31.3 2.4 %collective-permute-start.2 = (bf16[128,256]{1,0:T(8,128)(2,1)S(1)}, bf16[128,256]{1,0:T(8,128)(2,1)S(1)}, u32[]{:S(2)}, u32[]{:S(2)}) collective-permute-start(bf16[128,256]{1,0:T(8,128)(2,1)S(1)} %get-tuple-element.18), channel_id=1, source_target_pairs={{0,12},{4,0},{8,4},{12,8},{1,13},{5,1},{9,5},{13,9},{2,14},{6,2},{... | collective-permute-start | bytes 196616 | tf_op jit(solution)/shard_map/ppermute | solution.py:238
  33.7 3.9 %collective-permute-done.1 = bf16[128,256]{1,0:T(8,128)(2,1)S(1)} collective-permute-done((bf16[128,256]{1,0:T(8,128)(2,1)S(1)}, bf16[128,256]{1,0:T(8,128)(2,1)S(1)}, u32[]{:S(2)}, u32[]{:S(2)}) %collective-permute-start.1) | collective-permute-done | bytes 65568 | tf_op jit(solution)/shard_map/ppermute | solution.py:238
  37.7 3.0 %collective-permute-start.7 = (bf16[128,256]{1,0:T(8,128)(2,1)S(1)}, bf16[128,256]{1,0:T(8,128)(2,1)S(1)}, u32[]{:S(2)}, u32[]{:S(2)}) collective-permute-start(bf16[128,256]{1,0:T(8,128)(2,1)S(1)} %add_add_fusion.queries_ref), channel_id=1, source_target_pairs={{0,12},{4,0},{8,4},{12,8},{1,13},{5,1},{9,5},{13,9},{2,14},{6,2},{... | collective-permute-start | bytes 196616 | tf_op jit(solution)/shard_map/ppermute | solution.py:238
  40.7 0.4 collective-permute-start.5
  41.4 0.9 %keys_values.1 = (bf16[512,256]{1,0:T(8,128)(2,1)S(1)}, bf16[256,512]{1,0:T(8,128)(2,1)S(1)}) custom-call(s32[4]{0:T(128)S(1)} %copy-done.8, bf16[512,1536]{1,0:T(8,128)(2,1)S(1)} %copy-done, f32[3,1536]{1,0:T(4,128)S(1)} %copy-done.7, bf16[1536,256]{1,0:T(8,128)(2,1)S(1)} %copy-done.3, bf16[1536,256]{1,0:T(8,128)(2,1)S(1)} %copy-done.4, ...), custom_call_target="tpu_custom_call" | custom-call | flops 805306368 | bytes 3145728 | tf_op jit(solution)/shard_map/keys_values/pallas_call | solution.py:268
  42.3 5.0 %collective-permute-done.3.queries_ref = bf16[128,256]{1,0:T(8,128)(2,1)S(1)} collective-permute-done((bf16[128,256]{1,0:T(8,128)(2,1)S(1)}, bf16[128,256]{1,0:T(8,128)(2,1)S(1)}, u32[]{:S(2)}, u32[]{:S(2)}) %collective-permute-start.3) | collective-permute-done | bytes 65568 | tf_op jit(solution)/shard_map/ppermute | solution.py:238
  47.3 0.7 attend.5
  48.0 0.7 collective-permute-start.4
  48.8 0.7 attend.6
  49.5 3.6 %collective-permute-start.6 = (bf16[272,128]{1,0:T(8,128)(2,1)S(1)}, bf16[272,128]{1,0:T(8,128)(2,1)S(1)}, u32[]{:S(2)}, u32[]{:S(2)}) collective-permute-start(bf16[272,128]{1,0:T(8,128)(2,1)S(1)} %attend.6), channel_id=1, source_target_pairs={{0,8},{4,12},{8,0},{12,4},{1,9},{5,13},{9,1},{13,5},{2,10},{6,14},... | collective-permute-start | bytes 208904 | tf_op jit(solution)/shard_map/ppermute | solution.py:238
  53.1 0.7 attend.7
  54.0 0.7 attend.4.refs_0_
  54.7 0.9 %collective-permute-done.6.refs_2_ = bf16[272,128]{1,0:T(8,128)(2,1)S(1)} collective-permute-done((bf16[272,128]{1,0:T(8,128)(2,1)S(1)}, bf16[272,128]{1,0:T(8,128)(2,1)S(1)}, u32[]{:S(2)}, u32[]{:S(2)}) %collective-permute-start.6) | collective-permute-done | bytes 69664 | tf_op jit(solution)/shard_map/ppermute | solution.py:238
  55.6 5.1 %collective-permute-done.8.refs_3_ = bf16[272,128]{1,0:T(8,128)(2,1)S(1)} collective-permute-done((bf16[272,128]{1,0:T(8,128)(2,1)S(1)}, bf16[272,128]{1,0:T(8,128)(2,1)S(1)}, u32[]{:S(2)}, u32[]{:S(2)}) %collective-permute-start.8) | collective-permute-done | bytes 69664 | tf_op jit(solution)/shard_map/ppermute | solution.py:238
  60.9 1.9 %collective-permute-start.9 = (bf16[128,256]{1,0:T(8,128)(2,1)S(1)}, bf16[128,256]{1,0:T(8,128)(2,1)S(1)}, u32[]{:S(2)}, u32[]{:S(2)}) collective-permute-start(bf16[128,256]{1,0:T(8,128)(2,1)S(1)} %combine.1.refs_0_), channel_id=1, source_target_pairs={{0,4},{4,8},{8,12},{12,0},{1,5},{5,9},{9,13},{13,1},{2,6},{6,10},{... | collective-permute-start | bytes 196616 | tf_op jit(solution)/shard_map/ppermute | solution.py:238
  62.9 2.2 %collective-permute-done.11.refs_3_ = bf16[128,256]{1,0:T(8,128)(2,1)S(1)} collective-permute-done((bf16[128,256]{1,0:T(8,128)(2,1)S(1)}, bf16[128,256]{1,0:T(8,128)(2,1)S(1)}, u32[]{:S(2)}, u32[]{:S(2)}) %collective-permute-start.11) | collective-permute-done | bytes 65568 | tf_op jit(solution)/shard_map/ppermute | solution.py:238
  65.1 1.0 %collective-permute-done.10.refs_2_ = bf16[128,256]{1,0:T(8,128)(2,1)S(1)} collective-permute-done((bf16[128,256]{1,0:T(8,128)(2,1)S(1)}, bf16[128,256]{1,0:T(8,128)(2,1)S(1)}, u32[]{:S(2)}, u32[]{:S(2)}) %collective-permute-start.10) | collective-permute-done | bytes 65568 | tf_op jit(solution)/shard_map/ppermute | solution.py:238
  66.1 2.1 %collective-permute-done.9.refs_1_ = bf16[128,256]{1,0:T(8,128)(2,1)S(1)} collective-permute-done((bf16[128,256]{1,0:T(8,128)(2,1)S(1)}, bf16[128,256]{1,0:T(8,128)(2,1)S(1)}, u32[]{:S(2)}, u32[]{:S(2)}) %collective-permute-start.9) | collective-permute-done | bytes 65568 | tf_op jit(solution)/shard_map/ppermute | solution.py:238
  68.2 0.7 select.1
  69.0 1.6 %collective-permute-start.13 = (bf16[128,256]{1,0:T(8,128)(2,1)S(1)}, bf16[128,256]{1,0:T(8,128)(2,1)S(1)}, u32[]{:S(2)}, u32[]{:S(2)}) collective-permute-start(bf16[128,256]{1,0:T(8,128)(2,1)S(1)} %get-tuple-element.23), channel_id=1, source_target_pairs={{0,2},{1,3},{2,0},{3,1},{4,6},{5,7},{6,4},{7,5},{8,10},{9,11},{10,... | collective-permute-start | bytes 196616 | tf_op jit(solution)/shard_map/ppermute | solution.py:252
  70.5 0.3 collective-permute-start.14
  70.8 2.6 %collective-permute-done.13.refs_2_ = bf16[128,256]{1,0:T(8,128)(2,1)S(1)} collective-permute-done((bf16[128,256]{1,0:T(8,128)(2,1)S(1)}, bf16[128,256]{1,0:T(8,128)(2,1)S(1)}, u32[]{:S(2)}, u32[]{:S(2)}) %collective-permute-start.13) | collective-permute-done | bytes 65568 | tf_op jit(solution)/shard_map/ppermute | solution.py:252
  73.5 1.1 %collective-permute-done.14.refs_3_ = bf16[128,256]{1,0:T(8,128)(2,1)S(1)} collective-permute-done((bf16[128,256]{1,0:T(8,128)(2,1)S(1)}, bf16[128,256]{1,0:T(8,128)(2,1)S(1)}, u32[]{:S(2)}, u32[]{:S(2)}) %collective-permute-start.14) | collective-permute-done | bytes 65568 | tf_op jit(solution)/shard_map/ppermute | solution.py:252
  74.6 1.5 %project.1 = f32[128,1536]{1,0:T(8,128)} custom-call(s32[4]{0:T(128)S(1)} %copy-done.9, f32[3,1536]{1,0:T(4,128)S(1)} %copy-done.7, bf16[128,256]{1,0:T(8,128)(2,1)S(1)} %get-tuple-element.21.refs_0_, bf16[128,256]{1,0:T(8,128)(2,1)S(1)} %collective-permute-done.12.refs_1_, bf16[128,256]{1,0:T(8,128)(2,1)S(1)} %collective-permute-done.13.refs_2_, ...), custom_call_target="tpu_custom_call" | custom-call | flops 402653184 | bytes 3145728 | tf_op jit(solution)/shard_map/project/pallas_call | solution.py:322
  (34 shorter events, 0.7 us)
Async XLA Ops:
  0.0 20.7 %collective-permute-start.16 = (bf16[256,1536]{1,0:T(8,128)(2,1)}, bf16[256,1536]{1,0:T(8,128)(2,1)S(1)}, u32[]{:S(2)}, u32[]{:S(2)}) collective-permute-start(bf16[256,1536]{1,0:T(8,128)(2,1)} %refs_4_.1), channel_id=1, source_target_pairs={{0,2},{2,0},{1,3},{3,1},{4,6},{6,4},{5,7},{7,5},{8,10},{10,8},{9,1... | collective-permute-start | bytes 2359304 | tf_op jit(solution)/shard_map/ppermute | solution.py:241
  2.9 71.6 %collective-permute-start.15 = (bf16[256,1536]{1,0:T(8,128)(2,1)}, bf16[256,1536]{1,0:T(8,128)(2,1)S(1)}, u32[]{:S(2)}, u32[]{:S(2)}) collective-permute-start(bf16[256,1536]{1,0:T(8,128)(2,1)} %refs_4_.1), channel_id=1, source_target_pairs={{0,1},{1,0},{2,3},{3,2},{4,5},{5,4},{6,7},{7,6},{8,9},{9,8},{10,11... | collective-permute-start | bytes 2359304 | tf_op jit(solution)/shard_map/ppermute | solution.py:244
  20.7 53.9 %collective-permute-start.17 = (bf16[256,1536]{1,0:T(8,128)(2,1)S(1)}, bf16[256,1536]{1,0:T(8,128)(2,1)S(1)}, u32[]{:S(2)}, u32[]{:S(2)}) collective-permute-start(bf16[256,1536]{1,0:T(8,128)(2,1)S(1)} %collective-permute-done.16.refs_6_), channel_id=1, source_target_pairs={{0,1},{1,0},{2,3},{3,2},{4,5},{5,4},{6,7},{7,6},{8,9},{9,8},{10,11... | collective-permute-start | bytes 2359304 | tf_op jit(solution)/shard_map/ppermute | solution.py:244
  20.7 1.4 %copy-start = (bf16[512,1536]{1,0:T(8,128)(2,1)S(1)}, bf16[512,1536]{1,0:T(8,128)(2,1)}, u32[]{:S(2)}) copy-start(bf16[512,1536]{1,0:T(8,128)(2,1)} %latents_ref.3) | copy-start | bytes 4718596
  22.1 1.1 %copy-start.2 = (bf16[1536,256]{1,0:T(8,128)(2,1)S(1)}, bf16[1536,256]{1,0:T(8,128)(2,1)}, u32[]{:S(2)}) copy-start(bf16[1536,256]{1,0:T(8,128)(2,1)} %weight_ref.1) | copy-start | bytes 2359300
  23.2 0.7 copy-start.7
  24.0 0.7 copy-start.8
  24.6 16.7 %copy-start.3 = (bf16[1536,256]{1,0:T(8,128)(2,1)S(1)}, bf16[1536,256]{1,0:T(8,128)(2,1)}, u32[]{:S(2)}) copy-start(bf16[1536,256]{1,0:T(8,128)(2,1)} %key_weight_ref.1) | copy-start | bytes 2359300
  24.6 16.7 %copy-start.4 = (bf16[1536,256]{1,0:T(8,128)(2,1)S(1)}, bf16[1536,256]{1,0:T(8,128)(2,1)}, u32[]{:S(2)}) copy-start(bf16[1536,256]{1,0:T(8,128)(2,1)} %value_weight_ref.1) | copy-start | bytes 2359300
  24.6 16.7 %copy-start.5 = (bf16[512,256]{1,0:T(8,128)(2,1)S(1)}, bf16[512,256]{1,0:T(8,128)(2,1)}, u32[]{:S(2)}) copy-start(bf16[512,256]{1,0:T(8,128)(2,1)} %key_cache_ref.1) | copy-start | bytes 786436
  24.6 16.7 %copy-start.6 = (bf16[512,256]{1,0:T(8,128)(2,1)S(1)}, bf16[512,256]{1,0:T(8,128)(2,1)}, u32[]{:S(2)}) copy-start(bf16[512,256]{1,0:T(8,128)(2,1)} %value_cache_ref.1) | copy-start | bytes 786436
  25.9 7.8 %collective-permute-start = (bf16[128,256]{1,0:T(8,128)(2,1)S(1)}, bf16[128,256]{1,0:T(8,128)(2,1)S(1)}, u32[]{:S(2)}, u32[]{:S(2)}) collective-permute-start(bf16[128,256]{1,0:T(8,128)(2,1)S(1)} %get-tuple-element.16), channel_id=1, source_target_pairs={{0,4},{4,8},{8,12},{12,0},{1,5},{5,9},{9,13},{13,1},{2,6},{6,10},{... | collective-permute-start | bytes 196616 | tf_op jit(solution)/shard_map/ppermute | solution.py:238
  31.3 6.4 %collective-permute-start.1 = (bf16[128,256]{1,0:T(8,128)(2,1)S(1)}, bf16[128,256]{1,0:T(8,128)(2,1)S(1)}, u32[]{:S(2)}, u32[]{:S(2)}) collective-permute-start(bf16[128,256]{1,0:T(8,128)(2,1)S(1)} %get-tuple-element.17), channel_id=1, source_target_pairs={{0,8},{4,12},{8,0},{12,4},{1,9},{5,13},{9,1},{13,5},{2,10},{6,14},... | collective-permute-start | bytes 196616 | tf_op jit(solution)/shard_map/ppermute | solution.py:238
  31.3 6.4 %collective-permute-start.2 = (bf16[128,256]{1,0:T(8,128)(2,1)S(1)}, bf16[128,256]{1,0:T(8,128)(2,1)S(1)}, u32[]{:S(2)}, u32[]{:S(2)}) collective-permute-start(bf16[128,256]{1,0:T(8,128)(2,1)S(1)} %get-tuple-element.18), channel_id=1, source_target_pairs={{0,12},{4,0},{8,4},{12,8},{1,13},{5,1},{9,5},{13,9},{2,14},{6,2},{... | collective-permute-start | bytes 196616 | tf_op jit(solution)/shard_map/ppermute | solution.py:238
  37.7 15.4 %collective-permute-start.7 = (bf16[128,256]{1,0:T(8,128)(2,1)S(1)}, bf16[128,256]{1,0:T(8,128)(2,1)S(1)}, u32[]{:S(2)}, u32[]{:S(2)}) collective-permute-start(bf16[128,256]{1,0:T(8,128)(2,1)S(1)} %add_add_fusion.queries_ref), channel_id=1, source_target_pairs={{0,12},{4,0},{8,4},{12,8},{1,13},{5,1},{9,5},{13,9},{2,14},{6,2},{... | collective-permute-start | bytes 196616 | tf_op jit(solution)/shard_map/ppermute | solution.py:238
  40.7 8.1 %collective-permute-start.5 = (bf16[128,256]{1,0:T(8,128)(2,1)S(1)}, bf16[128,256]{1,0:T(8,128)(2,1)S(1)}, u32[]{:S(2)}, u32[]{:S(2)}) collective-permute-start(bf16[128,256]{1,0:T(8,128)(2,1)S(1)} %add_add_fusion.queries_ref), channel_id=1, source_target_pairs={{0,8},{4,12},{8,0},{12,4},{1,9},{5,13},{9,1},{13,5},{2,10},{6,14},... | collective-permute-start | bytes 196616 | tf_op jit(solution)/shard_map/ppermute | solution.py:238
  41.1 6.2 %collective-permute-start.3 = (bf16[128,256]{1,0:T(8,128)(2,1)S(1)}, bf16[128,256]{1,0:T(8,128)(2,1)S(1)}, u32[]{:S(2)}, u32[]{:S(2)}) collective-permute-start(bf16[128,256]{1,0:T(8,128)(2,1)S(1)} %add_add_fusion.queries_ref), channel_id=1, source_target_pairs={{0,4},{4,8},{8,12},{12,0},{1,5},{5,9},{9,13},{13,1},{2,6},{6,10},{... | collective-permute-start | bytes 196616 | tf_op jit(solution)/shard_map/ppermute | solution.py:238
  42.3 25.9 %copy-start.9 = (s32[4]{0:T(128)S(1)}, s32[4]{0:T(128)}, u32[]{:S(2)}) copy-start(s32[4]{0:T(128)} %worker_ref.7) | copy-start | bytes 52
  47.3 27.3 %copy-start.1 = (bf16[256,1536]{1,0:T(8,128)(2,1)S(1)}, bf16[256,1536]{1,0:T(8,128)(2,1)}, u32[]{:S(2)}) copy-start(bf16[256,1536]{1,0:T(8,128)(2,1)} %refs_4_.1) | copy-start | bytes 2359300
  48.0 6.7 %collective-permute-start.4 = (bf16[272,128]{1,0:T(8,128)(2,1)S(1)}, bf16[272,128]{1,0:T(8,128)(2,1)S(1)}, u32[]{:S(2)}, u32[]{:S(2)}) collective-permute-start(bf16[272,128]{1,0:T(8,128)(2,1)S(1)} %attend.5), channel_id=1, source_target_pairs={{0,12},{4,0},{8,4},{12,8},{1,13},{5,1},{9,5},{13,9},{2,14},{6,2},{... | collective-permute-start | bytes 208904 | tf_op jit(solution)/shard_map/ppermute | solution.py:238
  49.5 6.1 %collective-permute-start.6 = (bf16[272,128]{1,0:T(8,128)(2,1)S(1)}, bf16[272,128]{1,0:T(8,128)(2,1)S(1)}, u32[]{:S(2)}, u32[]{:S(2)}) collective-permute-start(bf16[272,128]{1,0:T(8,128)(2,1)S(1)} %attend.6), channel_id=1, source_target_pairs={{0,8},{4,12},{8,0},{12,4},{1,9},{5,13},{9,1},{13,5},{2,10},{6,14},... | collective-permute-start | bytes 208904 | tf_op jit(solution)/shard_map/ppermute | solution.py:238
  53.9 6.8 %collective-permute-start.8 = (bf16[272,128]{1,0:T(8,128)(2,1)S(1)}, bf16[272,128]{1,0:T(8,128)(2,1)S(1)}, u32[]{:S(2)}, u32[]{:S(2)}) collective-permute-start(bf16[272,128]{1,0:T(8,128)(2,1)S(1)} %attend.7), channel_id=1, source_target_pairs={{0,4},{4,8},{8,12},{12,0},{1,5},{5,9},{9,13},{13,1},{2,6},{6,10},{... | collective-permute-start | bytes 208904 | tf_op jit(solution)/shard_map/ppermute | solution.py:238
  60.8 4.3 %collective-permute-start.11 = (bf16[128,256]{1,0:T(8,128)(2,1)S(1)}, bf16[128,256]{1,0:T(8,128)(2,1)S(1)}, u32[]{:S(2)}, u32[]{:S(2)}) collective-permute-start(bf16[128,256]{1,0:T(8,128)(2,1)S(1)} %combine.1.refs_0_), channel_id=1, source_target_pairs={{0,12},{4,0},{8,4},{12,8},{1,13},{5,1},{9,5},{13,9},{2,14},{6,2},{... | collective-permute-start | bytes 196616 | tf_op jit(solution)/shard_map/ppermute | solution.py:238
  60.9 5.2 %collective-permute-start.10 = (bf16[128,256]{1,0:T(8,128)(2,1)S(1)}, bf16[128,256]{1,0:T(8,128)(2,1)S(1)}, u32[]{:S(2)}, u32[]{:S(2)}) collective-permute-start(bf16[128,256]{1,0:T(8,128)(2,1)S(1)} %combine.1.refs_0_), channel_id=1, source_target_pairs={{0,8},{4,12},{8,0},{12,4},{1,9},{5,13},{9,1},{13,5},{2,10},{6,14},... | collective-permute-start | bytes 196616 | tf_op jit(solution)/shard_map/ppermute | solution.py:238
  60.9 7.2 %collective-permute-start.9 = (bf16[128,256]{1,0:T(8,128)(2,1)S(1)}, bf16[128,256]{1,0:T(8,128)(2,1)S(1)}, u32[]{:S(2)}, u32[]{:S(2)}) collective-permute-start(bf16[128,256]{1,0:T(8,128)(2,1)S(1)} %combine.1.refs_0_), channel_id=1, source_target_pairs={{0,4},{4,8},{8,12},{12,0},{1,5},{5,9},{9,13},{13,1},{2,6},{6,10},{... | collective-permute-start | bytes 196616 | tf_op jit(solution)/shard_map/ppermute | solution.py:238
  68.9 1.9 %collective-permute-start.12 = (bf16[128,256]{1,0:T(8,128)(2,1)S(1)}, bf16[128,256]{1,0:T(8,128)(2,1)S(1)}, u32[]{:S(2)}, u32[]{:S(2)}) collective-permute-start(bf16[128,256]{1,0:T(8,128)(2,1)S(1)} %get-tuple-element.22), channel_id=1, source_target_pairs={{0,1},{1,0},{2,3},{3,2},{4,5},{5,4},{6,7},{7,6},{8,9},{9,8},{10,11... | collective-permute-start | bytes 196616 | tf_op jit(solution)/shard_map/ppermute | solution.py:252
  69.0 4.5 %collective-permute-start.13 = (bf16[128,256]{1,0:T(8,128)(2,1)S(1)}, bf16[128,256]{1,0:T(8,128)(2,1)S(1)}, u32[]{:S(2)}, u32[]{:S(2)}) collective-permute-start(bf16[128,256]{1,0:T(8,128)(2,1)S(1)} %get-tuple-element.23), channel_id=1, source_target_pairs={{0,2},{1,3},{2,0},{3,1},{4,6},{5,7},{6,4},{7,5},{8,10},{9,11},{10,... | collective-permute-start | bytes 196616 | tf_op jit(solution)/shard_map/ppermute | solution.py:252
  70.5 4.0 %collective-permute-start.14 = (bf16[128,256]{1,0:T(8,128)(2,1)S(1)}, bf16[128,256]{1,0:T(8,128)(2,1)S(1)}, u32[]{:S(2)}, u32[]{:S(2)}) collective-permute-start(bf16[128,256]{1,0:T(8,128)(2,1)S(1)} %get-tuple-element.24), channel_id=1, source_target_pairs={{0,3},{1,2},{2,1},{3,0},{4,7},{5,6},{6,5},{7,4},{8,11},{9,10},{10,... | collective-permute-start | bytes 196616 | tf_op jit(solution)/shard_map/ppermute | solution.py:252

commit v2 on v1

v2 whole, which is shorter than its diff:
```python
import functools

import jax
import jax.numpy as jnp
from jax import lax
from jax.experimental import pallas as pl
from jax.experimental.pallas import tpu as pltpu
from jax.sharding import PartitionSpec as P

HD = 128
EPS = 1e-06
CHUNK = 16
COLUMNS = 512
SLOTS = 3
TAIL = 16
MIB = 1 << 20

VMEM = pl.BlockSpec(memory_space=pltpu.VMEM)
HBM = pl.BlockSpec(memory_space=pltpu.HBM)
ANY = pl.BlockSpec(memory_space=pl.ANY)


def normalize_block(latents_ref, modulation_ref, normed_ref, start, block_rows):
    def one_chunk(c, carry):
        at = pl.multiple_of(start + c * CHUNK, CHUNK)
        floats = latents_ref[pl.ds(at, CHUNK), :].astype(jnp.float32)
        center = floats - jnp.mean(floats, axis=-1, keepdims=True)
        spread = jnp.mean(center * center, axis=-1, keepdims=True)
        normed_ref[pl.ds(at, CHUNK), :] = (
            center * lax.rsqrt(spread + EPS) * (1.0 + modulation_ref[1:2, :])
            + modulation_ref[0:1, :]
        ).astype(jnp.bfloat16)
        return carry

    lax.fori_loop(0, block_rows // CHUNK, one_chunk, 0, unroll=4)


def query_kernel(n_frame, worker_in, latents_in, modulation_in, weight_in, *rest):
    outs = rest[:n_frame]
    worker_ref, latents_ref, modulation_ref, weight_ref, normed_ref, queries_ref, sems = rest[
        n_frame:
    ]
    n_local = worker_ref.shape[0]
    block_rows = latents_ref.shape[0] // n_local
    frame = lax.axis_index("frame")
    blocks = [slice(j * block_rows, (j + 1) * block_rows) for j in range(n_local)]
    first = [
        pltpu.make_async_copy(worker_in, worker_ref, sems.at[0]),
        pltpu.make_async_copy(modulation_in, modulation_ref, sems.at[1]),
    ]
    each = [
        pltpu.make_async_copy(latents_in.at[rows, :], latents_ref.at[rows, :], sems.at[3 + j])
        for j, rows in enumerate(blocks)
    ]
    weight = pltpu.make_async_copy(weight_in, weight_ref, sems.at[2])
    for copy in first + each + [weight]:
        copy.start()
    for s in range(n_frame):
        outs[s][...] = jnp.zeros_like(outs[s])
    for copy in first:
        copy.wait()
    for j in range(n_local):
        each[j].wait()

        @pl.when(worker_ref[j] >= 0)
        def _():
            normalize_block(latents_ref, modulation_ref, normed_ref, j * block_rows, block_rows)

    weight.wait()
    queries_ref[...] = (
        jnp.dot(normed_ref[...], weight_ref[...], preferred_element_type=jnp.float32) * HD ** (-0.5)
    ).astype(jnp.bfloat16)
    for j in range(n_local):
        worker = worker_ref[j]
        away = lax.rem(worker - frame + n_frame, n_frame)
        for s in range(n_frame):

            @pl.when((worker >= 0) & (away == s))
            def _():
                outs[s][...] = queries_ref[blocks[j], :]


def key_value_kernel(
    n_frame,
    n_head,
    n_rep,
    worker_in,
    latents_in,
    modulation_in,
    key_weight_in,
    value_weight_in,
    key_cache_in,
    value_cache_in,
    keys_ref,
    values_t_ref,
    masks_ref,
    worker_ref,
    latents_ref,
    modulation_ref,
    key_weight_ref,
    value_weight_ref,
    value_cache_ref,
    normed_ref,
    fresh_ref,
    sems,
):
    n_local = worker_ref.shape[0]
    tokens = latents_ref.shape[0]
    block_rows = tokens // n_local
    blocks = [slice(j * block_rows, (j + 1) * block_rows) for j in range(n_local)]
    first = [
        pltpu.make_async_copy(worker_in, worker_ref, sems.at[0]),
        pltpu.make_async_copy(modulation_in, modulation_ref, sems.at[1]),
        pltpu.make_async_copy(latents_in, latents_ref, sems.at[2]),
    ]
    second = [
        pltpu.make_async_copy(key_weight_in, key_weight_ref, sems.at[3]),
        pltpu.make_async_copy(value_weight_in, value_weight_ref, sems.at[4]),
        pltpu.make_async_copy(key_cache_in, keys_ref, sems.at[5]),
        pltpu.make_async_copy(value_cache_in, value_cache_ref, sems.at[6]),
    ]
    for copy in first + second:
        copy.start()
    for copy in first:
        copy.wait()
    frame, head, rep = lax.axis_index("frame"), lax.axis_index("head"), lax.axis_index("rep")
    n_place = n_head * n_rep
    for d in range(n_place):
        target = lax.rem(head + d // n_rep, n_head) * n_rep + lax.rem(rep + d % n_rep, n_rep)
        worker = worker_ref[target * (tokens // n_place) // block_rows]
        away = jnp.where(worker < 0, -1, lax.rem(frame - worker + n_frame, n_frame))
        for s in range(n_frame):
            masks_ref[d * n_frame + s : d * n_frame + s + 1, :] = jnp.full(
                (1, masks_ref.shape[1]), jnp.where(away == s, 1.0, 0.0), jnp.float32
            )
    for j in range(n_local):

        @pl.when(worker_ref[j] >= 0)
        def _():
            normalize_block(latents_ref, modulation_ref, normed_ref, j * block_rows, block_rows)

    for copy in second:
        copy.wait()
    fresh_ref[...] = jnp.dot(
        normed_ref[...], key_weight_ref[...], preferred_element_type=jnp.float32
    ).astype(jnp.bfloat16)
    for j in range(n_local):

        @pl.when(worker_ref[j] >= 0)
        def _():
            keys_ref[blocks[j], :] = fresh_ref[blocks[j], :]

    fresh_ref[...] = jnp.dot(
        normed_ref[...], value_weight_ref[...], preferred_element_type=jnp.float32
    ).astype(jnp.bfloat16)
    for j in range(n_local):

        @pl.when(worker_ref[j] >= 0)
        def _():
            value_cache_ref[blocks[j], :] = fresh_ref[blocks[j], :]

    for h in range(keys_ref.shape[1] // HD):
        cols = slice(h * HD, (h + 1) * HD)
        values_t_ref[cols, :] = value_cache_ref[:, cols].T


def three_terms(x):
    first = x.astype(jnp.bfloat16).astype(jnp.float32)
    rest = x - first
    second = rest.astype(jnp.bfloat16).astype(jnp.float32)
    return [first, second, rest - second]


def collect_kernel(*refs):
    *parts, _, out_ref = refs
    out_ref[...] = sum(part[...].astype(jnp.float32) for part in parts).astype(jnp.bfloat16)


def attend_kernel(count, *refs):
    keys_ref, values_t_ref = refs[count : count + 2]
    for queries_ref, out_ref in zip(refs[:count], refs[-count:]):
        attend_slot(queries_ref, keys_ref, values_t_ref, out_ref)


def attend_slot(queries_ref, keys_ref, values_t_ref, out_ref):
    width = keys_ref.shape[1]
    stats = []
    for h in range(width // HD):
        cols = slice(h * HD, (h + 1) * HD)
        scores = lax.dot_general(
            keys_ref[:, cols],
            queries_ref[:, cols],
            (((1,), (1,)), ((), ())),
            preferred_element_type=jnp.float32,
        )
        highest = jnp.max(scores, axis=0, keepdims=True)
        weights = jnp.exp(scores - highest)
        total = jnp.sum(weights, axis=0, keepdims=True)
        out_ref[cols, :] = jnp.dot(
            values_t_ref[cols, :], weights.astype(jnp.bfloat16), preferred_element_type=jnp.float32
        ).astype(jnp.bfloat16)
        stats += three_terms(highest) + three_terms(total)
    shape = (out_ref.shape[0] - width, out_ref.shape[1])
    row = lax.broadcasted_iota(jnp.int32, shape, 0)
    tail = jnp.zeros(shape, jnp.float32)
    for i, stat in enumerate(stats):
        tail = jnp.where(row == i, stat, tail)
    out_ref[width:, :] = tail.astype(jnp.bfloat16)


def combine_kernel(n_frame, *refs):
    parts, out_ref = refs[:n_frame], refs[n_frame + (len(refs) - n_frame - 1) // 2]
    width = out_ref.shape[1]
    tails = [part[width:, :].astype(jnp.float32) for part in parts]
    for h in range(width // HD):
        cols = slice(h * HD, (h + 1) * HD)

        def stat(tail, at):
            at += 6 * h
            return tail[at : at + 1, :] + tail[at + 1 : at + 2, :] + tail[at + 2 : at + 3, :]

        maxima = [stat(tail, 0) for tail in tails]
        highest = functools.reduce(jnp.maximum, maxima)
        factors = [jnp.exp(m - highest) for m in maxima]
        total = sum(stat(tail, 3) * factor for tail, factor in zip(tails, factors))
        summed = sum(
            part[cols, :].astype(jnp.float32) * factor for part, factor in zip(parts, factors)
        )
        out_ref[:, cols] = (summed / total).T.astype(jnp.bfloat16)


def select_kernel(n_frame, n_head, n_rep, *refs):
    slots, masks_ref, outs = refs[:n_frame], refs[n_frame], refs[n_frame + 1 :]
    block_rows, width = slots[0].shape
    rows = outs[0].shape[0]
    head, rep = lax.axis_index("head"), lax.axis_index("rep")
    for d in range(n_head * n_rep):
        if rows == block_rows:
            some = slice(None)
        else:
            target = lax.rem(head + d // n_rep, n_head) * n_rep + lax.rem(rep + d % n_rep, n_rep)
            some = pl.ds(pl.multiple_of(lax.rem(target * rows, block_rows), rows), rows)
        for h in range(width // HD):
            cols = slice(h * HD, (h + 1) * HD)
            chosen = jnp.zeros((rows, HD), jnp.float32)
            for s in range(n_frame):
                mask = masks_ref[d * n_frame + s : d * n_frame + s + 1, :]
                chosen = jnp.where(mask > 0.5, slots[s][some, cols].astype(jnp.float32), chosen)
            outs[d][:, cols] = chosen.astype(jnp.bfloat16)


def project_kernel(modulation_ref, *refs):
    refs, out_ref = refs[:-1], refs[-1]
    parts, weights = refs[: len(refs) // 2], refs[len(refs) // 2 :]
    width = out_ref.shape[1]
    for start in range(0, width, COLUMNS):
        cols = slice(start, start + COLUMNS)
        total = sum(
            jnp.dot(part[...], weight[:, cols], preferred_element_type=jnp.float32)
            for part, weight in zip(parts, weights)
        )
        out_ref[:, cols] = total * modulation_ref[2:3, cols]


def params(mib):
    return pltpu.CompilerParams(vmem_limit_bytes=mib * MIB)


def cost(flops, moved, exps=0):
    return pl.CostEstimate(flops=flops, bytes_accessed=moved, transcendentals=exps)


def per_device(
    n_frame,
    n_head,
    n_rep,
    latents,
    modulation,
    key_cache,
    value_cache,
    block_worker,
    query_weight,
    key_weight,
    value_weight,
    out_weight,
):
    tokens, model = latents.shape
    n_local = block_worker.shape[0]
    block_rows = tokens // n_local
    width = query_weight.shape[1]
    n_place = n_head * n_rep
    own_rows = tokens // n_place
    tail = TAIL * -(-6 * (width // HD) // TAIL)
    half = jnp.bfloat16

    def along_frame(x, shift):
        return lax.ppermute(x, "frame", [(i, (i + shift) % n_frame) for i in range(n_frame)])

    def along_head(x, shift):
        return lax.ppermute(x, "head", [(i, (i + shift) % n_head) for i in range(n_head)])

    def along_rep(x, shift):
        return lax.ppermute(x, "rep", [(i, (i + shift) % n_rep) for i in range(n_rep)])

    def in_frame(x, d):
        pairs = []
        for h in range(n_head):
            for r in range(n_rep):
                to = ((h + d // n_rep) % n_head) * n_rep + (r + d % n_rep) % n_rep
                pairs.append((h * n_rep + r, to))
        return lax.ppermute(x, ("head", "rep"), pairs)

    across = [along_head(out_weight, dh) for dh in range(1, n_head)]

    slots = pl.pallas_call(
        functools.partial(query_kernel, n_frame),
        out_shape=[jax.ShapeDtypeStruct((block_rows, width), half)] * n_frame,
        in_specs=[HBM] * 4,
        out_specs=[VMEM] * n_frame,
        scratch_shapes=[
            pltpu.SMEM(block_worker.shape, jnp.int32),
            pltpu.VMEM(latents.shape, half),
            pltpu.VMEM(modulation.shape, jnp.float32),
            pltpu.VMEM(query_weight.shape, half),
            pltpu.VMEM(latents.shape, half),
            pltpu.VMEM((tokens, width), half),
            pltpu.SemaphoreType.DMA((3 + n_local,)),
        ],
        compiler_params=params(60),
        cost_estimate=cost(2 * tokens * model * width, 2 * tokens * model + 2 * model * width),
        name="queries",
    )(block_worker, latents, modulation, query_weight)
    arrived = [along_frame(slots[s], s) for s in range(1, n_frame)]

    keys, values_t, masks = pl.pallas_call(
        functools.partial(key_value_kernel, n_frame, n_head, n_rep),
        out_shape=[
            jax.ShapeDtypeStruct((tokens, width), half),
            jax.ShapeDtypeStruct((width, tokens), half),
            jax.ShapeDtypeStruct((n_place * n_frame, HD), jnp.float32),
        ],
        in_specs=[HBM] * 7,
        out_specs=[VMEM] * 3,
        scratch_shapes=[
            pltpu.SMEM(block_worker.shape, jnp.int32),
            pltpu.VMEM(latents.shape, half),
            pltpu.VMEM(modulation.shape, jnp.float32),
            pltpu.VMEM(key_weight.shape, half),
            pltpu.VMEM(value_weight.shape, half),
            pltpu.VMEM(value_cache.shape, half),
            pltpu.VMEM(latents.shape, half),
            pltpu.VMEM((tokens, width), half),
            pltpu.SemaphoreType.DMA((7,)),
        ],
        compiler_params=params(53),
        cost_estimate=cost(4 * tokens * model * width, 2 * tokens * model + 4 * model * width),
        name="keys_values",
    )(block_worker, latents, modulation, key_weight, value_weight, key_cache, value_cache)

    mine = pl.pallas_call(
        collect_kernel,
        out_shape=jax.ShapeDtypeStruct((block_rows, width), half),
        in_specs=[VMEM] * n_frame + [ANY],
        out_specs=VMEM,
        compiler_params=params(16),
        cost_estimate=cost(n_frame * block_rows * width, 2 * n_frame * block_rows * width),
        name="collect",
    )(slots[0], *arrived, masks)

    def attend(queries, after=()):
        count = len(queries)
        return pl.pallas_call(
            functools.partial(attend_kernel, count),
            out_shape=[jax.ShapeDtypeStruct((width + tail, block_rows), half)] * count,
            in_specs=[VMEM] * (count + 2) + [ANY] * len(after),
            out_specs=[VMEM] * count,
            compiler_params=params(16),
            cost_estimate=cost(
                4 * tokens * block_rows * width * count,
                4 * tokens * width,
                tokens * block_rows * width // HD * count,
            ),
            name="attend",
        )(*queries, keys, values_t, *after)

    partial = list(attend([mine]))
    shared = [along_frame(mine, s) for s in range(1, n_frame)]
    for start in range(0, n_frame - 1, SLOTS):
        partial += attend(shared[start : start + SLOTS], partial[:1])
    gathered = partial[:1] + [along_frame(partial[s], n_frame - s) for s in range(1, n_frame)]
    attended, *across = pl.pallas_call(
        functools.partial(combine_kernel, n_frame),
        out_shape=[jax.ShapeDtypeStruct((block_rows, width), half)]
        + [jax.ShapeDtypeStruct(w.shape, w.dtype) for w in across],
        in_specs=[VMEM] * n_frame + [ANY] * len(across),
        out_specs=[VMEM] + [ANY] * len(across),
        input_output_aliases={n_frame + h: 1 + h for h in range(len(across))},
        compiler_params=params(16),
        cost_estimate=cost(4 * n_frame * block_rows * width, 2 * n_frame * block_rows * width),
        name="combine",
    )(*gathered, *across)
    copies = [attended] + [along_frame(attended, s) for s in range(1, n_frame)]
    pieces = pl.pallas_call(
        functools.partial(select_kernel, n_frame, n_head, n_rep),
        out_shape=[jax.ShapeDtypeStruct((own_rows, width), half)] * n_place,
        in_specs=[VMEM] * (n_frame + 1),
        out_specs=[VMEM] * n_place,
        compiler_params=params(16),
        cost_estimate=cost(0, 4 * n_frame * block_rows * width),
        name="select",
    )(*copies, masks)
    pieces = [pieces[0]] + [in_frame(pieces[d], d) for d in range(1, n_place)]

    weights = []
    for held in [out_weight] + across:
        weights += [held] + [along_rep(held, dr) for dr in range(1, n_rep)]
    return pl.pallas_call(
        project_kernel,
        out_shape=jax.ShapeDtypeStruct((own_rows, model), jnp.float32),
        in_specs=[VMEM] * (1 + 2 * n_place),
        out_specs=VMEM,
        compiler_params=params(16),
        cost_estimate=cost(2 * own_rows * model * width * n_place, 2 * model * width * n_place),
        name="project",
    )(modulation, *pieces, *weights)


def solution(mesh):
    in_specs = (
        P(("groups", "frame"), None),
        P("groups", None),
        P(("groups", "frame"), ("head", "rep")),
        P(("groups", "frame"), ("head", "rep")),
        P(("groups", "frame")),
        P(None, ("head", "rep")),
        P(None, ("head", "rep")),
        P(None, ("head", "rep")),
        P(("head", "rep"), None),
    )
    out_specs = P(("groups", "frame", "head", "rep"), None)
    body = functools.partial(
        per_device, mesh.shape["frame"], mesh.shape["head"], mesh.shape["rep"]
    )
    return jax.shard_map(body, mesh=mesh, in_specs=in_specs, out_specs=out_specs, check_vma=False)
```

time: 76.3 us -> 51.1 us (0.67)
  waiting for transfers between devices: 41.7 us -> 20.7 us
  local copies, waits for them, and re-layouts: 3.96 us -> 0.02 us
  starting transfers between devices: 22.8 us -> 19.3 us
  Pallas kernels: 7.46 us -> 10.8 us
    ppermute x1, waiting for transfers between devices: 17.7 us -> 0.01 us  [along_head(): lax.ppermute(x, 'head', [(i, (i + shift) % n_head) for i in range(n_head)])]
    unnamed x20 -> x10, local copies, waits for them, and re-layouts: 3.96 us -> 0.02 us
    ppermute x12, starting transfers between devices: 18 us -> 14.3 us  [along_frame(): lax.ppermute(x, 'frame', [(i, (i + shift) % n_frame) for i in range(n_fra...]
    ppermute x12, waiting for transfers between devices: 20.2 us -> 17.1 us  [along_frame(): lax.ppermute(x, 'frame', [(i, (i + shift) % n_frame) for i in range(n_fra...]
    pallas_call x7 -> x6, Pallas kernels: 5.47 us -> 7.52 us  [the longest x1 4.07 us: per_device(): pl.pallas_call(functools.partial(key_value_kernel, n_frame, n_head, n_rep...]
    pallas_call x1, Pallas kernels: 1.27 us -> 3.04 us  [per_device(): pl.pallas_call(functools.partial(query_kernel, n_frame), out_shape=[jax.S...]
  transfers between devices with their start and end apart: 18 -> 18, of which waited for: 10 -> 9; matrix products, arithmetic and copies ran while one was open for 0% -> 0% of each run, Pallas kernels for 8% -> 18%
where the time goes in v2:
time: 51.1 us; the launch traced here: 50.9 us
  waiting for transfers between devices  20.7 us (41%)
  starting transfers between devices  19.3 us (38%)
  Pallas kernels  10.8 us (21%)
    ppermute x12, waiting for transfers between devices, along_frame(): lax.ppermute(x, 'frame', [(i, (i + shift) % n_frame) for i in range(n_fra...  17.1 us
    ppermute x12, starting transfers between devices, along_frame(): lax.ppermute(x, 'frame', [(i, (i + shift) % n_frame) for i in range(n_fra...  14.3 us
    pallas_call x1, Pallas kernels, per_device(): pl.pallas_call(functools.partial(key_value_kernel, n_frame, n_head, n_rep...  4.07 us
    ppermute x3, waiting for transfers between devices, in_frame(): return lax.ppermute(x, ('head', 'rep'), pairs)  3.59 us
    pallas_call x1, Pallas kernels, per_device(): pl.pallas_call(functools.partial(query_kernel, n_frame), out_shape=[jax.S...  3.04 us
    ppermute x1, starting transfers between devices, along_head(): lax.ppermute(x, 'head', [(i, (i + shift) % n_head) for i in range(n_head)])  3.01 us
    ppermute x3, starting transfers between devices, in_frame(): return lax.ppermute(x, ('head', 'rep'), pairs)  1.94 us
    pallas_call x2, Pallas kernels, attend(): pl.pallas_call(functools.partial(attend_kernel, count), out_shape=[jax.Sh...  1.81 us
  transfers between devices with their start and end apart: 18, of which 9 were waited for; matrix products, arithmetic and copies ran while one was open for 0% of the time, Pallas kernels for 18%

profile of v2, /device:TPU:0, one launch (start us, length us, event | category | flops | bytes accessed | tf_op | source)
XLA Modules:
  0.0 50.9 jit_solution(3284239372637321538)
XLA Ops:
  0.0 3.0 %collective-permute-start.9 = (bf16[256,1536]{1,0:T(8,128)(2,1)}, bf16[256,1536]{1,0:T(8,128)(2,1)S(1)}, u32[]{:S(2)}, u32[]{:S(2)}) collective-permute-start(bf16[256,1536]{1,0:T(8,128)(2,1)} %refs_4_.1), channel_id=1, source_target_pairs={{0,2},{2,0},{1,3},{3,1},{4,6},{6,4},{5,7},{7,5},{8,10},{10,8},{9,1... | collective-permute-start | bytes 2359304 | tf_op jit(solution)/shard_map/ppermute | solution.py:300
  3.0 3.0 %queries.1 = (bf16[128,256]{1,0:T(8,128)(2,1)}, bf16[128,256]{1,0:T(8,128)(2,1)}, bf16[128,256]{1,0:T(8,128)(2,1)}, bf16[128,256]{1,0:T(8,128)(2,1)}) custom-call(s32[4]{0:T(128)} %worker_in.3, bf16[512,1536]{1,0:T(8,128)(2,1)} %latents_in.3, f32[3,1536]{1,0:T(4,128)} %modulation_ref.1, bf16[1536,256]{1,0:T(8,128)(2,1)} %weight_in.1), custom_call_target="tpu_custom_call" | custom-call | flops 402653184 | bytes 2359296 | tf_op jit(solution)/shard_map/queries/pallas_call | solution.py:315
  6.1 3.0 %collective-permute-start = (bf16[128,256]{1,0:T(8,128)(2,1)}, bf16[128,256]{1,0:T(8,128)(2,1)S(1)}, u32[]{:S(2)}, u32[]{:S(2)}) collective-permute-start(bf16[128,256]{1,0:T(8,128)(2,1)} %get-tuple-element.22), channel_id=1, source_target_pairs={{0,4},{4,8},{8,12},{12,0},{1,5},{5,9},{9,13},{13,1},{2,6},{6,10},{... | collective-permute-start | bytes 196616 | tf_op jit(solution)/shard_map/ppermute | solution.py:297
  9.0 1.2 %collective-permute-start.1 = (bf16[128,256]{1,0:T(8,128)(2,1)}, bf16[128,256]{1,0:T(8,128)(2,1)S(1)}, u32[]{:S(2)}, u32[]{:S(2)}) collective-permute-start(bf16[128,256]{1,0:T(8,128)(2,1)} %get-tuple-element.23), channel_id=1, source_target_pairs={{0,8},{4,12},{8,0},{12,4},{1,9},{5,13},{9,1},{13,5},{2,10},{6,14},... | collective-permute-start | bytes 196616 | tf_op jit(solution)/shard_map/ppermute | solution.py:297
  10.3 1.3 %collective-permute-start.2 = (bf16[128,256]{1,0:T(8,128)(2,1)}, bf16[128,256]{1,0:T(8,128)(2,1)S(1)}, u32[]{:S(2)}, u32[]{:S(2)}) collective-permute-start(bf16[128,256]{1,0:T(8,128)(2,1)} %get-tuple-element.24), channel_id=1, source_target_pairs={{0,12},{4,0},{8,4},{12,8},{1,13},{5,1},{9,5},{13,9},{2,14},{6,2},{... | collective-permute-start | bytes 196616 | tf_op jit(solution)/shard_map/ppermute | solution.py:297
  11.6 4.1 %keys_values.1 = (bf16[512,256]{1,0:T(8,128)(2,1)S(1)}, bf16[256,512]{1,0:T(8,128)(2,1)S(1)}, f32[16,128]{1,0:T(8,128)S(1)}) custom-call(s32[4]{0:T(128)S(1)} %copy-done.4, bf16[512,1536]{1,0:T(8,128)(2,1)} %latents_in.3, f32[3,1536]{1,0:T(4,128)S(1)} %copy-done.2, bf16[1536,256]{1,0:T(8,128)(2,1)} %key_weight_in.1, bf16[1536,256]{1,0:T(8,128)(2,1)} %value_weight_in.1, ...), custom_call_target="tpu_custom_call" | custom-call | flops 805306368 | bytes 3145728 | tf_op jit(solution)/shard_map/keys_values/pallas_call | solution.py:335
  15.7 0.0 copy-start
  15.7 0.0 collective-permute-done.refs_1_
  15.8 2.2 %collective-permute-start.5 = (bf16[128,256]{1,0:T(8,128)(2,1)S(1)}, bf16[128,256]{1,0:T(8,128)(2,1)S(1)}, u32[]{:S(2)}, u32[]{:S(2)}) collective-permute-start(bf16[128,256]{1,0:T(8,128)(2,1)S(1)} %collect.1.refs_0_), channel_id=1, source_target_pairs={{0,12},{4,0},{8,4},{12,8},{1,13},{5,1},{9,5},{13,9},{2,14},{6,2},{... | collective-permute-start | bytes 196616 | tf_op jit(solution)/shard_map/ppermute | solution.py:297
  18.1 1.4 %collective-permute-start.4 = (bf16[128,256]{1,0:T(8,128)(2,1)S(1)}, bf16[128,256]{1,0:T(8,128)(2,1)S(1)}, u32[]{:S(2)}, u32[]{:S(2)}) collective-permute-start(bf16[128,256]{1,0:T(8,128)(2,1)S(1)} %collect.1.refs_0_), channel_id=1, source_target_pairs={{0,8},{4,12},{8,0},{12,4},{1,9},{5,13},{9,1},{13,5},{2,10},{6,14},... | collective-permute-start | bytes 196616 | tf_op jit(solution)/shard_map/ppermute | solution.py:297
  19.5 0.7 %attend.2.refs_5_.refs_0_ = bf16[272,128]{1,0:T(8,128)(2,1)S(1)} custom-call(bf16[128,256]{1,0:T(8,128)(2,1)S(1)} %collect.1.refs_0_, bf16[512,256]{1,0:T(8,128)(2,1)S(1)} %get-tuple-element.26.refs_1_.refs_3_, bf16[256,512]{1,0:T(8,128)(2,1)S(1)} %get-tuple-element.27.refs_2_.refs_4_), custom_call_target="tpu_custom_call" | custom-call | flops 67108864 | bytes 524288 | tf_op jit(solution)/shard_map/attend/pallas_call | solution.py:372
  20.2 0.6 %collective-permute-done.5.refs_2_ = bf16[128,256]{1,0:T(8,128)(2,1)S(1)} collective-permute-done((bf16[128,256]{1,0:T(8,128)(2,1)S(1)}, bf16[128,256]{1,0:T(8,128)(2,1)S(1)}, u32[]{:S(2)}, u32[]{:S(2)}) %collective-permute-start.5) | collective-permute-done | bytes 65568 | tf_op jit(solution)/shard_map/ppermute | solution.py:297
  20.8 3.3 %collective-permute-done.4.refs_1_ = bf16[128,256]{1,0:T(8,128)(2,1)S(1)} collective-permute-done((bf16[128,256]{1,0:T(8,128)(2,1)S(1)}, bf16[128,256]{1,0:T(8,128)(2,1)S(1)}, u32[]{:S(2)}, u32[]{:S(2)}) %collective-permute-start.4) | collective-permute-done | bytes 65568 | tf_op jit(solution)/shard_map/ppermute | solution.py:297
  24.1 1.4 %collective-permute-done.3.refs_0_ = bf16[128,256]{1,0:T(8,128)(2,1)S(1)} collective-permute-done((bf16[128,256]{1,0:T(8,128)(2,1)S(1)}, bf16[128,256]{1,0:T(8,128)(2,1)S(1)}, u32[]{:S(2)}, u32[]{:S(2)}) %collective-permute-start.3) | collective-permute-done | bytes 65568 | tf_op jit(solution)/shard_map/ppermute | solution.py:297
  25.6 1.1 %attend.3 = (bf16[272,128]{1,0:T(8,128)(2,1)S(1)}, bf16[272,128]{1,0:T(8,128)(2,1)S(1)}, bf16[272,128]{1,0:T(8,128)(2,1)S(1)}) custom-call(bf16[128,256]{1,0:T(8,128)(2,1)S(1)} %collective-permute-done.3.refs_0_, bf16[128,256]{1,0:T(8,128)(2,1)S(1)} %collective-permute-done.4.refs_1_, bf16[128,256]{1,0:T(8,128)(2,1)S(1)} %collective-permute-done.5.refs_2_, ...), custom_call_target="tpu_custom_call" | custom-call | flops 201326592 | bytes 524288 | tf_op jit(solution)/shard_map/attend/pallas_call | solution.py:372
  26.6 0.4 collective-permute-start.6
  27.1 1.8 %collective-permute-start.8 = (bf16[272,128]{1,0:T(8,128)(2,1)S(1)}, bf16[272,128]{1,0:T(8,128)(2,1)S(1)}, u32[]{:S(2)}, u32[]{:S(2)}) collective-permute-start(bf16[272,128]{1,0:T(8,128)(2,1)S(1)} %get-tuple-element.30), channel_id=1, source_target_pairs={{0,4},{4,8},{8,12},{12,0},{1,5},{5,9},{9,13},{13,1},{2,6},{6,10},{... | collective-permute-start | bytes 208904 | tf_op jit(solution)/shard_map/ppermute | solution.py:297
  28.9 3.5 %collective-permute-done.6.refs_1_ = bf16[272,128]{1,0:T(8,128)(2,1)S(1)} collective-permute-done((bf16[272,128]{1,0:T(8,128)(2,1)S(1)}, bf16[272,128]{1,0:T(8,128)(2,1)S(1)}, u32[]{:S(2)}, u32[]{:S(2)}) %collective-permute-start.6) | collective-permute-done | bytes 69664 | tf_op jit(solution)/shard_map/ppermute | solution.py:297
  32.5 1.6 %collective-permute-done.8.refs_3_ = bf16[272,128]{1,0:T(8,128)(2,1)S(1)} collective-permute-done((bf16[272,128]{1,0:T(8,128)(2,1)S(1)}, bf16[272,128]{1,0:T(8,128)(2,1)S(1)}, u32[]{:S(2)}, u32[]{:S(2)}) %collective-permute-start.8) | collective-permute-done | bytes 69664 | tf_op jit(solution)/shard_map/ppermute | solution.py:297
  34.1 0.1 combine.1
  34.3 0.1 collective-permute-start.17
  34.3 1.6 %collective-permute-start.12 = (bf16[128,256]{1,0:T(8,128)(2,1)S(1)}, bf16[128,256]{1,0:T(8,128)(2,1)S(1)}, u32[]{:S(2)}, u32[]{:S(2)}) collective-permute-start(bf16[128,256]{1,0:T(8,128)(2,1)S(1)} %get-tuple-element.31.refs_0_), channel_id=1, source_target_pairs={{0,12},{4,0},{8,4},{12,8},{1,13},{5,1},{9,5},{13,9},{2,14},{6,2},{... | collective-permute-start | bytes 196616 | tf_op jit(solution)/shard_map/ppermute | solution.py:297
  36.0 1.1 %collective-permute-start.10 = (bf16[128,256]{1,0:T(8,128)(2,1)S(1)}, bf16[128,256]{1,0:T(8,128)(2,1)S(1)}, u32[]{:S(2)}, u32[]{:S(2)}) collective-permute-start(bf16[128,256]{1,0:T(8,128)(2,1)S(1)} %get-tuple-element.31.refs_0_), channel_id=1, source_target_pairs={{0,4},{4,8},{8,12},{12,0},{1,5},{5,9},{9,13},{13,1},{2,6},{6,10},{... | collective-permute-start | bytes 196616 | tf_op jit(solution)/shard_map/ppermute | solution.py:297
  37.1 1.7 %collective-permute-done.12.refs_3_ = bf16[128,256]{1,0:T(8,128)(2,1)S(1)} collective-permute-done((bf16[128,256]{1,0:T(8,128)(2,1)S(1)}, bf16[128,256]{1,0:T(8,128)(2,1)S(1)}, u32[]{:S(2)}, u32[]{:S(2)}) %collective-permute-start.12) | collective-permute-done | bytes 65568 | tf_op jit(solution)/shard_map/ppermute | solution.py:297
  38.8 4.9 %collective-permute-done.11.refs_2_ = bf16[128,256]{1,0:T(8,128)(2,1)S(1)} collective-permute-done((bf16[128,256]{1,0:T(8,128)(2,1)S(1)}, bf16[128,256]{1,0:T(8,128)(2,1)S(1)}, u32[]{:S(2)}, u32[]{:S(2)}) %collective-permute-start.11) | collective-permute-done | bytes 65568 | tf_op jit(solution)/shard_map/ppermute | solution.py:297
  43.7 0.2 select.1
  43.9 0.1 collective-permute-start.13
  44.0 0.6 %collective-permute-start.14 = (bf16[128,256]{1,0:T(8,128)(2,1)S(1)}, bf16[128,256]{1,0:T(8,128)(2,1)S(1)}, u32[]{:S(2)}, u32[]{:S(2)}) collective-permute-start(bf16[128,256]{1,0:T(8,128)(2,1)S(1)} %get-tuple-element.34), channel_id=1, source_target_pairs={{0,2},{1,3},{2,0},{3,1},{4,6},{5,7},{6,4},{7,5},{8,10},{9,11},{10,... | collective-permute-start | bytes 196616 | tf_op jit(solution)/shard_map/ppermute | solution.py:311
  44.6 1.3 %collective-permute-start.15 = (bf16[128,256]{1,0:T(8,128)(2,1)S(1)}, bf16[128,256]{1,0:T(8,128)(2,1)S(1)}, u32[]{:S(2)}, u32[]{:S(2)}) collective-permute-start(bf16[128,256]{1,0:T(8,128)(2,1)S(1)} %get-tuple-element.35), channel_id=1, source_target_pairs={{0,3},{1,2},{2,1},{3,0},{4,7},{5,6},{6,5},{7,4},{8,11},{9,10},{10,... | collective-permute-start | bytes 196616 | tf_op jit(solution)/shard_map/ppermute | solution.py:311
  45.9 3.1 %collective-permute-done.14.refs_2_ = bf16[128,256]{1,0:T(8,128)(2,1)S(1)} collective-permute-done((bf16[128,256]{1,0:T(8,128)(2,1)S(1)}, bf16[128,256]{1,0:T(8,128)(2,1)S(1)}, u32[]{:S(2)}, u32[]{:S(2)}) %collective-permute-start.14) | collective-permute-done | bytes 65568 | tf_op jit(solution)/shard_map/ppermute | solution.py:311
  49.0 0.5 collective-permute-done.15.refs_3_
  49.5 1.5 %project.1 = f32[128,1536]{1,0:T(8,128)} custom-call(f32[3,1536]{1,0:T(4,128)S(1)} %copy-done.2, bf16[128,256]{1,0:T(8,128)(2,1)S(1)} %get-tuple-element.32.refs_0_, bf16[128,256]{1,0:T(8,128)(2,1)S(1)} %collective-permute-done.13.refs_1_, bf16[128,256]{1,0:T(8,128)(2,1)S(1)} %collective-permute-done.14.refs_2_, ...), custom_call_target="tpu_custom_call" | custom-call | flops 402653184 | bytes 3145728 | tf_op jit(solution)/shard_map/project/pallas_call | solution.py:417
  (22 shorter events, 0.1 us)
Async XLA Ops:
  0.0 11.6 %copy-start.2 = (f32[3,1536]{1,0:T(4,128)S(1)}, f32[3,1536]{1,0:T(4,128)}, u32[]{:S(2)}) copy-start(f32[3,1536]{1,0:T(4,128)} %modulation_ref.1) | copy-start | bytes 55300
  0.0 11.6 %copy-start.4 = (s32[4]{0:T(128)S(1)}, s32[4]{0:T(128)}, u32[]{:S(2)}) copy-start(s32[4]{0:T(128)} %worker_in.3) | copy-start | bytes 52
  0.0 11.6 %copy-start.1 = (bf16[512,256]{1,0:T(8,128)(2,1)S(1)}, bf16[512,256]{1,0:T(8,128)(2,1)}, u32[]{:S(2)}) copy-start(bf16[512,256]{1,0:T(8,128)(2,1)} %key_cache_in.1) | copy-start | bytes 786436
  0.0 34.1 %collective-permute-start.9 = (bf16[256,1536]{1,0:T(8,128)(2,1)}, bf16[256,1536]{1,0:T(8,128)(2,1)S(1)}, u32[]{:S(2)}, u32[]{:S(2)}) collective-permute-start(bf16[256,1536]{1,0:T(8,128)(2,1)} %refs_4_.1), channel_id=1, source_target_pairs={{0,2},{2,0},{1,3},{3,1},{4,6},{6,4},{5,7},{7,5},{8,10},{10,8},{9,1... | collective-permute-start | bytes 2359304 | tf_op jit(solution)/shard_map/ppermute | solution.py:300
  6.1 9.7 %collective-permute-start = (bf16[128,256]{1,0:T(8,128)(2,1)}, bf16[128,256]{1,0:T(8,128)(2,1)S(1)}, u32[]{:S(2)}, u32[]{:S(2)}) collective-permute-start(bf16[128,256]{1,0:T(8,128)(2,1)} %get-tuple-element.22), channel_id=1, source_target_pairs={{0,4},{4,8},{8,12},{12,0},{1,5},{5,9},{9,13},{13,1},{2,6},{6,10},{... | collective-permute-start | bytes 196616 | tf_op jit(solution)/shard_map/ppermute | solution.py:297
  9.0 6.7 %collective-permute-start.1 = (bf16[128,256]{1,0:T(8,128)(2,1)}, bf16[128,256]{1,0:T(8,128)(2,1)S(1)}, u32[]{:S(2)}, u32[]{:S(2)}) collective-permute-start(bf16[128,256]{1,0:T(8,128)(2,1)} %get-tuple-element.23), channel_id=1, source_target_pairs={{0,8},{4,12},{8,0},{12,4},{1,9},{5,13},{9,1},{13,5},{2,10},{6,14},... | collective-permute-start | bytes 196616 | tf_op jit(solution)/shard_map/ppermute | solution.py:297
  10.3 5.5 %copy-start.3 = (bf16[128,256]{1,0:T(8,128)(2,1)S(1)}, bf16[128,256]{1,0:T(8,128)(2,1)}, u32[]{:S(2)}) copy-start(bf16[128,256]{1,0:T(8,128)(2,1)} %get-tuple-element.21.refs_0_) | copy-start | bytes 196612
  10.3 5.5 %collective-permute-start.2 = (bf16[128,256]{1,0:T(8,128)(2,1)}, bf16[128,256]{1,0:T(8,128)(2,1)S(1)}, u32[]{:S(2)}, u32[]{:S(2)}) collective-permute-start(bf16[128,256]{1,0:T(8,128)(2,1)} %get-tuple-element.24), channel_id=1, source_target_pairs={{0,12},{4,0},{8,4},{12,8},{1,13},{5,1},{9,5},{13,9},{2,14},{6,2},{... | collective-permute-start | bytes 196616 | tf_op jit(solution)/shard_map/ppermute | solution.py:297
  15.7 13.2 %copy-start = (bf16[256,1536]{1,0:T(8,128)(2,1)S(1)}, bf16[256,1536]{1,0:T(8,128)(2,1)}, u32[]{:S(2)}) copy-start(bf16[256,1536]{1,0:T(8,128)(2,1)} %refs_4_.1) | copy-start | bytes 2359300
  15.8 5.0 %collective-permute-start.5 = (bf16[128,256]{1,0:T(8,128)(2,1)S(1)}, bf16[128,256]{1,0:T(8,128)(2,1)S(1)}, u32[]{:S(2)}, u32[]{:S(2)}) collective-permute-start(bf16[128,256]{1,0:T(8,128)(2,1)S(1)} %collect.1.refs_0_), channel_id=1, source_target_pairs={{0,12},{4,0},{8,4},{12,8},{1,13},{5,1},{9,5},{13,9},{2,14},{6,2},{... | collective-permute-start | bytes 196616 | tf_op jit(solution)/shard_map/ppermute | solution.py:297
  18.1 6.0 %collective-permute-start.4 = (bf16[128,256]{1,0:T(8,128)(2,1)S(1)}, bf16[128,256]{1,0:T(8,128)(2,1)S(1)}, u32[]{:S(2)}, u32[]{:S(2)}) collective-permute-start(bf16[128,256]{1,0:T(8,128)(2,1)S(1)} %collect.1.refs_0_), channel_id=1, source_target_pairs={{0,8},{4,12},{8,0},{12,4},{1,9},{5,13},{9,1},{13,5},{2,10},{6,14},... | collective-permute-start | bytes 196616 | tf_op jit(solution)/shard_map/ppermute | solution.py:297
  19.5 6.1 %collective-permute-start.3 = (bf16[128,256]{1,0:T(8,128)(2,1)S(1)}, bf16[128,256]{1,0:T(8,128)(2,1)S(1)}, u32[]{:S(2)}, u32[]{:S(2)}) collective-permute-start(bf16[128,256]{1,0:T(8,128)(2,1)S(1)} %collect.1.refs_0_), channel_id=1, source_target_pairs={{0,4},{4,8},{8,12},{12,0},{1,5},{5,9},{9,13},{13,1},{2,6},{6,10},{... | collective-permute-start | bytes 196616 | tf_op jit(solution)/shard_map/ppermute | solution.py:297
  26.6 5.8 %collective-permute-start.6 = (bf16[272,128]{1,0:T(8,128)(2,1)S(1)}, bf16[272,128]{1,0:T(8,128)(2,1)S(1)}, u32[]{:S(2)}, u32[]{:S(2)}) collective-permute-start(bf16[272,128]{1,0:T(8,128)(2,1)S(1)} %get-tuple-element.28), channel_id=1, source_target_pairs={{0,12},{4,0},{8,4},{12,8},{1,13},{5,1},{9,5},{13,9},{2,14},{6,2},{... | collective-permute-start | bytes 208904 | tf_op jit(solution)/shard_map/ppermute | solution.py:297
  27.1 5.4 %collective-permute-start.7 = (bf16[272,128]{1,0:T(8,128)(2,1)S(1)}, bf16[272,128]{1,0:T(8,128)(2,1)S(1)}, u32[]{:S(2)}, u32[]{:S(2)}) collective-permute-start(bf16[272,128]{1,0:T(8,128)(2,1)S(1)} %get-tuple-element.29), channel_id=1, source_target_pairs={{0,8},{4,12},{8,0},{12,4},{1,9},{5,13},{9,1},{13,5},{2,10},{6,14},... | collective-permute-start | bytes 208904 | tf_op jit(solution)/shard_map/ppermute | solution.py:297
  27.1 7.0 %collective-permute-start.8 = (bf16[272,128]{1,0:T(8,128)(2,1)S(1)}, bf16[272,128]{1,0:T(8,128)(2,1)S(1)}, u32[]{:S(2)}, u32[]{:S(2)}) collective-permute-start(bf16[272,128]{1,0:T(8,128)(2,1)S(1)} %get-tuple-element.30), channel_id=1, source_target_pairs={{0,4},{4,8},{8,12},{12,0},{1,5},{5,9},{9,13},{13,1},{2,6},{6,10},{... | collective-permute-start | bytes 208904 | tf_op jit(solution)/shard_map/ppermute | solution.py:297
  28.9 16.9 %collective-permute-start.16 = (bf16[256,1536]{1,0:T(8,128)(2,1)S(1)}, bf16[256,1536]{1,0:T(8,128)(2,1)S(1)}, u32[]{:S(2)}, u32[]{:S(2)}) collective-permute-start(bf16[256,1536]{1,0:T(8,128)(2,1)S(1)} %copy-done), channel_id=1, source_target_pairs={{0,1},{1,0},{2,3},{3,2},{4,5},{5,4},{6,7},{7,6},{8,9},{9,8},{10,11... | collective-permute-start | bytes 2359304 | tf_op jit(solution)/shard_map/ppermute | solution.py:303
  34.3 15.2 %collective-permute-start.17 = (bf16[256,1536]{1,0:T(8,128)(2,1)S(1)}, bf16[256,1536]{1,0:T(8,128)(2,1)S(1)}, u32[]{:S(2)}, u32[]{:S(2)}) collective-permute-start(bf16[256,1536]{1,0:T(8,128)(2,1)S(1)} %get-tuple-element.36.refs_6_), channel_id=1, source_target_pairs={{0,1},{1,0},{2,3},{3,2},{4,5},{5,4},{6,7},{7,6},{8,9},{9,8},{10,11... | collective-permute-start | bytes 2359304 | tf_op jit(solution)/shard_map/ppermute | solution.py:303
  34.3 4.5 %collective-permute-start.12 = (bf16[128,256]{1,0:T(8,128)(2,1)S(1)}, bf16[128,256]{1,0:T(8,128)(2,1)S(1)}, u32[]{:S(2)}, u32[]{:S(2)}) collective-permute-start(bf16[128,256]{1,0:T(8,128)(2,1)S(1)} %get-tuple-element.31.refs_0_), channel_id=1, source_target_pairs={{0,12},{4,0},{8,4},{12,8},{1,13},{5,1},{9,5},{13,9},{2,14},{6,2},{... | collective-permute-start | bytes 196616 | tf_op jit(solution)/shard_map/ppermute | solution.py:297
  36.0 7.8 %collective-permute-start.11 = (bf16[128,256]{1,0:T(8,128)(2,1)S(1)}, bf16[128,256]{1,0:T(8,128)(2,1)S(1)}, u32[]{:S(2)}, u32[]{:S(2)}) collective-permute-start(bf16[128,256]{1,0:T(8,128)(2,1)S(1)} %get-tuple-element.31.refs_0_), channel_id=1, source_target_pairs={{0,8},{4,12},{8,0},{12,4},{1,9},{5,13},{9,1},{13,5},{2,10},{6,14},... | collective-permute-start | bytes 196616 | tf_op jit(solution)/shard_map/ppermute | solution.py:297
  36.0 7.8 %collective-permute-start.10 = (bf16[128,256]{1,0:T(8,128)(2,1)S(1)}, bf16[128,256]{1,0:T(8,128)(2,1)S(1)}, u32[]{:S(2)}, u32[]{:S(2)}) collective-permute-start(bf16[128,256]{1,0:T(8,128)(2,1)S(1)} %get-tuple-element.31.refs_0_), channel_id=1, source_target_pairs={{0,4},{4,8},{8,12},{12,0},{1,5},{5,9},{9,13},{13,1},{2,6},{6,10},{... | collective-permute-start | bytes 196616 | tf_op jit(solution)/shard_map/ppermute | solution.py:297
  43.9 1.9 %collective-permute-start.13 = (bf16[128,256]{1,0:T(8,128)(2,1)S(1)}, bf16[128,256]{1,0:T(8,128)(2,1)S(1)}, u32[]{:S(2)}, u32[]{:S(2)}) collective-permute-start(bf16[128,256]{1,0:T(8,128)(2,1)S(1)} %get-tuple-element.33), channel_id=1, source_target_pairs={{0,1},{1,0},{2,3},{3,2},{4,5},{5,4},{6,7},{7,6},{8,9},{9,8},{10,11... | collective-permute-start | bytes 196616 | tf_op jit(solution)/shard_map/ppermute | solution.py:311
  44.0 5.0 %collective-permute-start.14 = (bf16[128,256]{1,0:T(8,128)(2,1)S(1)}, bf16[128,256]{1,0:T(8,128)(2,1)S(1)}, u32[]{:S(2)}, u32[]{:S(2)}) collective-permute-start(bf16[128,256]{1,0:T(8,128)(2,1)S(1)} %get-tuple-element.34), channel_id=1, source_target_pairs={{0,2},{1,3},{2,0},{3,1},{4,6},{5,7},{6,4},{7,5},{8,10},{9,11},{10,... | collective-permute-start | bytes 196616 | tf_op jit(solution)/shard_map/ppermute | solution.py:311
  44.6 4.9 %collective-permute-start.15 = (bf16[128,256]{1,0:T(8,128)(2,1)S(1)}, bf16[128,256]{1,0:T(8,128)(2,1)S(1)}, u32[]{:S(2)}, u32[]{:S(2)}) collective-permute-start(bf16[128,256]{1,0:T(8,128)(2,1)S(1)} %get-tuple-element.35), channel_id=1, source_target_pairs={{0,3},{1,2},{2,1},{3,0},{4,7},{5,6},{6,5},{7,4},{8,11},{9,10},{10,... | collective-permute-start | bytes 196616 | tf_op jit(solution)/shard_map/ppermute | solution.py:311

commit v3 on v2

--- a/solution.py
+++ b/solution.py
@@ -11,7 +11,7 @@
 EPS = 1e-06
 CHUNK = 16
 COLUMNS = 512
-SLOTS = 3
+SLOTS = 4
 TAIL = 16
 MIB = 1 << 20
 
@@ -82,8 +82,7 @@
 
 def key_value_kernel(
     n_frame,
-    n_head,
-    n_rep,
+    n_place,
     worker_in,
     latents_in,
     modulation_in,
@@ -123,15 +122,11 @@
         copy.start()
     for copy in first:
         copy.wait()
-    frame, head, rep = lax.axis_index("frame"), lax.axis_index("head"), lax.axis_index("rep")
-    n_place = n_head * n_rep
-    for d in range(n_place):
-        target = lax.rem(head + d // n_rep, n_head) * n_rep + lax.rem(rep + d % n_rep, n_rep)
-        worker = worker_ref[target * (tokens // n_place) // block_rows]
-        away = jnp.where(worker < 0, -1, lax.rem(frame - worker + n_frame, n_frame))
+    for p in range(n_place):
+        worker = worker_ref[p * (tokens // n_place) // block_rows]
         for s in range(n_frame):
-            masks_ref[d * n_frame + s : d * n_frame + s + 1, :] = jnp.full(
-                (1, masks_ref.shape[1]), jnp.where(away == s, 1.0, 0.0), jnp.float32
+            masks_ref[p * n_frame + s : p * n_frame + s + 1, :] = jnp.full(
+                (1, masks_ref.shape[1]), jnp.where(worker == s, 1.0, 0.0), jnp.float32
             )
     for j in range(n_local):
 
@@ -173,13 +168,19 @@
 
 def collect_kernel(*refs):
     *parts, _, out_ref = refs
-    out_ref[...] = sum(part[...].astype(jnp.float32) for part in parts).astype(jnp.bfloat16)
-
-
-def attend_kernel(count, *refs):
-    keys_ref, values_t_ref = refs[count : count + 2]
-    for queries_ref, out_ref in zip(refs[:count], refs[-count:]):
-        attend_slot(queries_ref, keys_ref, values_t_ref, out_ref)
+    mine = sum(part[...].astype(jnp.float32) for part in parts).astype(jnp.bfloat16)
+    for s in range(out_ref.shape[0]):
+        out_ref[s] = mine
+
+
+def attend_kernel(queries_ref, keys_ref, values_t_ref, out_ref):
+    count = queries_ref.shape[0]
+
+    def one_slot(s, carry):
+        attend_slot(queries_ref.at[s], keys_ref, values_t_ref, out_ref.at[s])
+        return carry
+
+    lax.fori_loop(0, count, one_slot, 0, unroll=min(count, SLOTS))
 
 
 def attend_slot(queries_ref, keys_ref, values_t_ref, out_ref):
@@ -208,9 +209,10 @@
     out_ref[width:, :] = tail.astype(jnp.bfloat16)
 
 
-def combine_kernel(n_frame, *refs):
-    parts, out_ref = refs[:n_frame], refs[n_frame + (len(refs) - n_frame - 1) // 2]
-    width = out_ref.shape[1]
+def combine_kernel(parts_ref, *refs):
+    out_ref = refs[len(refs) // 2]
+    count, _, width = out_ref.shape
+    parts = [parts_ref.at[s] for s in range(count)]
     tails = [part[width:, :].astype(jnp.float32) for part in parts]
     for h in range(width // HD):
         cols = slice(h * HD, (h + 1) * HD)
@@ -226,37 +228,38 @@
         summed = sum(
             part[cols, :].astype(jnp.float32) * factor for part, factor in zip(parts, factors)
         )
-        out_ref[:, cols] = (summed / total).T.astype(jnp.bfloat16)
-
-
-def select_kernel(n_frame, n_head, n_rep, *refs):
-    slots, masks_ref, outs = refs[:n_frame], refs[n_frame], refs[n_frame + 1 :]
-    block_rows, width = slots[0].shape
-    rows = outs[0].shape[0]
-    head, rep = lax.axis_index("head"), lax.axis_index("rep")
-    for d in range(n_head * n_rep):
-        if rows == block_rows:
-            some = slice(None)
-        else:
-            target = lax.rem(head + d // n_rep, n_head) * n_rep + lax.rem(rep + d % n_rep, n_rep)
-            some = pl.ds(pl.multiple_of(lax.rem(target * rows, block_rows), rows), rows)
+        attended = (summed / total).T.astype(jnp.bfloat16)
+        for s in range(count):
+            out_ref[s, :, cols] = attended
+
+
+def select_kernel(n_place, slots_ref, masks_ref, out_ref):
+    n_frame, block_rows, width = slots_ref.shape
+    rows = out_ref.shape[1]
+    for p in range(n_place):
+        start = p * rows % block_rows
         for h in range(width // HD):
             cols = slice(h * HD, (h + 1) * HD)
             chosen = jnp.zeros((rows, HD), jnp.float32)
             for s in range(n_frame):
-                mask = masks_ref[d * n_frame + s : d * n_frame + s + 1, :]
-                chosen = jnp.where(mask > 0.5, slots[s][some, cols].astype(jnp.float32), chosen)
-            outs[d][:, cols] = chosen.astype(jnp.bfloat16)
-
-
-def project_kernel(modulation_ref, *refs):
-    refs, out_ref = refs[:-1], refs[-1]
-    parts, weights = refs[: len(refs) // 2], refs[len(refs) // 2 :]
+                mask = masks_ref[p * n_frame + s : p * n_frame + s + 1, :]
+                slot = slots_ref[s, start : start + rows, cols].astype(jnp.float32)
+                chosen = jnp.where(mask > 0.5, slot, chosen)
+            out_ref[p, :, cols] = chosen.astype(jnp.bfloat16)
+
+
+def project_kernel(n_head, n_rep, modulation_ref, parts_ref, *refs):
+    weights, out_ref = refs[:-1], refs[-1]
+    head, rep = lax.axis_index("head"), lax.axis_index("rep")
     width = out_ref.shape[1]
+    parts = []
+    for d in range(n_head * n_rep):
+        source_head = lax.rem(head + n_head - d // n_rep, n_head)
+        parts.append(parts_ref[source_head * n_rep + lax.rem(rep + n_rep - d % n_rep, n_rep)])
     for start in range(0, width, COLUMNS):
         cols = slice(start, start + COLUMNS)
         total = sum(
-            jnp.dot(part[...], weight[:, cols], preferred_element_type=jnp.float32)
+            jnp.dot(part, weight[:, cols], preferred_element_type=jnp.float32)
             for part, weight in zip(parts, weights)
         )
         out_ref[:, cols] = total * modulation_ref[2:3, cols]
@@ -302,13 +305,8 @@
     def along_rep(x, shift):
         return lax.ppermute(x, "rep", [(i, (i + shift) % n_rep) for i in range(n_rep)])
 
-    def in_frame(x, d):
-        pairs = []
-        for h in range(n_head):
-            for r in range(n_rep):
-                to = ((h + d // n_rep) % n_head) * n_rep + (r + d % n_rep) % n_rep
-                pairs.append((h * n_rep + r, to))
-        return lax.ppermute(x, ("head", "rep"), pairs)
+    def exchange(x, axes):
+        return lax.all_to_all(x, axes, 0, 0, tiled=True)
 
     across = [along_head(out_weight, dh) for dh in range(1, n_head)]
 
@@ -333,7 +331,7 @@
     arrived = [along_frame(slots[s], s) for s in range(1, n_frame)]
 
     keys, values_t, masks = pl.pallas_call(
-        functools.partial(key_value_kernel, n_frame, n_head, n_rep),
+        functools.partial(key_value_kernel, n_frame, n_place),
         out_shape=[
             jax.ShapeDtypeStruct((tokens, width), half),
             jax.ShapeDtypeStruct((width, tokens), half),
@@ -357,72 +355,65 @@
         name="keys_values",
     )(block_worker, latents, modulation, key_weight, value_weight, key_cache, value_cache)
 
-    mine = pl.pallas_call(
+    copies = pl.pallas_call(
         collect_kernel,
-        out_shape=jax.ShapeDtypeStruct((block_rows, width), half),
+        out_shape=jax.ShapeDtypeStruct((n_frame, block_rows, width), half),
         in_specs=[VMEM] * n_frame + [ANY],
         out_specs=VMEM,
         compiler_params=params(16),
-        cost_estimate=cost(n_frame * block_rows * width, 2 * n_frame * block_rows * width),
+        cost_estimate=cost(n_frame * block_rows * width, 4 * n_frame * block_rows * width),
         name="collect",
     )(slots[0], *arrived, masks)
-
-    def attend(queries, after=()):
-        count = len(queries)
-        return pl.pallas_call(
-            functools.partial(attend_kernel, count),
-            out_shape=[jax.ShapeDtypeStruct((width + tail, block_rows), half)] * count,
-            in_specs=[VMEM] * (count + 2) + [ANY] * len(after),
-            out_specs=[VMEM] * count,
-            compiler_params=params(16),
-            cost_estimate=cost(
-                4 * tokens * block_rows * width * count,
-                4 * tokens * width,
-                tokens * block_rows * width // HD * count,
-            ),
-            name="attend",
-        )(*queries, keys, values_t, *after)
-
-    partial = list(attend([mine]))
-    shared = [along_frame(mine, s) for s in range(1, n_frame)]
-    for start in range(0, n_frame - 1, SLOTS):
-        partial += attend(shared[start : start + SLOTS], partial[:1])
-    gathered = partial[:1] + [along_frame(partial[s], n_frame - s) for s in range(1, n_frame)]
-    attended, *across = pl.pallas_call(
-        functools.partial(combine_kernel, n_frame),
-        out_shape=[jax.ShapeDtypeStruct((block_rows, width), half)]
+    queries = exchange(copies, "frame")
+    partial = pl.pallas_call(
+        attend_kernel,
+        out_shape=jax.ShapeDtypeStruct((n_frame, width + tail, block_rows), half),
+        in_specs=[VMEM] * 3,
+        out_specs=VMEM,
+        compiler_params=params(16),
+        cost_estimate=cost(
+            4 * tokens * block_rows * width * n_frame,
+            4 * tokens * width,
+            tokens * block_rows * width // HD * n_frame,
+        ),
+        name="attend",
+    )(queries, keys, values_t)
+    gathered = exchange(partial, "frame")
+    copies, *across = pl.pallas_call(
+        combine_kernel,
+        out_shape=[jax.ShapeDtypeStruct((n_frame, block_rows, width), half)]
         + [jax.ShapeDtypeStruct(w.shape, w.dtype) for w in across],
-        in_specs=[VMEM] * n_frame + [ANY] * len(across),
+        in_specs=[VMEM] + [ANY] * len(across),
         out_specs=[VMEM] + [ANY] * len(across),
-        input_output_aliases={n_frame + h: 1 + h for h in range(len(across))},
+        input_output_aliases={1 + h: 1 + h for h in range(len(across))},
         compiler_params=params(16),
         cost_estimate=cost(4 * n_frame * block_rows * width, 2 * n_frame * block_rows * width),
         name="combine",
-    )(*gathered, *across)
-    copies = [attended] + [along_frame(attended, s) for s in range(1, n_frame)]
+    )(gathered, *across)
+    attended = exchange(copies, "frame")
     pieces = pl.pallas_call(
-        functools.partial(select_kernel, n_frame, n_head, n_rep),
-        out_shape=[jax.ShapeDtypeStruct((own_rows, width), half)] * n_place,
-        in_specs=[VMEM] * (n_frame + 1),
-        out_specs=[VMEM] * n_place,
+        functools.partial(select_kernel, n_place),
+        out_shape=jax.ShapeDtypeStruct((n_place, own_rows, width), half),
+        in_specs=[VMEM] * 2,
+        out_specs=VMEM,
         compiler_params=params(16),
         cost_estimate=cost(0, 4 * n_frame * block_rows * width),
         name="select",
-    )(*copies, masks)
-    pieces = [pieces[0]] + [in_frame(pieces[d], d) for d in range(1, n_place)]
+    )(attended, masks)
+    pieces = exchange(pieces, ("head", "rep"))
 
     weights = []
     for held in [out_weight] + across:
         weights += [held] + [along_rep(held, dr) for dr in range(1, n_rep)]
     return pl.pallas_call(
-        project_kernel,
+        functools.partial(project_kernel, n_head, n_rep),
         out_shape=jax.ShapeDtypeStruct((own_rows, model), jnp.float32),
-        in_specs=[VMEM] * (1 + 2 * n_place),
+        in_specs=[VMEM] * (2 + n_place),
         out_specs=VMEM,
         compiler_params=params(16),
         cost_estimate=cost(2 * own_rows * model * width * n_place, 2 * model * width * n_place),
         name="project",
-    )(modulation, *pieces, *weights)
+    )(modulation, pieces, *weights)
 
 
 def solution(mesh):

time: 51.1 us -> 65.6 us (1.28)
  blocking collectives: 0 us -> 12.6 us
  Pallas kernels: 10.8 us -> 12.3 us
  starting transfers between devices: 19.3 us -> 20.3 us
  waiting for transfers between devices: 20.7 us -> 19.7 us
    ppermute x12 -> x3, waiting for transfers between devices: 17.1 us -> 0.01 us  [along_frame(): lax.ppermute(x, 'frame', [(i, (i + shift) % n_frame) for i in range(n_fra...]
    all_to_all x0 -> x3, waiting for transfers between devices: none -> 14.9 us  [exchange(): return lax.all_to_all(x, axes, 0, 0, tiled=True)]
    all_to_all x0 -> x1, blocking collectives: none -> 12.6 us  [exchange(): return lax.all_to_all(x, axes, 0, 0, tiled=True)]
    all_to_all x0 -> x3, starting transfers between devices: none -> 10.3 us  [exchange(): return lax.all_to_all(x, axes, 0, 0, tiled=True)]
    ppermute x12 -> x3, starting transfers between devices: 14.3 us -> 8.37 us  [along_frame(): lax.ppermute(x, 'frame', [(i, (i + shift) % n_frame) for i in range(n_fra...]
    ppermute x1, waiting for transfers between devices: 0.01 us -> 4.78 us  [along_head(): lax.ppermute(x, 'head', [(i, (i + shift) % n_head) for i in range(n_head)])]
    ppermute x3 -> x0, waiting for transfers between devices: 3.59 us -> none  [in_frame(): return lax.ppermute(x, ('head', 'rep'), pairs)]
    ppermute x3 -> x0, starting transfers between devices: 1.94 us -> none  [in_frame(): return lax.ppermute(x, ('head', 'rep'), pairs)]
  transfers between devices with their start and end apart: 18 -> 9, of which waited for: 9 -> 4; matrix products, arithmetic and copies ran while one was open for 0% -> 0% of each run, Pallas kernels for 18% -> 11%
where the time goes in v3:
time: 65.6 us; the launch traced here: 65.1 us
  starting transfers between devices  20.3 us (31%)
  waiting for transfers between devices  19.7 us (30%)
  blocking collectives  12.6 us (19%)
  Pallas kernels  12.3 us (19%)
    all_to_all x3, waiting for transfers between devices, exchange(): return lax.all_to_all(x, axes, 0, 0, tiled=True)  14.9 us
    all_to_all x1, blocking collectives, exchange(): return lax.all_to_all(x, axes, 0, 0, tiled=True)  12.6 us
    all_to_all x3, starting transfers between devices, exchange(): return lax.all_to_all(x, axes, 0, 0, tiled=True)  10.3 us
    ppermute x3, starting transfers between devices, along_frame(): lax.ppermute(x, 'frame', [(i, (i + shift) % n_frame) for i in range(n_fra...  8.37 us
    ppermute x1, waiting for transfers between devices, along_head(): lax.ppermute(x, 'head', [(i, (i + shift) % n_head) for i in range(n_head)])  4.78 us
    pallas_call x1, Pallas kernels, per_device(): pl.pallas_call(functools.partial(key_value_kernel, n_frame, n_place), out...  4.07 us
    pallas_call x1, Pallas kernels, per_device(): pl.pallas_call(functools.partial(query_kernel, n_frame), out_shape=[jax.S...  3.08 us
    pallas_call x1, Pallas kernels, per_device(): pl.pallas_call(attend_kernel, out_shape=jax.ShapeDtypeStruct((n_frame, wi...  1.92 us
  transfers between devices with their start and end apart: 9, of which 4 were waited for; matrix products, arithmetic and copies ran while one was open for 0% of the time, Pallas kernels for 11%

profile of v3, /device:TPU:0, one launch (start us, length us, event | category | flops | bytes accessed | tf_op | source)
XLA Modules:
  0.0 65.1 jit_solution(7663860347630975159)
XLA Ops:
  0.0 0.0 copy-start.4
  0.0 3.1 %queries.1 = (bf16[128,256]{1,0:T(8,128)(2,1)}, bf16[128,256]{1,0:T(8,128)(2,1)}, bf16[128,256]{1,0:T(8,128)(2,1)}, bf16[128,256]{1,0:T(8,128)(2,1)}) custom-call(s32[4]{0:T(128)} %worker_in.3, bf16[512,1536]{1,0:T(8,128)(2,1)} %latents_in.3, f32[3,1536]{1,0:T(4,128)} %modulation_ref.1, bf16[1536,256]{1,0:T(8,128)(2,1)} %weight_in.1), custom_call_target="tpu_custom_call" | custom-call | flops 402653184 | bytes 2359296 | tf_op jit(solution)/shard_map/queries/pallas_call | solution.py:313
  3.1 3.1 %collective-permute-start = (bf16[128,256]{1,0:T(8,128)(2,1)}, bf16[128,256]{1,0:T(8,128)(2,1)S(1)}, u32[]{:S(2)}, u32[]{:S(2)}) collective-permute-start(bf16[128,256]{1,0:T(8,128)(2,1)} %get-tuple-element.15), channel_id=1, source_target_pairs={{0,4},{4,8},{8,12},{12,0},{1,5},{5,9},{9,13},{13,1},{2,6},{6,10},{... | collective-permute-start | bytes 196616 | tf_op jit(solution)/shard_map/ppermute | solution.py:300
  6.2 2.6 %collective-permute-start.1 = (bf16[128,256]{1,0:T(8,128)(2,1)}, bf16[128,256]{1,0:T(8,128)(2,1)S(1)}, u32[]{:S(2)}, u32[]{:S(2)}) collective-permute-start(bf16[128,256]{1,0:T(8,128)(2,1)} %get-tuple-element.16), channel_id=1, source_target_pairs={{0,8},{4,12},{8,0},{12,4},{1,9},{5,13},{9,1},{13,5},{2,10},{6,14},... | collective-permute-start | bytes 196616 | tf_op jit(solution)/shard_map/ppermute | solution.py:300
  8.8 2.7 %collective-permute-start.2 = (bf16[128,256]{1,0:T(8,128)(2,1)}, bf16[128,256]{1,0:T(8,128)(2,1)S(1)}, u32[]{:S(2)}, u32[]{:S(2)}) collective-permute-start(bf16[128,256]{1,0:T(8,128)(2,1)} %get-tuple-element.17), channel_id=1, source_target_pairs={{0,12},{4,0},{8,4},{12,8},{1,13},{5,1},{9,5},{13,9},{2,14},{6,2},{... | collective-permute-start | bytes 196616 | tf_op jit(solution)/shard_map/ppermute | solution.py:300
  11.5 0.0 copy-done.2
  11.5 0.0 copy-done.4
  11.5 0.0 copy-done.1
  11.5 4.1 %keys_values.1 = (bf16[512,256]{1,0:T(8,128)(2,1)S(1)}, bf16[256,512]{1,0:T(8,128)(2,1)S(1)}, f32[16,128]{1,0:T(8,128)S(1)}) custom-call(s32[4]{0:T(128)S(1)} %copy-done.4, bf16[512,1536]{1,0:T(8,128)(2,1)} %latents_in.3, f32[3,1536]{1,0:T(4,128)S(1)} %copy-done.2, bf16[1536,256]{1,0:T(8,128)(2,1)} %key_weight_in.1, bf16[1536,256]{1,0:T(8,128)(2,1)} %value_weight_in.1, ...), custom_call_target="tpu_custom_call" | custom-call | flops 805306368 | bytes 3145728 | tf_op jit(solution)/shard_map/keys_values/pallas_call | solution.py:333
  15.6 0.0 collective-permute-done.refs_1_
  15.6 0.0 collective-permute-done.1.refs_2_
  15.6 0.0 collective-permute-done.2.refs_3_
  15.6 0.0 copy-done.3
  15.6 0.7 %collect.1 = bf16[4,128,256]{2,1,0:T(8,128)(2,1)} custom-call(bf16[128,256]{1,0:T(8,128)(2,1)S(1)} %copy-done.3, bf16[128,256]{1,0:T(8,128)(2,1)S(1)} %collective-permute-done.refs_1_, bf16[128,256]{1,0:T(8,128)(2,1)S(1)} %collective-permute-done.1.refs_2_, bf16[128,256]{1,0:T(8,128)(2,1)S(1)} %collective-permute-done.2.refs_3_, ...), custom_call_target="tpu_custom_call" | custom-call | flops 131072 | bytes 524288 | tf_op jit(solution)/shard_map/collect/pallas_call | solution.py:358
  16.3 3.4 %all-to-all-start = ((bf16[4,128,256]{2,1,0:T(8,128)(2,1)}), bf16[4,128,256]{2,1,0:T(8,128)(2,1)S(1)}, u32[]{:S(2)}, u32[]{:S(2)}) async-start(bf16[4,128,256]{2,1,0:T(8,128)(2,1)} %collect.1), calls=%async_computation | async-start | bytes 524288 | tf_op jit(solution)/shard_map/all_to_all | solution.py:309
  19.8 0.0 copy-done
  19.8 1.6 %collective-permute-start.3 = (bf16[256,1536]{1,0:T(8,128)(2,1)S(1)}, bf16[256,1536]{1,0:T(8,128)(2,1)S(1)}, u32[]{:S(2)}, u32[]{:S(2)}) collective-permute-start(bf16[256,1536]{1,0:T(8,128)(2,1)S(1)} %copy-done), channel_id=1, source_target_pairs={{0,2},{2,0},{1,3},{3,1},{4,6},{6,4},{5,7},{7,5},{8,10},{10,8},{9,1... | collective-permute-start | bytes 2359304 | tf_op jit(solution)/shard_map/ppermute | solution.py:303
  21.3 6.7 %all-to-all-done.queries_ref = bf16[4,128,256]{2,1,0:T(8,128)(2,1)S(1)} async-done(((bf16[4,128,256]{2,1,0:T(8,128)(2,1)}), bf16[4,128,256]{2,1,0:T(8,128)(2,1)S(1)}, u32[]{:S(2)}, u32[]{:S(2)}) %all-to-all-start) | async-done | bytes 262176 | tf_op jit(solution)/shard_map/all_to_all | solution.py:309
  28.0 1.9 %attend.1 = bf16[4,272,128]{2,1,0:T(8,128)(2,1)} custom-call(bf16[4,128,256]{2,1,0:T(8,128)(2,1)S(1)} %all-to-all-done.queries_ref, bf16[512,256]{1,0:T(8,128)(2,1)S(1)} %get-tuple-element.19.keys_ref, bf16[256,512]{1,0:T(8,128)(2,1)S(1)} %get-tuple-element.20.values_t_ref), custom_call_target="tpu_custom_call" | custom-call | flops 268435456 | bytes 524288 | tf_op jit(solution)/shard_map/attend/pallas_call | solution.py:368
  30.0 3.5 %all-to-all-start.1 = ((bf16[4,272,128]{2,1,0:T(8,128)(2,1)}), bf16[4,272,128]{2,1,0:T(8,128)(2,1)S(1)}, u32[]{:S(2)}, u32[]{:S(2)}) async-start(bf16[4,272,128]{2,1,0:T(8,128)(2,1)} %attend.1), calls=%async_computation.1 | async-start | bytes 557056 | tf_op jit(solution)/shard_map/all_to_all | solution.py:309
  33.4 0.1 collective-permute-start.4
  33.5 4.8 %collective-permute-done.3.refs_0_ = bf16[256,1536]{1,0:T(8,128)(2,1)S(1)} collective-permute-done((bf16[256,1536]{1,0:T(8,128)(2,1)S(1)}, bf16[256,1536]{1,0:T(8,128)(2,1)S(1)}, u32[]{:S(2)}, u32[]{:S(2)}) %collective-permute-start.3) | collective-permute-done | bytes 786464 | tf_op jit(solution)/shard_map/ppermute | solution.py:303
  38.3 2.2 %all-to-all-done.1.parts_ref = bf16[4,272,128]{2,1,0:T(8,128)(2,1)S(1)} async-done(((bf16[4,272,128]{2,1,0:T(8,128)(2,1)}), bf16[4,272,128]{2,1,0:T(8,128)(2,1)S(1)}, u32[]{:S(2)}, u32[]{:S(2)}) %all-to-all-start.1) | async-done | bytes 278560 | tf_op jit(solution)/shard_map/all_to_all | solution.py:309
  40.5 0.1 combine.1
  40.7 0.1 collective-permute-start.5
  40.7 12.6 %all_to_all.20.slots_ref = bf16[4,128,256]{2,1,0:T(8,128)(2,1)S(1)} all-to-all(bf16[4,128,256]{2,1,0:T(8,128)(2,1)S(1)} %get-tuple-element.21), channel_id=1, replica_groups=mesh['groups'=2,'frame'=4,'head'=2,'rep'=2] {'frame'}, dimensions={0} | all-to-all | bytes 524288 | tf_op jit(solution)/shard_map/all_to_all | solution.py:309
  53.4 0.9 %select.1 = bf16[4,128,256]{2,1,0:T(8,128)(2,1)} custom-call(bf16[4,128,256]{2,1,0:T(8,128)(2,1)S(1)} %all_to_all.20.slots_ref, f32[16,128]{1,0:T(8,128)S(1)} %get-tuple-element.18.refs_4_.masks_ref), custom_call_target="tpu_custom_call" | custom-call | bytes 524288 | tf_op jit(solution)/shard_map/select/pallas_call | solution.py:394
  54.3 3.4 %all-to-all-start.3 = ((bf16[4,128,256]{2,1,0:T(8,128)(2,1)}), bf16[4,128,256]{2,1,0:T(8,128)(2,1)S(1)}, u32[]{:S(2)}, u32[]{:S(2)}) async-start(bf16[4,128,256]{2,1,0:T(8,128)(2,1)} %select.1), calls=%async_computation.3 | async-start | bytes 524288 | tf_op jit(solution)/shard_map/all_to_all | solution.py:309
  57.7 0.0 collective-permute-done.4.refs_1_
  57.7 6.0 %all-to-all-done.3.parts_ref = bf16[4,128,256]{2,1,0:T(8,128)(2,1)S(1)} async-done(((bf16[4,128,256]{2,1,0:T(8,128)(2,1)}), bf16[4,128,256]{2,1,0:T(8,128)(2,1)S(1)}, u32[]{:S(2)}, u32[]{:S(2)}) %all-to-all-start.3) | async-done | bytes 262176 | tf_op jit(solution)/shard_map/all_to_all | solution.py:309
  63.7 0.0 collective-permute-done.5.refs_3_
  63.7 1.5 %project.1 = f32[128,1536]{1,0:T(8,128)} custom-call(f32[3,1536]{1,0:T(4,128)S(1)} %copy-done.2, bf16[4,128,256]{2,1,0:T(8,128)(2,1)S(1)} %all-to-all-done.3.parts_ref, bf16[256,1536]{1,0:T(8,128)(2,1)S(1)} %copy-done, bf16[256,1536]{1,0:T(8,128)(2,1)S(1)} %collective-permute-done.4.refs_1_, bf16[256,1536]{1,0:T(8,128)(2,1)S(1)} %get-tuple-element.22.refs_2_, ...), custom_call_target="tpu_custom_call" | custom-call | flops 402653184 | bytes 3145728 | tf_op jit(solution)/shard_map/project/pallas_call | solution.py:408
  (4 shorter events, 0.0 us)
Async XLA Ops:
  0.0 11.5 %copy-start.2 = (f32[3,1536]{1,0:T(4,128)S(1)}, f32[3,1536]{1,0:T(4,128)}, u32[]{:S(2)}) copy-start(f32[3,1536]{1,0:T(4,128)} %modulation_ref.1) | copy-start | bytes 55300
  0.0 11.5 %copy-start.4 = (s32[4]{0:T(128)S(1)}, s32[4]{0:T(128)}, u32[]{:S(2)}) copy-start(s32[4]{0:T(128)} %worker_in.3) | copy-start | bytes 52
  0.0 11.5 %copy-start.1 = (bf16[512,256]{1,0:T(8,128)(2,1)S(1)}, bf16[512,256]{1,0:T(8,128)(2,1)}, u32[]{:S(2)}) copy-start(bf16[512,256]{1,0:T(8,128)(2,1)} %key_cache_in.1) | copy-start | bytes 786436
  3.1 12.5 %collective-permute-start = (bf16[128,256]{1,0:T(8,128)(2,1)}, bf16[128,256]{1,0:T(8,128)(2,1)S(1)}, u32[]{:S(2)}, u32[]{:S(2)}) collective-permute-start(bf16[128,256]{1,0:T(8,128)(2,1)} %get-tuple-element.15), channel_id=1, source_target_pairs={{0,4},{4,8},{8,12},{12,0},{1,5},{5,9},{9,13},{13,1},{2,6},{6,10},{... | collective-permute-start | bytes 196616 | tf_op jit(solution)/shard_map/ppermute | solution.py:300
  6.2 9.4 %collective-permute-start.1 = (bf16[128,256]{1,0:T(8,128)(2,1)}, bf16[128,256]{1,0:T(8,128)(2,1)S(1)}, u32[]{:S(2)}, u32[]{:S(2)}) collective-permute-start(bf16[128,256]{1,0:T(8,128)(2,1)} %get-tuple-element.16), channel_id=1, source_target_pairs={{0,8},{4,12},{8,0},{12,4},{1,9},{5,13},{9,1},{13,5},{2,10},{6,14},... | collective-permute-start | bytes 196616 | tf_op jit(solution)/shard_map/ppermute | solution.py:300
  8.8 6.8 %copy-start.3 = (bf16[128,256]{1,0:T(8,128)(2,1)S(1)}, bf16[128,256]{1,0:T(8,128)(2,1)}, u32[]{:S(2)}) copy-start(bf16[128,256]{1,0:T(8,128)(2,1)} %get-tuple-element.14.refs_0_) | copy-start | bytes 196612
  8.8 11.0 %copy-start = (bf16[256,1536]{1,0:T(8,128)(2,1)S(1)}, bf16[256,1536]{1,0:T(8,128)(2,1)}, u32[]{:S(2)}) copy-start(bf16[256,1536]{1,0:T(8,128)(2,1)} %refs_0_.1) | copy-start | bytes 2359300
  8.8 6.8 %collective-permute-start.2 = (bf16[128,256]{1,0:T(8,128)(2,1)}, bf16[128,256]{1,0:T(8,128)(2,1)S(1)}, u32[]{:S(2)}, u32[]{:S(2)}) collective-permute-start(bf16[128,256]{1,0:T(8,128)(2,1)} %get-tuple-element.17), channel_id=1, source_target_pairs={{0,12},{4,0},{8,4},{12,8},{1,13},{5,1},{9,5},{13,9},{2,14},{6,2},{... | collective-permute-start | bytes 196616 | tf_op jit(solution)/shard_map/ppermute | solution.py:300
  16.3 11.7 %all-to-all-start = ((bf16[4,128,256]{2,1,0:T(8,128)(2,1)}), bf16[4,128,256]{2,1,0:T(8,128)(2,1)S(1)}, u32[]{:S(2)}, u32[]{:S(2)}) async-start(bf16[4,128,256]{2,1,0:T(8,128)(2,1)} %collect.1), calls=%async_computation | async-start | bytes 524288 | tf_op jit(solution)/shard_map/all_to_all | solution.py:309
  19.8 18.5 %collective-permute-start.3 = (bf16[256,1536]{1,0:T(8,128)(2,1)S(1)}, bf16[256,1536]{1,0:T(8,128)(2,1)S(1)}, u32[]{:S(2)}, u32[]{:S(2)}) collective-permute-start(bf16[256,1536]{1,0:T(8,128)(2,1)S(1)} %copy-done), channel_id=1, source_target_pairs={{0,2},{2,0},{1,3},{3,1},{4,6},{6,4},{5,7},{7,5},{8,10},{10,8},{9,1... | collective-permute-start | bytes 2359304 | tf_op jit(solution)/shard_map/ppermute | solution.py:303
  30.0 10.6 %all-to-all-start.1 = ((bf16[4,272,128]{2,1,0:T(8,128)(2,1)}), bf16[4,272,128]{2,1,0:T(8,128)(2,1)S(1)}, u32[]{:S(2)}, u32[]{:S(2)}) async-start(bf16[4,272,128]{2,1,0:T(8,128)(2,1)} %attend.1), calls=%async_computation.1 | async-start | bytes 557056 | tf_op jit(solution)/shard_map/all_to_all | solution.py:309
  33.4 24.3 %collective-permute-start.4 = (bf16[256,1536]{1,0:T(8,128)(2,1)S(1)}, bf16[256,1536]{1,0:T(8,128)(2,1)S(1)}, u32[]{:S(2)}, u32[]{:S(2)}) collective-permute-start(bf16[256,1536]{1,0:T(8,128)(2,1)S(1)} %copy-done), channel_id=1, source_target_pairs={{0,1},{1,0},{2,3},{3,2},{4,5},{5,4},{6,7},{7,6},{8,9},{9,8},{10,11... | collective-permute-start | bytes 2359304 | tf_op jit(solution)/shard_map/ppermute | solution.py:306
  40.7 23.0 %collective-permute-start.5 = (bf16[256,1536]{1,0:T(8,128)(2,1)S(1)}, bf16[256,1536]{1,0:T(8,128)(2,1)S(1)}, u32[]{:S(2)}, u32[]{:S(2)}) collective-permute-start(bf16[256,1536]{1,0:T(8,128)(2,1)S(1)} %get-tuple-element.22.refs_2_), channel_id=1, source_target_pairs={{0,1},{1,0},{2,3},{3,2},{4,5},{5,4},{6,7},{7,6},{8,9},{9,8},{10,11... | collective-permute-start | bytes 2359304 | tf_op jit(solution)/shard_map/ppermute | solution.py:306
  54.3 9.4 %all-to-all-start.3 = ((bf16[4,128,256]{2,1,0:T(8,128)(2,1)}), bf16[4,128,256]{2,1,0:T(8,128)(2,1)S(1)}, u32[]{:S(2)}, u32[]{:S(2)}) async-start(bf16[4,128,256]{2,1,0:T(8,128)(2,1)} %select.1), calls=%async_computation.3 | async-start | bytes 524288 | tf_op jit(solution)/shard_map/all_to_all | solution.py:309

commit v4 on v2

--- a/solution.py
+++ b/solution.py
@@ -11,7 +11,6 @@
 EPS = 1e-06
 CHUNK = 16
 COLUMNS = 512
-SLOTS = 3
 TAIL = 16
 MIB = 1 << 20
 
@@ -72,10 +71,9 @@
     ).astype(jnp.bfloat16)
     for j in range(n_local):
         worker = worker_ref[j]
-        away = lax.rem(worker - frame + n_frame, n_frame)
         for s in range(n_frame):
 
-            @pl.when((worker >= 0) & (away == s))
+            @pl.when((worker >= 0) & (jnp.bitwise_xor(frame, s) == worker))
             def _():
                 outs[s][...] = queries_ref[blocks[j], :]
 
@@ -128,10 +126,10 @@
     for d in range(n_place):
         target = lax.rem(head + d // n_rep, n_head) * n_rep + lax.rem(rep + d % n_rep, n_rep)
         worker = worker_ref[target * (tokens // n_place) // block_rows]
-        away = jnp.where(worker < 0, -1, lax.rem(frame - worker + n_frame, n_frame))
         for s in range(n_frame):
+            held = (worker >= 0) & (jnp.bitwise_xor(frame, s) == worker)
             masks_ref[d * n_frame + s : d * n_frame + s + 1, :] = jnp.full(
-                (1, masks_ref.shape[1]), jnp.where(away == s, 1.0, 0.0), jnp.float32
+                (1, masks_ref.shape[1]), jnp.where(held, 1.0, 0.0), jnp.float32
             )
     for j in range(n_local):
 
@@ -176,13 +174,8 @@
     out_ref[...] = sum(part[...].astype(jnp.float32) for part in parts).astype(jnp.bfloat16)
 
 
-def attend_kernel(count, *refs):
-    keys_ref, values_t_ref = refs[count : count + 2]
-    for queries_ref, out_ref in zip(refs[:count], refs[-count:]):
-        attend_slot(queries_ref, keys_ref, values_t_ref, out_ref)
-
-
-def attend_slot(queries_ref, keys_ref, values_t_ref, out_ref):
+def attend_kernel(queries_ref, keys_ref, values_t_ref, *refs):
+    out_ref = refs[len(refs) // 2]
     width = keys_ref.shape[1]
     stats = []
     for h in range(width // HD):
@@ -208,8 +201,8 @@
     out_ref[width:, :] = tail.astype(jnp.bfloat16)
 
 
-def combine_kernel(n_frame, *refs):
-    parts, out_ref = refs[:n_frame], refs[n_frame + (len(refs) - n_frame - 1) // 2]
+def combine_kernel(*refs):
+    parts, out_ref = refs[:-1], refs[-1]
     width = out_ref.shape[1]
     tails = [part[width:, :].astype(jnp.float32) for part in parts]
     for h in range(width // HD):
@@ -230,7 +223,9 @@
 
 
 def select_kernel(n_frame, n_head, n_rep, *refs):
-    slots, masks_ref, outs = refs[:n_frame], refs[n_frame], refs[n_frame + 1 :]
+    slots, masks_ref = refs[:n_frame], refs[n_frame]
+    first = len(refs) - (len(refs) - n_frame - 1 - n_head * n_rep) // 2 - n_head * n_rep
+    outs = refs[first : first + n_head * n_rep]
     block_rows, width = slots[0].shape
     rows = outs[0].shape[0]
     head, rep = lax.axis_index("head"), lax.axis_index("rep")
@@ -293,8 +288,8 @@
     tail = TAIL * -(-6 * (width // HD) // TAIL)
     half = jnp.bfloat16
 
-    def along_frame(x, shift):
-        return lax.ppermute(x, "frame", [(i, (i + shift) % n_frame) for i in range(n_frame)])
+    def along_frame(x, s):
+        return lax.ppermute(x, "frame", [(i, i ^ s) for i in range(n_frame)])
 
     def along_head(x, shift):
         return lax.ppermute(x, "head", [(i, (i + shift) % n_head) for i in range(n_head)])
@@ -367,48 +362,48 @@
         name="collect",
     )(slots[0], *arrived, masks)
 
-    def attend(queries, after=()):
-        count = len(queries)
+    def attend(queries, through=()):
         return pl.pallas_call(
-            functools.partial(attend_kernel, count),
-            out_shape=[jax.ShapeDtypeStruct((width + tail, block_rows), half)] * count,
-            in_specs=[VMEM] * (count + 2) + [ANY] * len(after),
-            out_specs=[VMEM] * count,
+            attend_kernel,
+            out_shape=[jax.ShapeDtypeStruct((width + tail, block_rows), half)]
+            + [jax.ShapeDtypeStruct(w.shape, w.dtype) for w in through],
+            in_specs=[VMEM] * 3 + [ANY] * len(through),
+            out_specs=[VMEM] + [ANY] * len(through),
+            input_output_aliases={3 + i: 1 + i for i in range(len(through))},
             compiler_params=params(16),
             cost_estimate=cost(
-                4 * tokens * block_rows * width * count,
-                4 * tokens * width,
-                tokens * block_rows * width // HD * count,
+                4 * tokens * block_rows * width,
+                20 * tokens * width,
+                tokens * block_rows * width // HD,
             ),
             name="attend",
-        )(*queries, keys, values_t, *after)
-
-    partial = list(attend([mine]))
+        )(queries, keys, values_t, *through)
+
     shared = [along_frame(mine, s) for s in range(1, n_frame)]
-    for start in range(0, n_frame - 1, SLOTS):
-        partial += attend(shared[start : start + SLOTS], partial[:1])
-    gathered = partial[:1] + [along_frame(partial[s], n_frame - s) for s in range(1, n_frame)]
-    attended, *across = pl.pallas_call(
-        functools.partial(combine_kernel, n_frame),
-        out_shape=[jax.ShapeDtypeStruct((block_rows, width), half)]
-        + [jax.ShapeDtypeStruct(w.shape, w.dtype) for w in across],
-        in_specs=[VMEM] * n_frame + [ANY] * len(across),
-        out_specs=[VMEM] + [ANY] * len(across),
-        input_output_aliases={n_frame + h: 1 + h for h in range(len(across))},
+    sent = [along_frame(attend(queries)[0], s) for s, queries in enumerate(shared, 1)]
+    (own,) = attend(mine)
+    attended = pl.pallas_call(
+        combine_kernel,
+        out_shape=jax.ShapeDtypeStruct((block_rows, width), half),
+        in_specs=[VMEM] * n_frame,
+        out_specs=VMEM,
         compiler_params=params(16),
         cost_estimate=cost(4 * n_frame * block_rows * width, 2 * n_frame * block_rows * width),
         name="combine",
-    )(*gathered, *across)
+    )(own, *sent)
     copies = [attended] + [along_frame(attended, s) for s in range(1, n_frame)]
     pieces = pl.pallas_call(
         functools.partial(select_kernel, n_frame, n_head, n_rep),
-        out_shape=[jax.ShapeDtypeStruct((own_rows, width), half)] * n_place,
-        in_specs=[VMEM] * (n_frame + 1),
-        out_specs=[VMEM] * n_place,
+        out_shape=[jax.ShapeDtypeStruct((own_rows, width), half)] * n_place
+        + [jax.ShapeDtypeStruct(w.shape, w.dtype) for w in across],
+        in_specs=[VMEM] * (n_frame + 1) + [ANY] * len(across),
+        out_specs=[VMEM] * n_place + [ANY] * len(across),
+        input_output_aliases={n_frame + 1 + i: n_place + i for i in range(len(across))},
         compiler_params=params(16),
         cost_estimate=cost(0, 4 * n_frame * block_rows * width),
         name="select",
-    )(*copies, masks)
+    )(*copies, masks, *across)
+    pieces, across = pieces[:n_place], list(pieces[n_place:])
     pieces = [pieces[0]] + [in_frame(pieces[d], d) for d in range(1, n_place)]
 
     weights = []

time: 51.1 us -> 48.6 us (0.951); the launches traced: 50.9 us -> 47.8 us
  waiting for transfers between devices: 20.7 us -> 10.4 us
  Pallas kernels: 10.8 us -> 14.7 us
  starting transfers between devices: 19.3 us -> 22.5 us
    ppermute x12, waiting for transfers between devices: 17.1 us -> 7.06 us  [along_frame(): return lax.ppermute(x, 'frame', [(i, i ^ s) for i in range(n_frame)])]
    ppermute x12, starting transfers between devices: 14.3 us -> 17.5 us  [along_frame(): return lax.ppermute(x, 'frame', [(i, i ^ s) for i in range(n_frame)])]
    pallas_call x1, Pallas kernels: 4.07 us -> 5.55 us  [per_device(): pl.pallas_call(functools.partial(key_value_kernel, n_frame, n_head, n_rep...]
    pallas_call x1, Pallas kernels: 3.04 us -> 4.38 us  [per_device(): pl.pallas_call(functools.partial(query_kernel, n_frame), out_shape=[jax.S...]
    pallas_call x3 -> x5, Pallas kernels: 1.95 us -> 3.08 us  [the longest x4 2.93 us: attend(): pl.pallas_call(attend_kernel, out_shape=[jax.ShapeDtypeStruct((width + ta...]
  transfers between devices with their start and end apart: 18 -> 18, of which waited for: 9 -> 6; matrix products, arithmetic and copies ran while one was open for 0% -> 0% of each run, Pallas kernels for 18% -> 28%
where the time goes in v4:
time: 48.6 us; the launch traced here: 47.8 us
  starting transfers between devices  22.5 us (46%)
  Pallas kernels  14.7 us (30%)
  waiting for transfers between devices  10.4 us (21%)
    ppermute x12, starting transfers between devices, along_frame(): return lax.ppermute(x, 'frame', [(i, i ^ s) for i in range(n_frame)])  17.5 us
    ppermute x12, waiting for transfers between devices, along_frame(): return lax.ppermute(x, 'frame', [(i, i ^ s) for i in range(n_frame)])  7.06 us
    pallas_call x1, Pallas kernels, per_device(): pl.pallas_call(functools.partial(key_value_kernel, n_frame, n_head, n_rep...  5.55 us
    pallas_call x1, Pallas kernels, per_device(): pl.pallas_call(functools.partial(query_kernel, n_frame), out_shape=[jax.S...  4.38 us
    ppermute x3, waiting for transfers between devices, in_frame(): return lax.ppermute(x, ('head', 'rep'), pairs)  3.35 us
    ppermute x1, starting transfers between devices, along_head(): lax.ppermute(x, 'head', [(i, (i + shift) % n_head) for i in range(n_head)])  3.01 us
    pallas_call x4, Pallas kernels, attend(): pl.pallas_call(attend_kernel, out_shape=[jax.ShapeDtypeStruct((width + ta...  2.93 us
    ppermute x3, starting transfers between devices, in_frame(): return lax.ppermute(x, ('head', 'rep'), pairs)  1.93 us
  transfers between devices with their start and end apart: 18, of which 6 were waited for; matrix products, arithmetic and copies ran while one was open for 0% of the time, Pallas kernels for 28%

profile of v4, /device:TPU:0, one launch (start us, length us, event | category | flops | bytes accessed | tf_op | source)
XLA Modules:
  0.0 47.8 jit_solution(6616013148866186872)
XLA Ops:
  0.0 3.0 %collective-permute-start.12 = (bf16[256,1536]{1,0:T(8,128)(2,1)}, bf16[256,1536]{1,0:T(8,128)(2,1)S(1)}, u32[]{:S(2)}, u32[]{:S(2)}) collective-permute-start(bf16[256,1536]{1,0:T(8,128)(2,1)} %refs_4_.1), channel_id=1, source_target_pairs={{0,2},{2,0},{1,3},{3,1},{4,6},{6,4},{5,7},{7,5},{8,10},{10,8},{9,1... | collective-permute-start | bytes 2359304 | tf_op jit(solution)/shard_map/ppermute | solution.py:295
  3.0 4.4 %queries.1 = (bf16[128,256]{1,0:T(8,128)(2,1)}, bf16[128,256]{1,0:T(8,128)(2,1)}, bf16[128,256]{1,0:T(8,128)(2,1)}, bf16[128,256]{1,0:T(8,128)(2,1)}) custom-call(s32[4]{0:T(128)} %worker_in.3, bf16[512,1536]{1,0:T(8,128)(2,1)} %latents_in.3, f32[3,1536]{1,0:T(4,128)} %modulation_ref.1, bf16[1536,256]{1,0:T(8,128)(2,1)} %weight_in.1), custom_call_target="tpu_custom_call" | custom-call | flops 402653184 | bytes 2359296 | tf_op jit(solution)/shard_map/queries/pallas_call | solution.py:310
  7.4 0.3 collective-permute-start
  7.7 2.6 %collective-permute-start.1 = (bf16[128,256]{1,0:T(8,128)(2,1)}, bf16[128,256]{1,0:T(8,128)(2,1)S(1)}, u32[]{:S(2)}, u32[]{:S(2)}) collective-permute-start(bf16[128,256]{1,0:T(8,128)(2,1)} %get-tuple-element.19), channel_id=1, source_target_pairs={{0,8},{4,12},{8,0},{12,4},{1,9},{5,13},{9,1},{13,5},{2,10},{6,14},... | collective-permute-start | bytes 196616 | tf_op jit(solution)/shard_map/ppermute | solution.py:292
  10.3 1.6 %collective-permute-start.2 = (bf16[128,256]{1,0:T(8,128)(2,1)}, bf16[128,256]{1,0:T(8,128)(2,1)S(1)}, u32[]{:S(2)}, u32[]{:S(2)}) collective-permute-start(bf16[128,256]{1,0:T(8,128)(2,1)} %get-tuple-element.20), channel_id=1, source_target_pairs={{0,12},{4,8},{8,4},{12,0},{1,13},{5,9},{9,5},{13,1},{2,14},{6,10},... | collective-permute-start | bytes 196616 | tf_op jit(solution)/shard_map/ppermute | solution.py:292
  11.9 5.5 %keys_values.1 = (bf16[512,256]{1,0:T(8,128)(2,1)S(1)}, bf16[256,512]{1,0:T(8,128)(2,1)S(1)}, f32[16,128]{1,0:T(8,128)S(1)}) custom-call(s32[4]{0:T(128)S(1)} %copy-done.4, bf16[512,1536]{1,0:T(8,128)(2,1)} %latents_in.3, f32[3,1536]{1,0:T(4,128)S(1)} %copy-done.2, bf16[1536,256]{1,0:T(8,128)(2,1)} %key_weight_in.1, bf16[1536,256]{1,0:T(8,128)(2,1)} %value_weight_in.1, ...), custom_call_target="tpu_custom_call" | custom-call | flops 805306368 | bytes 3145728 | tf_op jit(solution)/shard_map/keys_values/pallas_call | solution.py:330
  17.5 0.0 copy-start
  17.5 0.1 collective-permute-start.3
  17.6 1.3 %collective-permute-start.5 = (bf16[128,256]{1,0:T(8,128)(2,1)S(1)}, bf16[128,256]{1,0:T(8,128)(2,1)S(1)}, u32[]{:S(2)}, u32[]{:S(2)}) collective-permute-start(bf16[128,256]{1,0:T(8,128)(2,1)S(1)} %collect.1.queries_ref), channel_id=1, source_target_pairs={{0,8},{4,12},{8,0},{12,4},{1,9},{5,13},{9,1},{13,5},{2,10},{6,14},... | collective-permute-start | bytes 196616 | tf_op jit(solution)/shard_map/ppermute | solution.py:292
  18.9 3.0 %collective-permute-start.7 = (bf16[128,256]{1,0:T(8,128)(2,1)S(1)}, bf16[128,256]{1,0:T(8,128)(2,1)S(1)}, u32[]{:S(2)}, u32[]{:S(2)}) collective-permute-start(bf16[128,256]{1,0:T(8,128)(2,1)S(1)} %collect.1.queries_ref), channel_id=1, source_target_pairs={{0,12},{4,8},{8,4},{12,0},{1,13},{5,9},{9,5},{13,1},{2,14},{6,10},... | collective-permute-start | bytes 196616 | tf_op jit(solution)/shard_map/ppermute | solution.py:292
  22.0 0.7 %attend.5 = bf16[272,128]{1,0:T(8,128)(2,1)S(1)} custom-call(bf16[128,256]{1,0:T(8,128)(2,1)S(1)} %collective-permute-done.3.queries_ref, bf16[512,256]{1,0:T(8,128)(2,1)S(1)} %get-tuple-element.22.keys_ref, bf16[256,512]{1,0:T(8,128)(2,1)S(1)} %get-tuple-element.23.values_t_ref), custom_call_target="tpu_custom_call" | custom-call | flops 67108864 | bytes 2621440 | tf_op jit(solution)/shard_map/attend/pallas_call | solution.py:366
  22.7 0.1 collective-permute-start.4
  22.8 0.9 %collective-permute-done.5.queries_ref = bf16[128,256]{1,0:T(8,128)(2,1)S(1)} collective-permute-done((bf16[128,256]{1,0:T(8,128)(2,1)S(1)}, bf16[128,256]{1,0:T(8,128)(2,1)S(1)}, u32[]{:S(2)}, u32[]{:S(2)}) %collective-permute-start.5) | collective-permute-done | bytes 65568 | tf_op jit(solution)/shard_map/ppermute | solution.py:292
  23.7 0.7 %attend.6 = bf16[272,128]{1,0:T(8,128)(2,1)S(1)} custom-call(bf16[128,256]{1,0:T(8,128)(2,1)S(1)} %collective-permute-done.5.queries_ref, bf16[512,256]{1,0:T(8,128)(2,1)S(1)} %get-tuple-element.22.keys_ref, bf16[256,512]{1,0:T(8,128)(2,1)S(1)} %get-tuple-element.23.values_t_ref), custom_call_target="tpu_custom_call" | custom-call | flops 67108864 | bytes 2621440 | tf_op jit(solution)/shard_map/attend/pallas_call | solution.py:366
  24.5 1.0 %collective-permute-start.6 = (bf16[272,128]{1,0:T(8,128)(2,1)S(1)}, bf16[272,128]{1,0:T(8,128)(2,1)S(1)}, u32[]{:S(2)}, u32[]{:S(2)}) collective-permute-start(bf16[272,128]{1,0:T(8,128)(2,1)S(1)} %attend.6), channel_id=1, source_target_pairs={{0,8},{4,12},{8,0},{12,4},{1,9},{5,13},{9,1},{13,5},{2,10},{6,14},... | collective-permute-start | bytes 208904 | tf_op jit(solution)/shard_map/ppermute | solution.py:292
  25.5 0.7 %attend.7 = bf16[272,128]{1,0:T(8,128)(2,1)S(1)} custom-call(bf16[128,256]{1,0:T(8,128)(2,1)S(1)} %collective-permute-done.7.queries_ref, bf16[512,256]{1,0:T(8,128)(2,1)S(1)} %get-tuple-element.22.keys_ref, bf16[256,512]{1,0:T(8,128)(2,1)S(1)} %get-tuple-element.23.values_t_ref), custom_call_target="tpu_custom_call" | custom-call | flops 67108864 | bytes 2621440 | tf_op jit(solution)/shard_map/attend/pallas_call | solution.py:366
  26.2 3.1 %collective-permute-start.8 = (bf16[272,128]{1,0:T(8,128)(2,1)S(1)}, bf16[272,128]{1,0:T(8,128)(2,1)S(1)}, u32[]{:S(2)}, u32[]{:S(2)}) collective-permute-start(bf16[272,128]{1,0:T(8,128)(2,1)S(1)} %attend.7), channel_id=1, source_target_pairs={{0,12},{4,8},{8,4},{12,0},{1,13},{5,9},{9,5},{13,1},{2,14},{6,10},... | collective-permute-start | bytes 208904 | tf_op jit(solution)/shard_map/ppermute | solution.py:292
  29.3 0.7 %attend.4.refs_0_ = bf16[272,128]{1,0:T(8,128)(2,1)S(1)} custom-call(bf16[128,256]{1,0:T(8,128)(2,1)S(1)} %collect.1.queries_ref, bf16[512,256]{1,0:T(8,128)(2,1)S(1)} %get-tuple-element.22.keys_ref, bf16[256,512]{1,0:T(8,128)(2,1)S(1)} %get-tuple-element.23.values_t_ref), custom_call_target="tpu_custom_call" | custom-call | flops 67108864 | bytes 2621440 | tf_op jit(solution)/shard_map/attend/pallas_call | solution.py:366
  30.1 2.4 %collective-permute-done.8.refs_3_ = bf16[272,128]{1,0:T(8,128)(2,1)S(1)} collective-permute-done((bf16[272,128]{1,0:T(8,128)(2,1)S(1)}, bf16[272,128]{1,0:T(8,128)(2,1)S(1)}, u32[]{:S(2)}, u32[]{:S(2)}) %collective-permute-start.8) | collective-permute-done | bytes 69664 | tf_op jit(solution)/shard_map/ppermute | solution.py:292
  32.5 0.1 combine.1.refs_0_
  32.6 3.0 %collective-permute-start.11 = (bf16[128,256]{1,0:T(8,128)(2,1)S(1)}, bf16[128,256]{1,0:T(8,128)(2,1)S(1)}, u32[]{:S(2)}, u32[]{:S(2)}) collective-permute-start(bf16[128,256]{1,0:T(8,128)(2,1)S(1)} %combine.1.refs_0_), channel_id=1, source_target_pairs={{0,12},{4,8},{8,4},{12,0},{1,13},{5,9},{9,5},{13,1},{2,14},{6,10},... | collective-permute-start | bytes 196616 | tf_op jit(solution)/shard_map/ppermute | solution.py:292
  35.6 1.5 %collective-permute-start.9 = (bf16[128,256]{1,0:T(8,128)(2,1)S(1)}, bf16[128,256]{1,0:T(8,128)(2,1)S(1)}, u32[]{:S(2)}, u32[]{:S(2)}) collective-permute-start(bf16[128,256]{1,0:T(8,128)(2,1)S(1)} %combine.1.refs_0_), channel_id=1, source_target_pairs={{0,4},{4,0},{8,12},{12,8},{1,5},{5,1},{9,13},{13,9},{2,6},{6,2},{1... | collective-permute-start | bytes 196616 | tf_op jit(solution)/shard_map/ppermute | solution.py:292
  37.1 1.7 %collective-permute-done.11.refs_3_ = bf16[128,256]{1,0:T(8,128)(2,1)S(1)} collective-permute-done((bf16[128,256]{1,0:T(8,128)(2,1)S(1)}, bf16[128,256]{1,0:T(8,128)(2,1)S(1)}, u32[]{:S(2)}, u32[]{:S(2)}) %collective-permute-start.11) | collective-permute-done | bytes 65568 | tf_op jit(solution)/shard_map/ppermute | solution.py:292
  38.8 2.0 %collective-permute-done.10.refs_2_ = bf16[128,256]{1,0:T(8,128)(2,1)S(1)} collective-permute-done((bf16[128,256]{1,0:T(8,128)(2,1)S(1)}, bf16[128,256]{1,0:T(8,128)(2,1)S(1)}, u32[]{:S(2)}, u32[]{:S(2)}) %collective-permute-start.10) | collective-permute-done | bytes 65568 | tf_op jit(solution)/shard_map/ppermute | solution.py:292
  40.8 0.2 select.1
  41.0 0.1 collective-permute-start.17
  41.1 0.5 %collective-permute-start.13 = (bf16[128,256]{1,0:T(8,128)(2,1)S(1)}, bf16[128,256]{1,0:T(8,128)(2,1)S(1)}, u32[]{:S(2)}, u32[]{:S(2)}) collective-permute-start(bf16[128,256]{1,0:T(8,128)(2,1)S(1)} %get-tuple-element.25), channel_id=1, source_target_pairs={{0,1},{1,0},{2,3},{3,2},{4,5},{5,4},{6,7},{7,6},{8,9},{9,8},{10,11... | collective-permute-start | bytes 196616 | tf_op jit(solution)/shard_map/ppermute | solution.py:306
  41.6 0.4 collective-permute-start.14
  41.9 1.1 %collective-permute-start.15 = (bf16[128,256]{1,0:T(8,128)(2,1)S(1)}, bf16[128,256]{1,0:T(8,128)(2,1)S(1)}, u32[]{:S(2)}, u32[]{:S(2)}) collective-permute-start(bf16[128,256]{1,0:T(8,128)(2,1)S(1)} %get-tuple-element.27), channel_id=1, source_target_pairs={{0,3},{1,2},{2,1},{3,0},{4,7},{5,6},{6,5},{7,4},{8,11},{9,10},{10,... | collective-permute-start | bytes 196616 | tf_op jit(solution)/shard_map/ppermute | solution.py:306
  43.0 0.4 collective-permute-done.13.refs_1_
  43.4 2.9 %collective-permute-done.14.refs_2_ = bf16[128,256]{1,0:T(8,128)(2,1)S(1)} collective-permute-done((bf16[128,256]{1,0:T(8,128)(2,1)S(1)}, bf16[128,256]{1,0:T(8,128)(2,1)S(1)}, u32[]{:S(2)}, u32[]{:S(2)}) %collective-permute-start.14) | collective-permute-done | bytes 65568 | tf_op jit(solution)/shard_map/ppermute | solution.py:306
  46.4 1.5 %project.1 = f32[128,1536]{1,0:T(8,128)} custom-call(f32[3,1536]{1,0:T(4,128)S(1)} %copy-done.2, bf16[128,256]{1,0:T(8,128)(2,1)S(1)} %get-tuple-element.24.refs_0_, bf16[128,256]{1,0:T(8,128)(2,1)S(1)} %collective-permute-done.13.refs_1_, bf16[128,256]{1,0:T(8,128)(2,1)S(1)} %collective-permute-done.14.refs_2_, ...), custom_call_target="tpu_custom_call" | custom-call | flops 402653184 | bytes 3145728 | tf_op jit(solution)/shard_map/project/pallas_call | solution.py:412
  (24 shorter events, 0.1 us)
Async XLA Ops:
  0.0 11.9 %copy-start.2 = (f32[3,1536]{1,0:T(4,128)S(1)}, f32[3,1536]{1,0:T(4,128)}, u32[]{:S(2)}) copy-start(f32[3,1536]{1,0:T(4,128)} %modulation_ref.1) | copy-start | bytes 55300
  0.0 11.9 %copy-start.4 = (s32[4]{0:T(128)S(1)}, s32[4]{0:T(128)}, u32[]{:S(2)}) copy-start(s32[4]{0:T(128)} %worker_in.3) | copy-start | bytes 52
  0.0 11.9 %copy-start.1 = (bf16[512,256]{1,0:T(8,128)(2,1)S(1)}, bf16[512,256]{1,0:T(8,128)(2,1)}, u32[]{:S(2)}) copy-start(bf16[512,256]{1,0:T(8,128)(2,1)} %key_cache_in.1) | copy-start | bytes 786436
  0.0 40.8 %collective-permute-start.12 = (bf16[256,1536]{1,0:T(8,128)(2,1)}, bf16[256,1536]{1,0:T(8,128)(2,1)S(1)}, u32[]{:S(2)}, u32[]{:S(2)}) collective-permute-start(bf16[256,1536]{1,0:T(8,128)(2,1)} %refs_4_.1), channel_id=1, source_target_pairs={{0,2},{2,0},{1,3},{3,1},{4,6},{6,4},{5,7},{7,5},{8,10},{10,8},{9,1... | collective-permute-start | bytes 2359304 | tf_op jit(solution)/shard_map/ppermute | solution.py:295
  7.4 10.0 %collective-permute-start = (bf16[128,256]{1,0:T(8,128)(2,1)}, bf16[128,256]{1,0:T(8,128)(2,1)S(1)}, u32[]{:S(2)}, u32[]{:S(2)}) collective-permute-start(bf16[128,256]{1,0:T(8,128)(2,1)} %get-tuple-element.18), channel_id=1, source_target_pairs={{0,4},{4,0},{8,12},{12,8},{1,5},{5,1},{9,13},{13,9},{2,6},{6,2},{1... | collective-permute-start | bytes 196616 | tf_op jit(solution)/shard_map/ppermute | solution.py:292
  7.7 9.7 %collective-permute-start.1 = (bf16[128,256]{1,0:T(8,128)(2,1)}, bf16[128,256]{1,0:T(8,128)(2,1)S(1)}, u32[]{:S(2)}, u32[]{:S(2)}) collective-permute-start(bf16[128,256]{1,0:T(8,128)(2,1)} %get-tuple-element.19), channel_id=1, source_target_pairs={{0,8},{4,12},{8,0},{12,4},{1,9},{5,13},{9,1},{13,5},{2,10},{6,14},... | collective-permute-start | bytes 196616 | tf_op jit(solution)/shard_map/ppermute | solution.py:292
  10.3 7.2 %copy-start.3 = (bf16[128,256]{1,0:T(8,128)(2,1)S(1)}, bf16[128,256]{1,0:T(8,128)(2,1)}, u32[]{:S(2)}) copy-start(bf16[128,256]{1,0:T(8,128)(2,1)} %get-tuple-element.17.refs_0_) | copy-start | bytes 196612
  10.3 7.2 %collective-permute-start.2 = (bf16[128,256]{1,0:T(8,128)(2,1)}, bf16[128,256]{1,0:T(8,128)(2,1)S(1)}, u32[]{:S(2)}, u32[]{:S(2)}) collective-permute-start(bf16[128,256]{1,0:T(8,128)(2,1)} %get-tuple-element.20), channel_id=1, source_target_pairs={{0,12},{4,8},{8,4},{12,0},{1,13},{5,9},{9,5},{13,1},{2,14},{6,10},... | collective-permute-start | bytes 196616 | tf_op jit(solution)/shard_map/ppermute | solution.py:292
  17.5 19.6 %copy-start = (bf16[256,1536]{1,0:T(8,128)(2,1)S(1)}, bf16[256,1536]{1,0:T(8,128)(2,1)}, u32[]{:S(2)}) copy-start(bf16[256,1536]{1,0:T(8,128)(2,1)} %refs_4_.1) | copy-start | bytes 2359300
  17.5 4.5 %collective-permute-start.3 = (bf16[128,256]{1,0:T(8,128)(2,1)S(1)}, bf16[128,256]{1,0:T(8,128)(2,1)S(1)}, u32[]{:S(2)}, u32[]{:S(2)}) collective-permute-start(bf16[128,256]{1,0:T(8,128)(2,1)S(1)} %collect.1.queries_ref), channel_id=1, source_target_pairs={{0,4},{4,0},{8,12},{12,8},{1,5},{5,1},{9,13},{13,9},{2,6},{6,2},{1... | collective-permute-start | bytes 196616 | tf_op jit(solution)/shard_map/ppermute | solution.py:292
  17.6 6.1 %collective-permute-start.5 = (bf16[128,256]{1,0:T(8,128)(2,1)S(1)}, bf16[128,256]{1,0:T(8,128)(2,1)S(1)}, u32[]{:S(2)}, u32[]{:S(2)}) collective-permute-start(bf16[128,256]{1,0:T(8,128)(2,1)S(1)} %collect.1.queries_ref), channel_id=1, source_target_pairs={{0,8},{4,12},{8,0},{12,4},{1,9},{5,13},{9,1},{13,5},{2,10},{6,14},... | collective-permute-start | bytes 196616 | tf_op jit(solution)/shard_map/ppermute | solution.py:292
  18.9 6.5 %collective-permute-start.7 = (bf16[128,256]{1,0:T(8,128)(2,1)S(1)}, bf16[128,256]{1,0:T(8,128)(2,1)S(1)}, u32[]{:S(2)}, u32[]{:S(2)}) collective-permute-start(bf16[128,256]{1,0:T(8,128)(2,1)S(1)} %collect.1.queries_ref), channel_id=1, source_target_pairs={{0,12},{4,8},{8,4},{12,0},{1,13},{5,9},{9,5},{13,1},{2,14},{6,10},... | collective-permute-start | bytes 196616 | tf_op jit(solution)/shard_map/ppermute | solution.py:292
  22.7 7.3 %collective-permute-start.4 = (bf16[272,128]{1,0:T(8,128)(2,1)S(1)}, bf16[272,128]{1,0:T(8,128)(2,1)S(1)}, u32[]{:S(2)}, u32[]{:S(2)}) collective-permute-start(bf16[272,128]{1,0:T(8,128)(2,1)S(1)} %attend.5), channel_id=1, source_target_pairs={{0,4},{4,0},{8,12},{12,8},{1,5},{5,1},{9,13},{13,9},{2,6},{6,2},{1... | collective-permute-start | bytes 208904 | tf_op jit(solution)/shard_map/ppermute | solution.py:292
  24.5 5.6 %collective-permute-start.6 = (bf16[272,128]{1,0:T(8,128)(2,1)S(1)}, bf16[272,128]{1,0:T(8,128)(2,1)S(1)}, u32[]{:S(2)}, u32[]{:S(2)}) collective-permute-start(bf16[272,128]{1,0:T(8,128)(2,1)S(1)} %attend.6), channel_id=1, source_target_pairs={{0,8},{4,12},{8,0},{12,4},{1,9},{5,13},{9,1},{13,5},{2,10},{6,14},... | collective-permute-start | bytes 208904 | tf_op jit(solution)/shard_map/ppermute | solution.py:292
  26.2 6.3 %collective-permute-start.8 = (bf16[272,128]{1,0:T(8,128)(2,1)S(1)}, bf16[272,128]{1,0:T(8,128)(2,1)S(1)}, u32[]{:S(2)}, u32[]{:S(2)}) collective-permute-start(bf16[272,128]{1,0:T(8,128)(2,1)S(1)} %attend.7), channel_id=1, source_target_pairs={{0,12},{4,8},{8,4},{12,0},{1,13},{5,9},{9,5},{13,1},{2,14},{6,10},... | collective-permute-start | bytes 208904 | tf_op jit(solution)/shard_map/ppermute | solution.py:292
  32.6 6.1 %collective-permute-start.11 = (bf16[128,256]{1,0:T(8,128)(2,1)S(1)}, bf16[128,256]{1,0:T(8,128)(2,1)S(1)}, u32[]{:S(2)}, u32[]{:S(2)}) collective-permute-start(bf16[128,256]{1,0:T(8,128)(2,1)S(1)} %combine.1.refs_0_), channel_id=1, source_target_pairs={{0,12},{4,8},{8,4},{12,0},{1,13},{5,9},{9,5},{13,1},{2,14},{6,10},... | collective-permute-start | bytes 196616 | tf_op jit(solution)/shard_map/ppermute | solution.py:292
  35.6 5.2 %collective-permute-start.10 = (bf16[128,256]{1,0:T(8,128)(2,1)S(1)}, bf16[128,256]{1,0:T(8,128)(2,1)S(1)}, u32[]{:S(2)}, u32[]{:S(2)}) collective-permute-start(bf16[128,256]{1,0:T(8,128)(2,1)S(1)} %combine.1.refs_0_), channel_id=1, source_target_pairs={{0,8},{4,12},{8,0},{12,4},{1,9},{5,13},{9,1},{13,5},{2,10},{6,14},... | collective-permute-start | bytes 196616 | tf_op jit(solution)/shard_map/ppermute | solution.py:292
  35.6 5.2 %collective-permute-start.9 = (bf16[128,256]{1,0:T(8,128)(2,1)S(1)}, bf16[128,256]{1,0:T(8,128)(2,1)S(1)}, u32[]{:S(2)}, u32[]{:S(2)}) collective-permute-start(bf16[128,256]{1,0:T(8,128)(2,1)S(1)} %combine.1.refs_0_), channel_id=1, source_target_pairs={{0,4},{4,0},{8,12},{12,8},{1,5},{5,1},{9,13},{13,9},{2,6},{6,2},{1... | collective-permute-start | bytes 196616 | tf_op jit(solution)/shard_map/ppermute | solution.py:292
  37.1 5.9 %collective-permute-start.16 = (bf16[256,1536]{1,0:T(8,128)(2,1)S(1)}, bf16[256,1536]{1,0:T(8,128)(2,1)S(1)}, u32[]{:S(2)}, u32[]{:S(2)}) collective-permute-start(bf16[256,1536]{1,0:T(8,128)(2,1)S(1)} %copy-done), channel_id=1, source_target_pairs={{0,1},{1,0},{2,3},{3,2},{4,5},{5,4},{6,7},{7,6},{8,9},{9,8},{10,11... | collective-permute-start | bytes 2359304 | tf_op jit(solution)/shard_map/ppermute | solution.py:298
  41.0 5.4 %collective-permute-start.17 = (bf16[256,1536]{1,0:T(8,128)(2,1)S(1)}, bf16[256,1536]{1,0:T(8,128)(2,1)S(1)}, u32[]{:S(2)}, u32[]{:S(2)}) collective-permute-start(bf16[256,1536]{1,0:T(8,128)(2,1)S(1)} %get-tuple-element.28.refs_6_), channel_id=1, source_target_pairs={{0,1},{1,0},{2,3},{3,2},{4,5},{5,4},{6,7},{7,6},{8,9},{9,8},{10,11... | collective-permute-start | bytes 2359304 | tf_op jit(solution)/shard_map/ppermute | solution.py:298
  41.1 2.4 %collective-permute-start.13 = (bf16[128,256]{1,0:T(8,128)(2,1)S(1)}, bf16[128,256]{1,0:T(8,128)(2,1)S(1)}, u32[]{:S(2)}, u32[]{:S(2)}) collective-permute-start(bf16[128,256]{1,0:T(8,128)(2,1)S(1)} %get-tuple-element.25), channel_id=1, source_target_pairs={{0,1},{1,0},{2,3},{3,2},{4,5},{5,4},{6,7},{7,6},{8,9},{9,8},{10,11... | collective-permute-start | bytes 196616 | tf_op jit(solution)/shard_map/ppermute | solution.py:306
  41.6 4.8 %collective-permute-start.14 = (bf16[128,256]{1,0:T(8,128)(2,1)S(1)}, bf16[128,256]{1,0:T(8,128)(2,1)S(1)}, u32[]{:S(2)}, u32[]{:S(2)}) collective-permute-start(bf16[128,256]{1,0:T(8,128)(2,1)S(1)} %get-tuple-element.26), channel_id=1, source_target_pairs={{0,2},{1,3},{2,0},{3,1},{4,6},{5,7},{6,4},{7,5},{8,10},{9,11},{10,... | collective-permute-start | bytes 196616 | tf_op jit(solution)/shard_map/ppermute | solution.py:306
  41.9 4.4 %collective-permute-start.15 = (bf16[128,256]{1,0:T(8,128)(2,1)S(1)}, bf16[128,256]{1,0:T(8,128)(2,1)S(1)}, u32[]{:S(2)}, u32[]{:S(2)}) collective-permute-start(bf16[128,256]{1,0:T(8,128)(2,1)S(1)} %get-tuple-element.27), channel_id=1, source_target_pairs={{0,3},{1,2},{2,1},{3,0},{4,7},{5,6},{6,5},{7,4},{8,11},{9,10},{10,... | collective-permute-start | bytes 196616 | tf_op jit(solution)/shard_map/ppermute | solution.py:306

commit v5 on v4

--- a/solution.py
+++ b/solution.py
@@ -35,9 +35,9 @@
 
 
 def query_kernel(n_frame, worker_in, latents_in, modulation_in, weight_in, *rest):
-    outs = rest[:n_frame]
+    outs, normed_out = rest[:n_frame], rest[n_frame]
     worker_ref, latents_ref, modulation_ref, weight_ref, normed_ref, queries_ref, sems = rest[
-        n_frame:
+        n_frame + 1 :
     ]
     n_local = worker_ref.shape[0]
     block_rows = latents_ref.shape[0] // n_local
@@ -49,6 +49,12 @@
     ]
     each = [
         pltpu.make_async_copy(latents_in.at[rows, :], latents_ref.at[rows, :], sems.at[3 + j])
+        for j, rows in enumerate(blocks)
+    ]
+    back = [
+        pltpu.make_async_copy(
+            normed_ref.at[rows, :], normed_out.at[rows, :], sems.at[3 + n_local + j]
+        )
         for j, rows in enumerate(blocks)
     ]
     weight = pltpu.make_async_copy(weight_in, weight_ref, sems.at[2])
@@ -64,6 +70,7 @@
         @pl.when(worker_ref[j] >= 0)
         def _():
             normalize_block(latents_ref, modulation_ref, normed_ref, j * block_rows, block_rows)
+            back[j].start()
 
     weight.wait()
     queries_ref[...] = (
@@ -77,50 +84,76 @@
             def _():
                 outs[s][...] = queries_ref[blocks[j], :]
 
-
-def key_value_kernel(
+        @pl.when(worker >= 0)
+        def _():
+            back[j].wait()
+
+
+def key_kernel(
+    worker_in, normed_in, weight_in, cache_in, keys_ref, worker_ref, normed_ref, weight_ref, sems
+):
+    n_local = worker_ref.shape[0]
+    block_rows = normed_ref.shape[0] // n_local
+    copies = [
+        pltpu.make_async_copy(source, target, sems.at[i])
+        for i, (source, target) in enumerate(
+            [
+                (worker_in, worker_ref),
+                (normed_in, normed_ref),
+                (weight_in, weight_ref),
+                (cache_in, keys_ref),
+            ]
+        )
+    ]
+    for copy in copies:
+        copy.start()
+    for copy in copies:
+        copy.wait()
+    fresh = jnp.dot(
+        normed_ref[...], weight_ref[...], preferred_element_type=jnp.float32
+    ).astype(jnp.bfloat16)
+    for j in range(n_local):
+        rows = slice(j * block_rows, (j + 1) * block_rows)
+
+        @pl.when(worker_ref[j] >= 0)
+        def _():
+            keys_ref[rows, :] = fresh[rows, :]
+
+
+def value_kernel(
     n_frame,
     n_head,
     n_rep,
     worker_in,
-    latents_in,
-    modulation_in,
-    key_weight_in,
-    value_weight_in,
-    key_cache_in,
-    value_cache_in,
-    keys_ref,
+    normed_in,
+    weight_in,
+    cache_in,
+    _,
     values_t_ref,
     masks_ref,
     worker_ref,
-    latents_ref,
-    modulation_ref,
-    key_weight_ref,
-    value_weight_ref,
-    value_cache_ref,
     normed_ref,
-    fresh_ref,
+    weight_ref,
+    values_ref,
     sems,
 ):
     n_local = worker_ref.shape[0]
-    tokens = latents_ref.shape[0]
+    tokens = normed_ref.shape[0]
     block_rows = tokens // n_local
-    blocks = [slice(j * block_rows, (j + 1) * block_rows) for j in range(n_local)]
-    first = [
-        pltpu.make_async_copy(worker_in, worker_ref, sems.at[0]),
-        pltpu.make_async_copy(modulation_in, modulation_ref, sems.at[1]),
-        pltpu.make_async_copy(latents_in, latents_ref, sems.at[2]),
-    ]
-    second = [
-        pltpu.make_async_copy(key_weight_in, key_weight_ref, sems.at[3]),
-        pltpu.make_async_copy(value_weight_in, value_weight_ref, sems.at[4]),
-        pltpu.make_async_copy(key_cache_in, keys_ref, sems.at[5]),
-        pltpu.make_async_copy(value_cache_in, value_cache_ref, sems.at[6]),
-    ]
-    for copy in first + second:
+    copies = [
+        pltpu.make_async_copy(source, target, sems.at[i])
+        for i, (source, target) in enumerate(
+            [
+                (worker_in, worker_ref),
+                (normed_in, normed_ref),
+                (weight_in, weight_ref),
+                (cache_in, values_ref),
+            ]
+        )
+    ]
+    for copy in copies:
         copy.start()
-    for copy in first:
-        copy.wait()
+    copies[0].wait()
     frame, head, rep = lax.axis_index("frame"), lax.axis_index("head"), lax.axis_index("rep")
     n_place = n_head * n_rep
     for d in range(n_place):
@@ -131,35 +164,21 @@
             masks_ref[d * n_frame + s : d * n_frame + s + 1, :] = jnp.full(
                 (1, masks_ref.shape[1]), jnp.where(held, 1.0, 0.0), jnp.float32
             )
+    for copy in copies[1:]:
+        copy.wait()
+    fresh = jnp.dot(
+        normed_ref[...], weight_ref[...], preferred_element_type=jnp.float32
+    ).astype(jnp.bfloat16)
     for j in range(n_local):
+        rows = slice(j * block_rows, (j + 1) * block_rows)
 
         @pl.when(worker_ref[j] >= 0)
         def _():
-            normalize_block(latents_ref, modulation_ref, normed_ref, j * block_rows, block_rows)
-
-    for copy in second:
-        copy.wait()
-    fresh_ref[...] = jnp.dot(
-        normed_ref[...], key_weight_ref[...], preferred_element_type=jnp.float32
-    ).astype(jnp.bfloat16)
-    for j in range(n_local):
-
-        @pl.when(worker_ref[j] >= 0)
-        def _():
-            keys_ref[blocks[j], :] = fresh_ref[blocks[j], :]
-
-    fresh_ref[...] = jnp.dot(
-        normed_ref[...], value_weight_ref[...], preferred_element_type=jnp.float32
-    ).astype(jnp.bfloat16)
-    for j in range(n_local):
-
-        @pl.when(worker_ref[j] >= 0)
-        def _():
-            value_cache_ref[blocks[j], :] = fresh_ref[blocks[j], :]
-
-    for h in range(keys_ref.shape[1] // HD):
+            values_ref[rows, :] = fresh[rows, :]
+
+    for h in range(values_ref.shape[1] // HD):
         cols = slice(h * HD, (h + 1) * HD)
-        values_t_ref[cols, :] = value_cache_ref[:, cols].T
+        values_t_ref[cols, :] = values_ref[:, cols].T
 
 
 def three_terms(x):
@@ -244,13 +263,23 @@
             outs[d][:, cols] = chosen.astype(jnp.bfloat16)
 
 
-def project_kernel(modulation_ref, *refs):
+def project_near_kernel(*refs):
     refs, out_ref = refs[:-1], refs[-1]
     parts, weights = refs[: len(refs) // 2], refs[len(refs) // 2 :]
-    width = out_ref.shape[1]
-    for start in range(0, width, COLUMNS):
+    for start in range(0, out_ref.shape[1], COLUMNS):
         cols = slice(start, start + COLUMNS)
-        total = sum(
+        out_ref[:, cols] = sum(
+            jnp.dot(part[...], weight[:, cols], preferred_element_type=jnp.float32)
+            for part, weight in zip(parts, weights)
+        )
+
+
+def project_kernel(modulation_ref, near_ref, *refs):
+    refs, out_ref = refs[:-1], refs[-1]
+    parts, weights = refs[: len(refs) // 2], refs[len(refs) // 2 :]
+    for start in range(0, out_ref.shape[1], COLUMNS):
+        cols = slice(start, start + COLUMNS)
+        total = near_ref[:, cols] + sum(
             jnp.dot(part[...], weight[:, cols], preferred_element_type=jnp.float32)
             for part, weight in zip(parts, weights)
         )
@@ -307,11 +336,12 @@
 
     across = [along_head(out_weight, dh) for dh in range(1, n_head)]
 
-    slots = pl.pallas_call(
+    *slots, normed = pl.pallas_call(
         functools.partial(query_kernel, n_frame),
-        out_shape=[jax.ShapeDtypeStruct((block_rows, width), half)] * n_frame,
+        out_shape=[jax.ShapeDtypeStruct((block_rows, width), half)] * n_frame
+        + [jax.ShapeDtypeStruct(latents.shape, half)],
         in_specs=[HBM] * 4,
-        out_specs=[VMEM] * n_frame,
+        out_specs=[VMEM] * n_frame + [HBM],
         scratch_shapes=[
             pltpu.SMEM(block_worker.shape, jnp.int32),
             pltpu.VMEM(latents.shape, half),
@@ -319,38 +349,29 @@
             pltpu.VMEM(query_weight.shape, half),
             pltpu.VMEM(latents.shape, half),
             pltpu.VMEM((tokens, width), half),
-            pltpu.SemaphoreType.DMA((3 + n_local,)),
+            pltpu.SemaphoreType.DMA((3 + 2 * n_local,)),
         ],
         compiler_params=params(60),
         cost_estimate=cost(2 * tokens * model * width, 2 * tokens * model + 2 * model * width),
         name="queries",
     )(block_worker, latents, modulation, query_weight)
-    arrived = [along_frame(slots[s], s) for s in range(1, n_frame)]
-
-    keys, values_t, masks = pl.pallas_call(
-        functools.partial(key_value_kernel, n_frame, n_head, n_rep),
-        out_shape=[
-            jax.ShapeDtypeStruct((tokens, width), half),
-            jax.ShapeDtypeStruct((width, tokens), half),
-            jax.ShapeDtypeStruct((n_place * n_frame, HD), jnp.float32),
-        ],
-        in_specs=[HBM] * 7,
-        out_specs=[VMEM] * 3,
+    arrived = [along_frame(slots[s], s) for s in range(n_frame - 1, 0, -1)]
+
+    keys = pl.pallas_call(
+        key_kernel,
+        out_shape=jax.ShapeDtypeStruct((tokens, width), half),
+        in_specs=[HBM] * 4,
+        out_specs=VMEM,
         scratch_shapes=[
             pltpu.SMEM(block_worker.shape, jnp.int32),
             pltpu.VMEM(latents.shape, half),
-            pltpu.VMEM(modulation.shape, jnp.float32),
             pltpu.VMEM(key_weight.shape, half),
-            pltpu.VMEM(value_weight.shape, half),
-            pltpu.VMEM(value_cache.shape, half),
-            pltpu.VMEM(latents.shape, half),
-            pltpu.VMEM((tokens, width), half),
-            pltpu.SemaphoreType.DMA((7,)),
+            pltpu.SemaphoreType.DMA((4,)),
         ],
         compiler_params=params(53),
-        cost_estimate=cost(4 * tokens * model * width, 2 * tokens * model + 4 * model * width),
-        name="keys_values",
-    )(block_worker, latents, modulation, key_weight, value_weight, key_cache, value_cache)
+        cost_estimate=cost(2 * tokens * model * width, 6 * tokens * model),
+        name="keys",
+    )(block_worker, normed, key_weight, key_cache)
 
     mine = pl.pallas_call(
         collect_kernel,
@@ -360,7 +381,27 @@
         compiler_params=params(16),
         cost_estimate=cost(n_frame * block_rows * width, 2 * n_frame * block_rows * width),
         name="collect",
-    )(slots[0], *arrived, masks)
+    )(slots[0], *arrived, keys)
+
+    values_t, masks = pl.pallas_call(
+        functools.partial(value_kernel, n_frame, n_head, n_rep),
+        out_shape=[
+            jax.ShapeDtypeStruct((width, tokens), half),
+            jax.ShapeDtypeStruct((n_place * n_frame, HD), jnp.float32),
+        ],
+        in_specs=[HBM] * 4 + [ANY],
+        out_specs=[VMEM] * 2,
+        scratch_shapes=[
+            pltpu.SMEM(block_worker.shape, jnp.int32),
+            pltpu.VMEM(latents.shape, half),
+            pltpu.VMEM(value_weight.shape, half),
+            pltpu.VMEM(value_cache.shape, half),
+            pltpu.SemaphoreType.DMA((4,)),
+        ],
+        compiler_params=params(53),
+        cost_estimate=cost(2 * tokens * model * width, 6 * tokens * model),
+        name="values",
+    )(block_worker, normed, value_weight, value_cache, mine)
 
     def attend(queries, through=()):
         return pl.pallas_call(
@@ -379,8 +420,9 @@
             name="attend",
         )(queries, keys, values_t, *through)
 
-    shared = [along_frame(mine, s) for s in range(1, n_frame)]
-    sent = [along_frame(attend(queries)[0], s) for s, queries in enumerate(shared, 1)]
+    far_first = range(n_frame - 1, 0, -1)
+    shared = {s: along_frame(mine, s) for s in far_first}
+    sent = [along_frame(attend(shared[s])[0], s) for s in far_first]
     (own,) = attend(mine)
     attended = pl.pallas_call(
         combine_kernel,
@@ -391,7 +433,8 @@
         cost_estimate=cost(4 * n_frame * block_rows * width, 2 * n_frame * block_rows * width),
         name="combine",
     )(own, *sent)
-    copies = [attended] + [along_frame(attended, s) for s in range(1, n_frame)]
+    copies = {s: along_frame(attended, s) for s in far_first}
+    copies = [attended] + [copies[s] for s in range(1, n_frame)]
     pieces = pl.pallas_call(
         functools.partial(select_kernel, n_frame, n_head, n_rep),
         out_shape=[jax.ShapeDtypeStruct((own_rows, width), half)] * n_place
@@ -409,15 +452,24 @@
     weights = []
     for held in [out_weight] + across:
         weights += [held] + [along_rep(held, dr) for dr in range(1, n_rep)]
+    near = pl.pallas_call(
+        project_near_kernel,
+        out_shape=jax.ShapeDtypeStruct((own_rows, model), jnp.float32),
+        in_specs=[VMEM] * (2 * n_rep),
+        out_specs=VMEM,
+        compiler_params=params(16),
+        cost_estimate=cost(2 * own_rows * model * width * n_rep, 4 * model * width * n_rep),
+        name="project_near",
+    )(*pieces[:n_rep], *weights[:n_rep])
     return pl.pallas_call(
         project_kernel,
         out_shape=jax.ShapeDtypeStruct((own_rows, model), jnp.float32),
-        in_specs=[VMEM] * (1 + 2 * n_place),
+        in_specs=[VMEM] * (2 + 2 * (n_place - n_rep)),
         out_specs=VMEM,
         compiler_params=params(16),
-        cost_estimate=cost(2 * own_rows * model * width * n_place, 2 * model * width * n_place),
+        cost_estimate=cost(2 * own_rows * model * width * n_rep, 2 * model * width * n_place),
         name="project",
-    )(modulation, *pieces, *weights)
+    )(modulation, near, *pieces[n_rep:], *weights[n_rep:])
 
 
 def solution(mesh):

time: 48.6 us -> 48.7 us (level)
  waiting for transfers between devices: 10.4 us -> 13.2 us
  Pallas kernels: 14.7 us -> 12.6 us
  starting transfers between devices: 22.5 us -> 22 us
    ppermute x12, waiting for transfers between devices: 7.06 us -> 10.1 us  [along_frame(): return lax.ppermute(x, 'frame', [(i, i ^ s) for i in range(n_frame)])]
    pallas_call x1, Pallas kernels: 4.38 us -> 3.08 us  [per_device(): pl.pallas_call(functools.partial(query_kernel, n_frame), out_shape=[jax.S...]
    pallas_call x1 -> x3, Pallas kernels: 5.55 us -> 5 us  [the longest x1 2.36 us: per_device(): pl.pallas_call(functools.partial(value_kernel, n_frame, n_head, n_rep), o...]
  transfers between devices with their start and end apart: 18 -> 18, of which waited for: 6 -> 9; matrix products, arithmetic and copies ran while one was open for 0% -> 0% of each run, Pallas kernels for 28% -> 24%
where the time goes in v5:
time: 48.7 us; the launch traced here: 48.1 us
  starting transfers between devices  22 us (45%)
  waiting for transfers between devices  13.2 us (27%)
  Pallas kernels  12.6 us (26%)
    ppermute x12, starting transfers between devices, along_frame(): return lax.ppermute(x, 'frame', [(i, i ^ s) for i in range(n_frame)])  17.1 us
    ppermute x12, waiting for transfers between devices, along_frame(): return lax.ppermute(x, 'frame', [(i, i ^ s) for i in range(n_frame)])  10.1 us
    ppermute x3, waiting for transfers between devices, in_frame(): return lax.ppermute(x, ('head', 'rep'), pairs)  3.12 us
    pallas_call x1, Pallas kernels, per_device(): pl.pallas_call(functools.partial(query_kernel, n_frame), out_shape=[jax.S...  3.08 us
    ppermute x1, starting transfers between devices, along_head(): lax.ppermute(x, 'head', [(i, (i + shift) % n_head) for i in range(n_head)])  2.94 us
    pallas_call x4, Pallas kernels, attend(): pl.pallas_call(attend_kernel, out_shape=[jax.ShapeDtypeStruct((width + ta...  2.93 us
    pallas_call x1, Pallas kernels, per_device(): pl.pallas_call(functools.partial(value_kernel, n_frame, n_head, n_rep), o...  2.36 us
    pallas_call x1, Pallas kernels, per_device(): pl.pallas_call(key_kernel, out_shape=jax.ShapeDtypeStruct((tokens, width)...  2.28 us
  transfers between devices with their start and end apart: 18, of which 9 were waited for; matrix products, arithmetic and copies ran while one was open for 0% of the time, Pallas kernels for 24%

profile of v5, /device:TPU:0, one launch (start us, length us, event | category | flops | bytes accessed | tf_op | source)
XLA Modules:
  0.0 48.1 jit_solution(3794847741317925887)
XLA Ops:
  0.0 2.9 %collective-permute-start.12 = (bf16[256,1536]{1,0:T(8,128)(2,1)}, bf16[256,1536]{1,0:T(8,128)(2,1)S(1)}, u32[]{:S(2)}, u32[]{:S(2)}) collective-permute-start(bf16[256,1536]{1,0:T(8,128)(2,1)} %refs_2_.1), channel_id=1, source_target_pairs={{0,2},{2,0},{1,3},{3,1},{4,6},{6,4},{5,7},{7,5},{8,10},{10,8},{9,1... | collective-permute-start | bytes 2359304 | tf_op jit(solution)/shard_map/ppermute | solution.py:324
  2.9 3.1 %queries.1 = (bf16[128,256]{1,0:T(8,128)(2,1)}, bf16[128,256]{1,0:T(8,128)(2,1)}, bf16[128,256]{1,0:T(8,128)(2,1)}, bf16[128,256]{1,0:T(8,128)(2,1)}, bf16[512,1536]{1,0:T(8,128)(2,1)}) custom-call(s32[4]{0:T(128)} %worker_in.5, bf16[512,1536]{1,0:T(8,128)(2,1)} %latents_in.1, f32[3,1536]{1,0:T(4,128)} %modulation_ref.1, bf16[1536,256]{1,0:T(8,128)(2,1)} %weight_in.3), custom_call_target="tpu_custom_call" | custom-call | flops 402653184 | bytes 2359296 | tf_op jit(solution)/shard_map/queries/pallas_call | solution.py:339
  6.0 3.7 %collective-permute-start = (bf16[128,256]{1,0:T(8,128)(2,1)}, bf16[128,256]{1,0:T(8,128)(2,1)S(1)}, u32[]{:S(2)}, u32[]{:S(2)}) collective-permute-start(bf16[128,256]{1,0:T(8,128)(2,1)} %get-tuple-element.18), channel_id=1, source_target_pairs={{0,12},{4,8},{8,4},{12,0},{1,13},{5,9},{9,5},{13,1},{2,14},{6,10},... | collective-permute-start | bytes 196616 | tf_op jit(solution)/shard_map/ppermute | solution.py:321
  9.7 0.9 %collective-permute-start.1 = (bf16[128,256]{1,0:T(8,128)(2,1)}, bf16[128,256]{1,0:T(8,128)(2,1)S(1)}, u32[]{:S(2)}, u32[]{:S(2)}) collective-permute-start(bf16[128,256]{1,0:T(8,128)(2,1)} %get-tuple-element.19), channel_id=1, source_target_pairs={{0,8},{4,12},{8,0},{12,4},{1,9},{5,13},{9,1},{13,5},{2,10},{6,14},... | collective-permute-start | bytes 196616 | tf_op jit(solution)/shard_map/ppermute | solution.py:321
  10.6 2.3 %keys.1.refs_4_.keys_ref = bf16[512,256]{1,0:T(8,128)(2,1)S(1)} custom-call(s32[4]{0:T(128)S(1)} %copy-done.5, bf16[512,1536]{1,0:T(8,128)(2,1)} %get-tuple-element.21.normed_in, bf16[1536,256]{1,0:T(8,128)(2,1)} %weight_in.4, bf16[512,256]{1,0:T(8,128)(2,1)S(1)} %copy-done.1), custom_call_target="tpu_custom_call" | custom-call | flops 402653184 | bytes 4718592 | tf_op jit(solution)/shard_map/keys/pallas_call | solution.py:360
  13.0 3.1 %collective-permute-done.1.refs_2_ = bf16[128,256]{1,0:T(8,128)(2,1)S(1)} collective-permute-done((bf16[128,256]{1,0:T(8,128)(2,1)}, bf16[128,256]{1,0:T(8,128)(2,1)S(1)}, u32[]{:S(2)}, u32[]{:S(2)}) %collective-permute-start.1) | collective-permute-done | bytes 65568 | tf_op jit(solution)/shard_map/ppermute | solution.py:321
  16.1 0.2 collective-permute-done.2.refs_3_
  16.3 0.2 collective-permute-start.7
  16.4 2.2 %collective-permute-start.5 = (bf16[128,256]{1,0:T(8,128)(2,1)S(1)}, bf16[128,256]{1,0:T(8,128)(2,1)S(1)}, u32[]{:S(2)}, u32[]{:S(2)}) collective-permute-start(bf16[128,256]{1,0:T(8,128)(2,1)S(1)} %collect.1._.queries_ref), channel_id=1, source_target_pairs={{0,8},{4,12},{8,0},{12,4},{1,9},{5,13},{9,1},{13,5},{2,10},{6,14},... | collective-permute-start | bytes 196616 | tf_op jit(solution)/shard_map/ppermute | solution.py:321
  18.6 2.1 %collective-permute-start.3 = (bf16[128,256]{1,0:T(8,128)(2,1)S(1)}, bf16[128,256]{1,0:T(8,128)(2,1)S(1)}, u32[]{:S(2)}, u32[]{:S(2)}) collective-permute-start(bf16[128,256]{1,0:T(8,128)(2,1)S(1)} %collect.1._.queries_ref), channel_id=1, source_target_pairs={{0,12},{4,8},{8,4},{12,0},{1,13},{5,9},{9,5},{13,1},{2,14},{6,10},... | collective-permute-start | bytes 196616 | tf_op jit(solution)/shard_map/ppermute | solution.py:321
  20.7 2.4 %values.1 = (bf16[256,512]{1,0:T(8,128)(2,1)S(1)}, f32[16,128]{1,0:T(8,128)S(1)}) custom-call(s32[4]{0:T(128)S(1)} %copy-done.5, bf16[512,1536]{1,0:T(8,128)(2,1)} %get-tuple-element.21.normed_in, bf16[1536,256]{1,0:T(8,128)(2,1)} %weight_in.5, bf16[512,256]{1,0:T(8,128)(2,1)S(1)} %copy-done.2, bf16[128,256]{1,0:T(8,128)(2,1)S(1)} %collect.1._.queries_ref), custom_call_target="tpu_custom_call" | custom-call | flops 402653184 | bytes 4718592 | tf_op jit(solution)/shard_map/values/pallas_call | solution.py:386
  23.1 0.7 %attend.7 = bf16[272,128]{1,0:T(8,128)(2,1)S(1)} custom-call(bf16[128,256]{1,0:T(8,128)(2,1)S(1)} %collective-permute-done.7.queries_ref, bf16[512,256]{1,0:T(8,128)(2,1)S(1)} %keys.1.refs_4_.keys_ref, bf16[256,512]{1,0:T(8,128)(2,1)S(1)} %get-tuple-element.22.values_t_ref), custom_call_target="tpu_custom_call" | custom-call | flops 67108864 | bytes 2621440 | tf_op jit(solution)/shard_map/attend/pallas_call | solution.py:407
  23.9 0.7 %attend.6 = bf16[272,128]{1,0:T(8,128)(2,1)S(1)} custom-call(bf16[128,256]{1,0:T(8,128)(2,1)S(1)} %collective-permute-done.5.queries_ref, bf16[512,256]{1,0:T(8,128)(2,1)S(1)} %keys.1.refs_4_.keys_ref, bf16[256,512]{1,0:T(8,128)(2,1)S(1)} %get-tuple-element.22.values_t_ref), custom_call_target="tpu_custom_call" | custom-call | flops 67108864 | bytes 2621440 | tf_op jit(solution)/shard_map/attend/pallas_call | solution.py:407
  24.7 2.4 %collective-permute-start.6 = (bf16[272,128]{1,0:T(8,128)(2,1)S(1)}, bf16[272,128]{1,0:T(8,128)(2,1)S(1)}, u32[]{:S(2)}, u32[]{:S(2)}) collective-permute-start(bf16[272,128]{1,0:T(8,128)(2,1)S(1)} %attend.6), channel_id=1, source_target_pairs={{0,8},{4,12},{8,0},{12,4},{1,9},{5,13},{9,1},{13,5},{2,10},{6,14},... | collective-permute-start | bytes 208904 | tf_op jit(solution)/shard_map/ppermute | solution.py:321
  27.0 0.7 %attend.5 = bf16[272,128]{1,0:T(8,128)(2,1)S(1)} custom-call(bf16[128,256]{1,0:T(8,128)(2,1)S(1)} %collective-permute-done.3.queries_ref, bf16[512,256]{1,0:T(8,128)(2,1)S(1)} %keys.1.refs_4_.keys_ref, bf16[256,512]{1,0:T(8,128)(2,1)S(1)} %get-tuple-element.22.values_t_ref), custom_call_target="tpu_custom_call" | custom-call | flops 67108864 | bytes 2621440 | tf_op jit(solution)/shard_map/attend/pallas_call | solution.py:407
  27.8 2.1 %collective-permute-start.4 = (bf16[272,128]{1,0:T(8,128)(2,1)S(1)}, bf16[272,128]{1,0:T(8,128)(2,1)S(1)}, u32[]{:S(2)}, u32[]{:S(2)}) collective-permute-start(bf16[272,128]{1,0:T(8,128)(2,1)S(1)} %attend.5), channel_id=1, source_target_pairs={{0,12},{4,8},{8,4},{12,0},{1,13},{5,9},{9,5},{13,1},{2,14},{6,10},... | collective-permute-start | bytes 208904 | tf_op jit(solution)/shard_map/ppermute | solution.py:321
  29.9 0.7 %attend.4.refs_0_ = bf16[272,128]{1,0:T(8,128)(2,1)S(1)} custom-call(bf16[128,256]{1,0:T(8,128)(2,1)S(1)} %collect.1._.queries_ref, bf16[512,256]{1,0:T(8,128)(2,1)S(1)} %keys.1.refs_4_.keys_ref, bf16[256,512]{1,0:T(8,128)(2,1)S(1)} %get-tuple-element.22.values_t_ref), custom_call_target="tpu_custom_call" | custom-call | flops 67108864 | bytes 2621440 | tf_op jit(solution)/shard_map/attend/pallas_call | solution.py:407
  30.7 3.4 %collective-permute-done.4.refs_1_ = bf16[272,128]{1,0:T(8,128)(2,1)S(1)} collective-permute-done((bf16[272,128]{1,0:T(8,128)(2,1)S(1)}, bf16[272,128]{1,0:T(8,128)(2,1)S(1)}, u32[]{:S(2)}, u32[]{:S(2)}) %collective-permute-start.4) | collective-permute-done | bytes 69664 | tf_op jit(solution)/shard_map/ppermute | solution.py:321
  34.1 0.1 combine.1.refs_0_
  34.3 2.0 %collective-permute-start.11 = (bf16[128,256]{1,0:T(8,128)(2,1)S(1)}, bf16[128,256]{1,0:T(8,128)(2,1)S(1)}, u32[]{:S(2)}, u32[]{:S(2)}) collective-permute-start(bf16[128,256]{1,0:T(8,128)(2,1)S(1)} %combine.1.refs_0_), channel_id=1, source_target_pairs={{0,12},{4,8},{8,4},{12,0},{1,13},{5,9},{9,5},{13,1},{2,14},{6,10},... | collective-permute-start | bytes 196616 | tf_op jit(solution)/shard_map/ppermute | solution.py:321
  36.3 1.4 %collective-permute-start.9 = (bf16[128,256]{1,0:T(8,128)(2,1)S(1)}, bf16[128,256]{1,0:T(8,128)(2,1)S(1)}, u32[]{:S(2)}, u32[]{:S(2)}) collective-permute-start(bf16[128,256]{1,0:T(8,128)(2,1)S(1)} %combine.1.refs_0_), channel_id=1, source_target_pairs={{0,4},{4,0},{8,12},{12,8},{1,5},{5,1},{9,13},{13,9},{2,6},{6,2},{1... | collective-permute-start | bytes 196616 | tf_op jit(solution)/shard_map/ppermute | solution.py:321
  37.8 1.7 %collective-permute-done.10.refs_2_ = bf16[128,256]{1,0:T(8,128)(2,1)S(1)} collective-permute-done((bf16[128,256]{1,0:T(8,128)(2,1)S(1)}, bf16[128,256]{1,0:T(8,128)(2,1)S(1)}, u32[]{:S(2)}, u32[]{:S(2)}) %collective-permute-start.10) | collective-permute-done | bytes 65568 | tf_op jit(solution)/shard_map/ppermute | solution.py:321
  39.4 1.0 %collective-permute-done.11.refs_3_ = bf16[128,256]{1,0:T(8,128)(2,1)S(1)} collective-permute-done((bf16[128,256]{1,0:T(8,128)(2,1)S(1)}, bf16[128,256]{1,0:T(8,128)(2,1)S(1)}, u32[]{:S(2)}, u32[]{:S(2)}) %collective-permute-start.11) | collective-permute-done | bytes 65568 | tf_op jit(solution)/shard_map/ppermute | solution.py:321
  40.5 0.6 %collective-permute-done.9.refs_1_ = bf16[128,256]{1,0:T(8,128)(2,1)S(1)} collective-permute-done((bf16[128,256]{1,0:T(8,128)(2,1)S(1)}, bf16[128,256]{1,0:T(8,128)(2,1)S(1)}, u32[]{:S(2)}, u32[]{:S(2)}) %collective-permute-start.9) | collective-permute-done | bytes 65568 | tf_op jit(solution)/shard_map/ppermute | solution.py:321
  41.1 0.2 select.1
  41.4 0.5 %collective-permute-start.13 = (bf16[128,256]{1,0:T(8,128)(2,1)S(1)}, bf16[128,256]{1,0:T(8,128)(2,1)S(1)}, u32[]{:S(2)}, u32[]{:S(2)}) collective-permute-start(bf16[128,256]{1,0:T(8,128)(2,1)S(1)} %get-tuple-element.25), channel_id=1, source_target_pairs={{0,1},{1,0},{2,3},{3,2},{4,5},{5,4},{6,7},{7,6},{8,9},{9,8},{10,11... | collective-permute-start | bytes 196616 | tf_op jit(solution)/shard_map/ppermute | solution.py:335
  41.9 0.5 %collective-permute-start.15 = (bf16[128,256]{1,0:T(8,128)(2,1)S(1)}, bf16[128,256]{1,0:T(8,128)(2,1)S(1)}, u32[]{:S(2)}, u32[]{:S(2)}) collective-permute-start(bf16[128,256]{1,0:T(8,128)(2,1)S(1)} %get-tuple-element.26), channel_id=1, source_target_pairs={{0,2},{1,3},{2,0},{3,1},{4,6},{5,7},{6,4},{7,5},{8,10},{9,11},{10,... | collective-permute-start | bytes 196616 | tf_op jit(solution)/shard_map/ppermute | solution.py:335
  42.4 0.9 %collective-permute-start.16 = (bf16[128,256]{1,0:T(8,128)(2,1)S(1)}, bf16[128,256]{1,0:T(8,128)(2,1)S(1)}, u32[]{:S(2)}, u32[]{:S(2)}) collective-permute-start(bf16[128,256]{1,0:T(8,128)(2,1)S(1)} %get-tuple-element.27), channel_id=1, source_target_pairs={{0,3},{1,2},{2,1},{3,0},{4,7},{5,6},{6,5},{7,4},{8,11},{9,10},{10,... | collective-permute-start | bytes 196616 | tf_op jit(solution)/shard_map/ppermute | solution.py:335
  43.3 0.4 collective-permute-done.13.refs_1_
  43.8 0.4 project_near.1.near_ref
  44.1 2.7 %collective-permute-done.15.refs_0_ = bf16[128,256]{1,0:T(8,128)(2,1)S(1)} collective-permute-done((bf16[128,256]{1,0:T(8,128)(2,1)S(1)}, bf16[128,256]{1,0:T(8,128)(2,1)S(1)}, u32[]{:S(2)}, u32[]{:S(2)}) %collective-permute-start.15) | collective-permute-done | bytes 65568 | tf_op jit(solution)/shard_map/ppermute | solution.py:335
  46.8 1.3 %project.1 = f32[128,1536]{1,0:T(8,128)} custom-call(f32[3,1536]{1,0:T(4,128)S(1)} %copy-done.3, f32[128,1536]{1,0:T(8,128)S(1)} %project_near.1.near_ref, bf16[128,256]{1,0:T(8,128)(2,1)S(1)} %collective-permute-done.15.refs_0_, bf16[128,256]{1,0:T(8,128)(2,1)S(1)} %collective-permute-done.16.refs_1_, bf16[256,1536]{1,0:T(8,128)(2,1)S(1)} %get-tuple-element.28.refs_2_, ...), custom_call_target="tpu_custom_call" | custom-call | flops 201326592 | bytes 3145728 | tf_op jit(solution)/shard_map/project/pallas_call | solution.py:464
  (28 shorter events, 0.4 us)
Async XLA Ops:
  0.0 10.6 %copy-start.5 = (s32[4]{0:T(128)S(1)}, s32[4]{0:T(128)}, u32[]{:S(2)}) copy-start(s32[4]{0:T(128)} %worker_in.5) | copy-start | bytes 52
  0.0 10.6 %copy-start.1 = (bf16[512,256]{1,0:T(8,128)(2,1)S(1)}, bf16[512,256]{1,0:T(8,128)(2,1)}, u32[]{:S(2)}) copy-start(bf16[512,256]{1,0:T(8,128)(2,1)} %cache_in.2) | copy-start | bytes 786436
  0.0 41.1 %collective-permute-start.12 = (bf16[256,1536]{1,0:T(8,128)(2,1)}, bf16[256,1536]{1,0:T(8,128)(2,1)S(1)}, u32[]{:S(2)}, u32[]{:S(2)}) collective-permute-start(bf16[256,1536]{1,0:T(8,128)(2,1)} %refs_2_.1), channel_id=1, source_target_pairs={{0,2},{2,0},{1,3},{3,1},{4,6},{6,4},{5,7},{7,5},{8,10},{10,8},{9,1... | collective-permute-start | bytes 2359304 | tf_op jit(solution)/shard_map/ppermute | solution.py:324
  6.0 10.2 %copy-start.4 = (bf16[128,256]{1,0:T(8,128)(2,1)S(1)}, bf16[128,256]{1,0:T(8,128)(2,1)}, u32[]{:S(2)}) copy-start(bf16[128,256]{1,0:T(8,128)(2,1)} %get-tuple-element.17.refs_0_) | copy-start | bytes 196612
  6.0 6.9 %collective-permute-start = (bf16[128,256]{1,0:T(8,128)(2,1)}, bf16[128,256]{1,0:T(8,128)(2,1)S(1)}, u32[]{:S(2)}, u32[]{:S(2)}) collective-permute-start(bf16[128,256]{1,0:T(8,128)(2,1)} %get-tuple-element.18), channel_id=1, source_target_pairs={{0,12},{4,8},{8,4},{12,0},{1,13},{5,9},{9,5},{13,1},{2,14},{6,10},... | collective-permute-start | bytes 196616 | tf_op jit(solution)/shard_map/ppermute | solution.py:321
  9.7 6.3 %collective-permute-start.1 = (bf16[128,256]{1,0:T(8,128)(2,1)}, bf16[128,256]{1,0:T(8,128)(2,1)S(1)}, u32[]{:S(2)}, u32[]{:S(2)}) collective-permute-start(bf16[128,256]{1,0:T(8,128)(2,1)} %get-tuple-element.19), channel_id=1, source_target_pairs={{0,8},{4,12},{8,0},{12,4},{1,9},{5,13},{9,1},{13,5},{2,10},{6,14},... | collective-permute-start | bytes 196616 | tf_op jit(solution)/shard_map/ppermute | solution.py:321
  10.6 5.6 %collective-permute-start.2 = (bf16[128,256]{1,0:T(8,128)(2,1)}, bf16[128,256]{1,0:T(8,128)(2,1)S(1)}, u32[]{:S(2)}, u32[]{:S(2)}) collective-permute-start(bf16[128,256]{1,0:T(8,128)(2,1)} %get-tuple-element.20), channel_id=1, source_target_pairs={{0,4},{4,0},{8,12},{12,8},{1,5},{5,1},{9,13},{13,9},{2,6},{6,2},{1... | collective-permute-start | bytes 196616 | tf_op jit(solution)/shard_map/ppermute | solution.py:321
  10.6 10.1 %copy-start.2 = (bf16[512,256]{1,0:T(8,128)(2,1)S(1)}, bf16[512,256]{1,0:T(8,128)(2,1)}, u32[]{:S(2)}) copy-start(bf16[512,256]{1,0:T(8,128)(2,1)} %cache_in.3) | copy-start | bytes 786436
  16.3 6.8 %collective-permute-start.7 = (bf16[128,256]{1,0:T(8,128)(2,1)S(1)}, bf16[128,256]{1,0:T(8,128)(2,1)S(1)}, u32[]{:S(2)}, u32[]{:S(2)}) collective-permute-start(bf16[128,256]{1,0:T(8,128)(2,1)S(1)} %collect.1._.queries_ref), channel_id=1, source_target_pairs={{0,4},{4,0},{8,12},{12,8},{1,5},{5,1},{9,13},{13,9},{2,6},{6,2},{1... | collective-permute-start | bytes 196616 | tf_op jit(solution)/shard_map/ppermute | solution.py:321
  16.4 7.5 %collective-permute-start.5 = (bf16[128,256]{1,0:T(8,128)(2,1)S(1)}, bf16[128,256]{1,0:T(8,128)(2,1)S(1)}, u32[]{:S(2)}, u32[]{:S(2)}) collective-permute-start(bf16[128,256]{1,0:T(8,128)(2,1)S(1)} %collect.1._.queries_ref), channel_id=1, source_target_pairs={{0,8},{4,12},{8,0},{12,4},{1,9},{5,13},{9,1},{13,5},{2,10},{6,14},... | collective-permute-start | bytes 196616 | tf_op jit(solution)/shard_map/ppermute | solution.py:321
  18.6 8.4 %collective-permute-start.3 = (bf16[128,256]{1,0:T(8,128)(2,1)S(1)}, bf16[128,256]{1,0:T(8,128)(2,1)S(1)}, u32[]{:S(2)}, u32[]{:S(2)}) collective-permute-start(bf16[128,256]{1,0:T(8,128)(2,1)S(1)} %collect.1._.queries_ref), channel_id=1, source_target_pairs={{0,12},{4,8},{8,4},{12,0},{1,13},{5,9},{9,5},{13,1},{2,14},{6,10},... | collective-permute-start | bytes 196616 | tf_op jit(solution)/shard_map/ppermute | solution.py:321
  23.1 14.7 %copy-start = (bf16[256,1536]{1,0:T(8,128)(2,1)S(1)}, bf16[256,1536]{1,0:T(8,128)(2,1)}, u32[]{:S(2)}) copy-start(bf16[256,1536]{1,0:T(8,128)(2,1)} %refs_2_.1) | copy-start | bytes 2359300
  23.9 6.8 %collective-permute-start.8 = (bf16[272,128]{1,0:T(8,128)(2,1)S(1)}, bf16[272,128]{1,0:T(8,128)(2,1)S(1)}, u32[]{:S(2)}, u32[]{:S(2)}) collective-permute-start(bf16[272,128]{1,0:T(8,128)(2,1)S(1)} %attend.7), channel_id=1, source_target_pairs={{0,4},{4,0},{8,12},{12,8},{1,5},{5,1},{9,13},{13,9},{2,6},{6,2},{1... | collective-permute-start | bytes 208904 | tf_op jit(solution)/shard_map/ppermute | solution.py:321
  24.7 6.0 %collective-permute-start.6 = (bf16[272,128]{1,0:T(8,128)(2,1)S(1)}, bf16[272,128]{1,0:T(8,128)(2,1)S(1)}, u32[]{:S(2)}, u32[]{:S(2)}) collective-permute-start(bf16[272,128]{1,0:T(8,128)(2,1)S(1)} %attend.6), channel_id=1, source_target_pairs={{0,8},{4,12},{8,0},{12,4},{1,9},{5,13},{9,1},{13,5},{2,10},{6,14},... | collective-permute-start | bytes 208904 | tf_op jit(solution)/shard_map/ppermute | solution.py:321
  27.8 6.3 %collective-permute-start.4 = (bf16[272,128]{1,0:T(8,128)(2,1)S(1)}, bf16[272,128]{1,0:T(8,128)(2,1)S(1)}, u32[]{:S(2)}, u32[]{:S(2)}) collective-permute-start(bf16[272,128]{1,0:T(8,128)(2,1)S(1)} %attend.5), channel_id=1, source_target_pairs={{0,12},{4,8},{8,4},{12,0},{1,13},{5,9},{9,5},{13,1},{2,14},{6,10},... | collective-permute-start | bytes 208904 | tf_op jit(solution)/shard_map/ppermute | solution.py:321
  34.2 5.2 %collective-permute-start.10 = (bf16[128,256]{1,0:T(8,128)(2,1)S(1)}, bf16[128,256]{1,0:T(8,128)(2,1)S(1)}, u32[]{:S(2)}, u32[]{:S(2)}) collective-permute-start(bf16[128,256]{1,0:T(8,128)(2,1)S(1)} %combine.1.refs_0_), channel_id=1, source_target_pairs={{0,8},{4,12},{8,0},{12,4},{1,9},{5,13},{9,1},{13,5},{2,10},{6,14},... | collective-permute-start | bytes 196616 | tf_op jit(solution)/shard_map/ppermute | solution.py:321
  34.3 6.2 %collective-permute-start.11 = (bf16[128,256]{1,0:T(8,128)(2,1)S(1)}, bf16[128,256]{1,0:T(8,128)(2,1)S(1)}, u32[]{:S(2)}, u32[]{:S(2)}) collective-permute-start(bf16[128,256]{1,0:T(8,128)(2,1)S(1)} %combine.1.refs_0_), channel_id=1, source_target_pairs={{0,12},{4,8},{8,4},{12,0},{1,13},{5,9},{9,5},{13,1},{2,14},{6,10},... | collective-permute-start | bytes 196616 | tf_op jit(solution)/shard_map/ppermute | solution.py:321
  36.3 4.8 %collective-permute-start.9 = (bf16[128,256]{1,0:T(8,128)(2,1)S(1)}, bf16[128,256]{1,0:T(8,128)(2,1)S(1)}, u32[]{:S(2)}, u32[]{:S(2)}) collective-permute-start(bf16[128,256]{1,0:T(8,128)(2,1)S(1)} %combine.1.refs_0_), channel_id=1, source_target_pairs={{0,4},{4,0},{8,12},{12,8},{1,5},{5,1},{9,13},{13,9},{2,6},{6,2},{1... | collective-permute-start | bytes 196616 | tf_op jit(solution)/shard_map/ppermute | solution.py:321
  37.8 5.6 %collective-permute-start.14 = (bf16[256,1536]{1,0:T(8,128)(2,1)S(1)}, bf16[256,1536]{1,0:T(8,128)(2,1)S(1)}, u32[]{:S(2)}, u32[]{:S(2)}) collective-permute-start(bf16[256,1536]{1,0:T(8,128)(2,1)S(1)} %copy-done), channel_id=1, source_target_pairs={{0,1},{1,0},{2,3},{3,2},{4,5},{5,4},{6,7},{7,6},{8,9},{9,8},{10,11... | collective-permute-start | bytes 2359304 | tf_op jit(solution)/shard_map/ppermute | solution.py:327
  41.1 5.7 %copy-start.3 = (f32[3,1536]{1,0:T(4,128)S(1)}, f32[3,1536]{1,0:T(4,128)}, u32[]{:S(2)}) copy-start(f32[3,1536]{1,0:T(4,128)} %modulation_ref.1) | copy-start | bytes 55300
  41.3 5.5 %collective-permute-start.17 = (bf16[256,1536]{1,0:T(8,128)(2,1)S(1)}, bf16[256,1536]{1,0:T(8,128)(2,1)S(1)}, u32[]{:S(2)}, u32[]{:S(2)}) collective-permute-start(bf16[256,1536]{1,0:T(8,128)(2,1)S(1)} %get-tuple-element.28.refs_2_), channel_id=1, source_target_pairs={{0,1},{1,0},{2,3},{3,2},{4,5},{5,4},{6,7},{7,6},{8,9},{9,8},{10,11... | collective-permute-start | bytes 2359304 | tf_op jit(solution)/shard_map/ppermute | solution.py:327
  41.4 2.4 %collective-permute-start.13 = (bf16[128,256]{1,0:T(8,128)(2,1)S(1)}, bf16[128,256]{1,0:T(8,128)(2,1)S(1)}, u32[]{:S(2)}, u32[]{:S(2)}) collective-permute-start(bf16[128,256]{1,0:T(8,128)(2,1)S(1)} %get-tuple-element.25), channel_id=1, source_target_pairs={{0,1},{1,0},{2,3},{3,2},{4,5},{5,4},{6,7},{7,6},{8,9},{9,8},{10,11... | collective-permute-start | bytes 196616 | tf_op jit(solution)/shard_map/ppermute | solution.py:335
  41.9 4.9 %collective-permute-start.15 = (bf16[128,256]{1,0:T(8,128)(2,1)S(1)}, bf16[128,256]{1,0:T(8,128)(2,1)S(1)}, u32[]{:S(2)}, u32[]{:S(2)}) collective-permute-start(bf16[128,256]{1,0:T(8,128)(2,1)S(1)} %get-tuple-element.26), channel_id=1, source_target_pairs={{0,2},{1,3},{2,0},{3,1},{4,6},{5,7},{6,4},{7,5},{8,10},{9,11},{10,... | collective-permute-start | bytes 196616 | tf_op jit(solution)/shard_map/ppermute | solution.py:335
  42.4 4.4 %collective-permute-start.16 = (bf16[128,256]{1,0:T(8,128)(2,1)S(1)}, bf16[128,256]{1,0:T(8,128)(2,1)S(1)}, u32[]{:S(2)}, u32[]{:S(2)}) collective-permute-start(bf16[128,256]{1,0:T(8,128)(2,1)S(1)} %get-tuple-element.27), channel_id=1, source_target_pairs={{0,3},{1,2},{2,1},{3,0},{4,7},{5,6},{6,5},{7,4},{8,11},{9,10},{10,... | collective-permute-start | bytes 196616 | tf_op jit(solution)/shard_map/ppermute | solution.py:335

commit v6 on v5

--- a/solution.py
+++ b/solution.py
@@ -11,6 +11,7 @@
 EPS = 1e-06
 CHUNK = 16
 COLUMNS = 512
+SLOTS = 3
 TAIL = 16
 MIB = 1 << 20
 
@@ -193,8 +194,13 @@
     out_ref[...] = sum(part[...].astype(jnp.float32) for part in parts).astype(jnp.bfloat16)
 
 
-def attend_kernel(queries_ref, keys_ref, values_t_ref, *refs):
-    out_ref = refs[len(refs) // 2]
+def attend_kernel(count, *refs):
+    keys_ref, values_t_ref = refs[count : count + 2]
+    for queries_ref, out_ref in zip(refs[:count], refs[-count:]):
+        attend_slot(queries_ref, keys_ref, values_t_ref, out_ref)
+
+
+def attend_slot(queries_ref, keys_ref, values_t_ref, out_ref):
     width = keys_ref.shape[1]
     stats = []
     for h in range(width // HD):
@@ -275,15 +281,20 @@
 
 
 def project_kernel(modulation_ref, near_ref, *refs):
-    refs, out_ref = refs[:-1], refs[-1]
+    refs, (out, total_ref, sems) = refs[:-3], refs[-3:]
     parts, weights = refs[: len(refs) // 2], refs[len(refs) // 2 :]
-    for start in range(0, out_ref.shape[1], COLUMNS):
+    copies = []
+    for i, start in enumerate(range(0, total_ref.shape[1], COLUMNS)):
         cols = slice(start, start + COLUMNS)
         total = near_ref[:, cols] + sum(
             jnp.dot(part[...], weight[:, cols], preferred_element_type=jnp.float32)
             for part, weight in zip(parts, weights)
         )
-        out_ref[:, cols] = total * modulation_ref[2:3, cols]
+        total_ref[:, cols] = total * modulation_ref[2:3, cols]
+        copies.append(pltpu.make_async_copy(total_ref.at[:, cols], out.at[:, cols], sems.at[i]))
+        copies[-1].start()
+    for copy in copies:
+        copy.wait()
 
 
 def params(mib):
@@ -403,27 +414,29 @@
         name="values",
     )(block_worker, normed, value_weight, value_cache, mine)
 
-    def attend(queries, through=()):
+    def attend(queries, after=()):
+        count = len(queries)
         return pl.pallas_call(
-            attend_kernel,
-            out_shape=[jax.ShapeDtypeStruct((width + tail, block_rows), half)]
-            + [jax.ShapeDtypeStruct(w.shape, w.dtype) for w in through],
-            in_specs=[VMEM] * 3 + [ANY] * len(through),
-            out_specs=[VMEM] + [ANY] * len(through),
-            input_output_aliases={3 + i: 1 + i for i in range(len(through))},
+            functools.partial(attend_kernel, count),
+            out_shape=[jax.ShapeDtypeStruct((width + tail, block_rows), half)] * count,
+            in_specs=[VMEM] * (count + 2) + [ANY] * len(after),
+            out_specs=[VMEM] * count,
             compiler_params=params(16),
             cost_estimate=cost(
-                4 * tokens * block_rows * width,
+                4 * tokens * block_rows * width * count,
                 20 * tokens * width,
-                tokens * block_rows * width // HD,
+                tokens * block_rows * width // HD * count,
             ),
             name="attend",
-        )(queries, keys, values_t, *through)
-
-    far_first = range(n_frame - 1, 0, -1)
-    shared = {s: along_frame(mine, s) for s in far_first}
-    sent = [along_frame(attend(shared[s])[0], s) for s in far_first]
-    (own,) = attend(mine)
+        )(*queries, keys, values_t, *after)
+
+    far_first = list(range(n_frame - 1, 0, -1))
+    shared = [along_frame(mine, s) for s in far_first]
+    own = list(attend([mine]))
+    partial = []
+    for start in range(0, n_frame - 1, SLOTS):
+        partial += attend(shared[start : start + SLOTS], own)
+    sent = [along_frame(x, s) for s, x in zip(far_first, partial)]
     attended = pl.pallas_call(
         combine_kernel,
         out_shape=jax.ShapeDtypeStruct((block_rows, width), half),
@@ -432,7 +445,7 @@
         compiler_params=params(16),
         cost_estimate=cost(4 * n_frame * block_rows * width, 2 * n_frame * block_rows * width),
         name="combine",
-    )(own, *sent)
+    )(*own, *sent)
     copies = {s: along_frame(attended, s) for s in far_first}
     copies = [attended] + [copies[s] for s in range(1, n_frame)]
     pieces = pl.pallas_call(
@@ -447,7 +460,8 @@
         name="select",
     )(*copies, masks, *across)
     pieces, across = pieces[:n_place], list(pieces[n_place:])
-    pieces = [pieces[0]] + [in_frame(pieces[d], d) for d in range(1, n_place)]
+    moved = {d: in_frame(pieces[d], d) for d in range(n_place - 1, 0, -1)}
+    pieces = [pieces[0]] + [moved[d] for d in range(1, n_place)]
 
     weights = []
     for held in [out_weight] + across:
@@ -465,7 +479,11 @@
         project_kernel,
         out_shape=jax.ShapeDtypeStruct((own_rows, model), jnp.float32),
         in_specs=[VMEM] * (2 + 2 * (n_place - n_rep)),
-        out_specs=VMEM,
+        out_specs=ANY,
+        scratch_shapes=[
+            pltpu.VMEM((own_rows, model), jnp.float32),
+            pltpu.SemaphoreType.DMA((-(-model // COLUMNS),)),
+        ],
         compiler_params=params(16),
         cost_estimate=cost(2 * own_rows * model * width * n_rep, 2 * model * width * n_place),
         name="project",

time: 48.7 us -> 49.5 us (1.016)
  starting transfers between devices: 22 us -> 23.3 us
  Pallas kernels: 12.6 us -> 11.4 us
  waiting for transfers between devices: 13.2 us -> 13.9 us
    ppermute x12, starting transfers between devices: 17.1 us -> 18.3 us  [along_frame(): return lax.ppermute(x, 'frame', [(i, i ^ s) for i in range(n_frame)])]
    pallas_call x4 -> x2, Pallas kernels: 2.93 us -> 1.81 us  [attend(): pl.pallas_call(functools.partial(attend_kernel, count), out_shape=[jax.Sh...]
    ppermute x12, waiting for transfers between devices: 10.1 us -> 10.8 us  [along_frame(): return lax.ppermute(x, 'frame', [(i, i ^ s) for i in range(n_frame)])]
  transfers between devices with their start and end apart: 18 -> 18, of which waited for: 9 -> 9; matrix products, arithmetic and copies ran while one was open for 0% -> 0% of each run, Pallas kernels for 24% -> 21%
where the time goes in v6:
time: 49.5 us; the launch traced here: 48.8 us
  starting transfers between devices  23.3 us (47%)
  waiting for transfers between devices  13.9 us (28%)
  Pallas kernels  11.4 us (23%)
    ppermute x12, starting transfers between devices, along_frame(): return lax.ppermute(x, 'frame', [(i, i ^ s) for i in range(n_frame)])  18.3 us
    ppermute x12, waiting for transfers between devices, along_frame(): return lax.ppermute(x, 'frame', [(i, i ^ s) for i in range(n_frame)])  10.8 us
    ppermute x3, waiting for transfers between devices, in_frame(): return lax.ppermute(x, ('head', 'rep'), pairs)  3.12 us
    pallas_call x1, Pallas kernels, per_device(): pl.pallas_call(functools.partial(query_kernel, n_frame), out_shape=[jax.S...  3.07 us
    ppermute x1, starting transfers between devices, along_head(): lax.ppermute(x, 'head', [(i, (i + shift) % n_head) for i in range(n_head)])  2.94 us
    pallas_call x1, Pallas kernels, per_device(): pl.pallas_call(functools.partial(value_kernel, n_frame, n_head, n_rep), o...  2.36 us
    pallas_call x1, Pallas kernels, per_device(): pl.pallas_call(key_kernel, out_shape=jax.ShapeDtypeStruct((tokens, width)...  2.28 us
    ppermute x3, starting transfers between devices, in_frame(): return lax.ppermute(x, ('head', 'rep'), pairs)  1.93 us
  transfers between devices with their start and end apart: 18, of which 9 were waited for; matrix products, arithmetic and copies ran while one was open for 0% of the time, Pallas kernels for 21%

profile of v6, /device:TPU:0, one launch (start us, length us, event | category | flops | bytes accessed | tf_op | source)
XLA Modules:
  0.0 48.8 jit_solution(10616262536476553154)
XLA Ops:
  0.0 2.9 %collective-permute-start.12 = (bf16[256,1536]{1,0:T(8,128)(2,1)}, bf16[256,1536]{1,0:T(8,128)(2,1)S(1)}, u32[]{:S(2)}, u32[]{:S(2)}) collective-permute-start(bf16[256,1536]{1,0:T(8,128)(2,1)} %refs_2_.1), channel_id=1, source_target_pairs={{0,2},{2,0},{1,3},{3,1},{4,6},{6,4},{5,7},{7,5},{8,10},{10,8},{9,1... | collective-permute-start | bytes 2359304 | tf_op jit(solution)/shard_map/ppermute | solution.py:335
  2.9 3.1 %queries.1 = (bf16[128,256]{1,0:T(8,128)(2,1)}, bf16[128,256]{1,0:T(8,128)(2,1)}, bf16[128,256]{1,0:T(8,128)(2,1)}, bf16[128,256]{1,0:T(8,128)(2,1)}, bf16[512,1536]{1,0:T(8,128)(2,1)}) custom-call(s32[4]{0:T(128)} %worker_in.5, bf16[512,1536]{1,0:T(8,128)(2,1)} %latents_in.1, f32[3,1536]{1,0:T(4,128)} %modulation_ref.1, bf16[1536,256]{1,0:T(8,128)(2,1)} %weight_in.3), custom_call_target="tpu_custom_call" | custom-call | flops 402653184 | bytes 2359296 | tf_op jit(solution)/shard_map/queries/pallas_call | solution.py:350
  6.0 5.1 %collective-permute-start = (bf16[128,256]{1,0:T(8,128)(2,1)}, bf16[128,256]{1,0:T(8,128)(2,1)S(1)}, u32[]{:S(2)}, u32[]{:S(2)}) collective-permute-start(bf16[128,256]{1,0:T(8,128)(2,1)} %get-tuple-element.21), channel_id=1, source_target_pairs={{0,12},{4,8},{8,4},{12,0},{1,13},{5,9},{9,5},{13,1},{2,14},{6,10},... | collective-permute-start | bytes 196616 | tf_op jit(solution)/shard_map/ppermute | solution.py:332
  11.1 0.6 %collective-permute-start.2 = (bf16[128,256]{1,0:T(8,128)(2,1)}, bf16[128,256]{1,0:T(8,128)(2,1)S(1)}, u32[]{:S(2)}, u32[]{:S(2)}) collective-permute-start(bf16[128,256]{1,0:T(8,128)(2,1)} %get-tuple-element.23), channel_id=1, source_target_pairs={{0,4},{4,0},{8,12},{12,8},{1,5},{5,1},{9,13},{13,9},{2,6},{6,2},{1... | collective-permute-start | bytes 196616 | tf_op jit(solution)/shard_map/ppermute | solution.py:332
  11.8 2.3 %keys.1.refs_4_.refs_1_.refs_3_ = bf16[512,256]{1,0:T(8,128)(2,1)S(1)} custom-call(s32[4]{0:T(128)S(1)} %copy-done.5, bf16[512,1536]{1,0:T(8,128)(2,1)} %get-tuple-element.24.normed_in, bf16[1536,256]{1,0:T(8,128)(2,1)} %weight_in.4, bf16[512,256]{1,0:T(8,128)(2,1)S(1)} %copy-done.1), custom_call_target="tpu_custom_call" | custom-call | flops 402653184 | bytes 4718592 | tf_op jit(solution)/shard_map/keys/pallas_call | solution.py:371
  14.1 2.5 %collective-permute-done.1.refs_2_ = bf16[128,256]{1,0:T(8,128)(2,1)S(1)} collective-permute-done((bf16[128,256]{1,0:T(8,128)(2,1)}, bf16[128,256]{1,0:T(8,128)(2,1)S(1)}, u32[]{:S(2)}, u32[]{:S(2)}) %collective-permute-start.1) | collective-permute-done | bytes 65568 | tf_op jit(solution)/shard_map/ppermute | solution.py:332
  16.7 2.2 %collective-permute-start.3 = (bf16[128,256]{1,0:T(8,128)(2,1)S(1)}, bf16[128,256]{1,0:T(8,128)(2,1)S(1)}, u32[]{:S(2)}, u32[]{:S(2)}) collective-permute-start(bf16[128,256]{1,0:T(8,128)(2,1)S(1)} %collect.1._.refs_0_), channel_id=1, source_target_pairs={{0,12},{4,8},{8,4},{12,0},{1,13},{5,9},{9,5},{13,1},{2,14},{6,10},... | collective-permute-start | bytes 196616 | tf_op jit(solution)/shard_map/ppermute | solution.py:332
  18.9 0.4 collective-permute-start.4
  19.3 1.9 %collective-permute-start.5 = (bf16[128,256]{1,0:T(8,128)(2,1)S(1)}, bf16[128,256]{1,0:T(8,128)(2,1)S(1)}, u32[]{:S(2)}, u32[]{:S(2)}) collective-permute-start(bf16[128,256]{1,0:T(8,128)(2,1)S(1)} %collect.1._.refs_0_), channel_id=1, source_target_pairs={{0,4},{4,0},{8,12},{12,8},{1,5},{5,1},{9,13},{13,9},{2,6},{6,2},{1... | collective-permute-start | bytes 196616 | tf_op jit(solution)/shard_map/ppermute | solution.py:332
  21.2 2.4 %values.1 = (bf16[256,512]{1,0:T(8,128)(2,1)S(1)}, f32[16,128]{1,0:T(8,128)S(1)}) custom-call(s32[4]{0:T(128)S(1)} %copy-done.5, bf16[512,1536]{1,0:T(8,128)(2,1)} %get-tuple-element.24.normed_in, bf16[1536,256]{1,0:T(8,128)(2,1)} %weight_in.5, bf16[512,256]{1,0:T(8,128)(2,1)S(1)} %copy-done.2, bf16[128,256]{1,0:T(8,128)(2,1)S(1)} %collect.1._.refs_0_), custom_call_target="tpu_custom_call" | custom-call | flops 402653184 | bytes 4718592 | tf_op jit(solution)/shard_map/values/pallas_call | solution.py:397
  23.5 0.7 %attend.2.refs_5_.refs_0_ = bf16[272,128]{1,0:T(8,128)(2,1)S(1)} custom-call(bf16[128,256]{1,0:T(8,128)(2,1)S(1)} %collect.1._.refs_0_, bf16[512,256]{1,0:T(8,128)(2,1)S(1)} %keys.1.refs_4_.refs_1_.refs_3_, bf16[256,512]{1,0:T(8,128)(2,1)S(1)} %get-tuple-element.25.refs_2_.refs_4_), custom_call_target="tpu_custom_call" | custom-call | flops 67108864 | bytes 2621440 | tf_op jit(solution)/shard_map/attend/pallas_call | solution.py:419
  24.3 0.3 collective-permute-done.4.refs_1_
  24.5 1.1 %attend.3 = (bf16[272,128]{1,0:T(8,128)(2,1)S(1)}, bf16[272,128]{1,0:T(8,128)(2,1)S(1)}, bf16[272,128]{1,0:T(8,128)(2,1)S(1)}) custom-call(bf16[128,256]{1,0:T(8,128)(2,1)S(1)} %collective-permute-done.3.refs_0_, bf16[128,256]{1,0:T(8,128)(2,1)S(1)} %collective-permute-done.4.refs_1_, bf16[128,256]{1,0:T(8,128)(2,1)S(1)} %collective-permute-done.5.refs_2_, ...), custom_call_target="tpu_custom_call" | custom-call | flops 201326592 | bytes 2621440 | tf_op jit(solution)/shard_map/attend/pallas_call | solution.py:419
  25.6 2.1 %collective-permute-start.6 = (bf16[272,128]{1,0:T(8,128)(2,1)S(1)}, bf16[272,128]{1,0:T(8,128)(2,1)S(1)}, u32[]{:S(2)}, u32[]{:S(2)}) collective-permute-start(bf16[272,128]{1,0:T(8,128)(2,1)S(1)} %get-tuple-element.26), channel_id=1, source_target_pairs={{0,12},{4,8},{8,4},{12,0},{1,13},{5,9},{9,5},{13,1},{2,14},{6,10},... | collective-permute-start | bytes 208904 | tf_op jit(solution)/shard_map/ppermute | solution.py:332
  27.7 0.4 collective-permute-start.7
  28.0 2.0 %collective-permute-start.8 = (bf16[272,128]{1,0:T(8,128)(2,1)S(1)}, bf16[272,128]{1,0:T(8,128)(2,1)S(1)}, u32[]{:S(2)}, u32[]{:S(2)}) collective-permute-start(bf16[272,128]{1,0:T(8,128)(2,1)S(1)} %get-tuple-element.28), channel_id=1, source_target_pairs={{0,4},{4,0},{8,12},{12,8},{1,5},{5,1},{9,13},{13,9},{2,6},{6,2},{1... | collective-permute-start | bytes 208904 | tf_op jit(solution)/shard_map/ppermute | solution.py:332
  30.1 1.8 %collective-permute-done.6.refs_1_ = bf16[272,128]{1,0:T(8,128)(2,1)S(1)} collective-permute-done((bf16[272,128]{1,0:T(8,128)(2,1)S(1)}, bf16[272,128]{1,0:T(8,128)(2,1)S(1)}, u32[]{:S(2)}, u32[]{:S(2)}) %collective-permute-start.6) | collective-permute-done | bytes 69664 | tf_op jit(solution)/shard_map/ppermute | solution.py:332
  31.8 1.5 %collective-permute-done.7.refs_2_ = bf16[272,128]{1,0:T(8,128)(2,1)S(1)} collective-permute-done((bf16[272,128]{1,0:T(8,128)(2,1)S(1)}, bf16[272,128]{1,0:T(8,128)(2,1)S(1)}, u32[]{:S(2)}, u32[]{:S(2)}) %collective-permute-start.7) | collective-permute-done | bytes 69664 | tf_op jit(solution)/shard_map/ppermute | solution.py:332
  33.3 0.1 combine.1.refs_0_
  33.5 1.7 %collective-permute-start.10 = (bf16[128,256]{1,0:T(8,128)(2,1)S(1)}, bf16[128,256]{1,0:T(8,128)(2,1)S(1)}, u32[]{:S(2)}, u32[]{:S(2)}) collective-permute-start(bf16[128,256]{1,0:T(8,128)(2,1)S(1)} %combine.1.refs_0_), channel_id=1, source_target_pairs={{0,8},{4,12},{8,0},{12,4},{1,9},{5,13},{9,1},{13,5},{2,10},{6,14},... | collective-permute-start | bytes 196616 | tf_op jit(solution)/shard_map/ppermute | solution.py:332
  35.1 2.0 %collective-permute-start.11 = (bf16[128,256]{1,0:T(8,128)(2,1)S(1)}, bf16[128,256]{1,0:T(8,128)(2,1)S(1)}, u32[]{:S(2)}, u32[]{:S(2)}) collective-permute-start(bf16[128,256]{1,0:T(8,128)(2,1)S(1)} %combine.1.refs_0_), channel_id=1, source_target_pairs={{0,12},{4,8},{8,4},{12,0},{1,13},{5,9},{9,5},{13,1},{2,14},{6,10},... | collective-permute-start | bytes 196616 | tf_op jit(solution)/shard_map/ppermute | solution.py:332
  37.2 1.5 %collective-permute-done.10.refs_2_ = bf16[128,256]{1,0:T(8,128)(2,1)S(1)} collective-permute-done((bf16[128,256]{1,0:T(8,128)(2,1)S(1)}, bf16[128,256]{1,0:T(8,128)(2,1)S(1)}, u32[]{:S(2)}, u32[]{:S(2)}) %collective-permute-start.10) | collective-permute-done | bytes 65568 | tf_op jit(solution)/shard_map/ppermute | solution.py:332
  38.7 2.5 %collective-permute-done.11.refs_3_ = bf16[128,256]{1,0:T(8,128)(2,1)S(1)} collective-permute-done((bf16[128,256]{1,0:T(8,128)(2,1)S(1)}, bf16[128,256]{1,0:T(8,128)(2,1)S(1)}, u32[]{:S(2)}, u32[]{:S(2)}) %collective-permute-start.11) | collective-permute-done | bytes 65568 | tf_op jit(solution)/shard_map/ppermute | solution.py:332
  41.2 0.7 %collective-permute-done.9.refs_1_ = bf16[128,256]{1,0:T(8,128)(2,1)S(1)} collective-permute-done((bf16[128,256]{1,0:T(8,128)(2,1)S(1)}, bf16[128,256]{1,0:T(8,128)(2,1)S(1)}, u32[]{:S(2)}, u32[]{:S(2)}) %collective-permute-start.9) | collective-permute-done | bytes 65568 | tf_op jit(solution)/shard_map/ppermute | solution.py:332
  41.9 0.2 select.1
  42.2 0.5 %collective-permute-start.13 = (bf16[128,256]{1,0:T(8,128)(2,1)S(1)}, bf16[128,256]{1,0:T(8,128)(2,1)S(1)}, u32[]{:S(2)}, u32[]{:S(2)}) collective-permute-start(bf16[128,256]{1,0:T(8,128)(2,1)S(1)} %get-tuple-element.31), channel_id=1, source_target_pairs={{0,1},{1,0},{2,3},{3,2},{4,5},{5,4},{6,7},{7,6},{8,9},{9,8},{10,11... | collective-permute-start | bytes 196616 | tf_op jit(solution)/shard_map/ppermute | solution.py:346
  42.7 0.5 %collective-permute-start.15 = (bf16[128,256]{1,0:T(8,128)(2,1)S(1)}, bf16[128,256]{1,0:T(8,128)(2,1)S(1)}, u32[]{:S(2)}, u32[]{:S(2)}) collective-permute-start(bf16[128,256]{1,0:T(8,128)(2,1)S(1)} %get-tuple-element.32), channel_id=1, source_target_pairs={{0,2},{1,3},{2,0},{3,1},{4,6},{5,7},{6,4},{7,5},{8,10},{9,11},{10,... | collective-permute-start | bytes 196616 | tf_op jit(solution)/shard_map/ppermute | solution.py:346
  43.2 0.9 %collective-permute-start.16 = (bf16[128,256]{1,0:T(8,128)(2,1)S(1)}, bf16[128,256]{1,0:T(8,128)(2,1)S(1)}, u32[]{:S(2)}, u32[]{:S(2)}) collective-permute-start(bf16[128,256]{1,0:T(8,128)(2,1)S(1)} %get-tuple-element.33), channel_id=1, source_target_pairs={{0,3},{1,2},{2,1},{3,0},{4,7},{5,6},{6,5},{7,4},{8,11},{9,10},{10,... | collective-permute-start | bytes 196616 | tf_op jit(solution)/shard_map/ppermute | solution.py:346
  44.1 0.4 collective-permute-done.13.refs_1_
  44.5 0.4 project_near.1.near_ref
  44.9 2.7 %collective-permute-done.15.refs_0_ = bf16[128,256]{1,0:T(8,128)(2,1)S(1)} collective-permute-done((bf16[128,256]{1,0:T(8,128)(2,1)S(1)}, bf16[128,256]{1,0:T(8,128)(2,1)S(1)}, u32[]{:S(2)}, u32[]{:S(2)}) %collective-permute-start.15) | collective-permute-done | bytes 65568 | tf_op jit(solution)/shard_map/ppermute | solution.py:346
  47.6 1.2 %project.1 = f32[128,1536]{1,0:T(8,128)} custom-call(f32[3,1536]{1,0:T(4,128)S(1)} %copy-done.3, f32[128,1536]{1,0:T(8,128)S(1)} %project_near.1.near_ref, bf16[128,256]{1,0:T(8,128)(2,1)S(1)} %collective-permute-done.15.refs_0_, bf16[128,256]{1,0:T(8,128)(2,1)S(1)} %collective-permute-done.16.refs_1_, bf16[256,1536]{1,0:T(8,128)(2,1)S(1)} %get-tuple-element.34.refs_2_, ...), custom_call_target="tpu_custom_call" | custom-call | flops 201326592 | bytes 3145728 | tf_op jit(solution)/shard_map/project/pallas_call | solution.py:478
  (26 shorter events, 0.2 us)
Async XLA Ops:
  0.0 11.8 %copy-start.5 = (s32[4]{0:T(128)S(1)}, s32[4]{0:T(128)}, u32[]{:S(2)}) copy-start(s32[4]{0:T(128)} %worker_in.5) | copy-start | bytes 52
  0.0 11.8 %copy-start.1 = (bf16[512,256]{1,0:T(8,128)(2,1)S(1)}, bf16[512,256]{1,0:T(8,128)(2,1)}, u32[]{:S(2)}) copy-start(bf16[512,256]{1,0:T(8,128)(2,1)} %cache_in.2) | copy-start | bytes 786436
  0.0 41.9 %collective-permute-start.12 = (bf16[256,1536]{1,0:T(8,128)(2,1)}, bf16[256,1536]{1,0:T(8,128)(2,1)S(1)}, u32[]{:S(2)}, u32[]{:S(2)}) collective-permute-start(bf16[256,1536]{1,0:T(8,128)(2,1)} %refs_2_.1), channel_id=1, source_target_pairs={{0,2},{2,0},{1,3},{3,1},{4,6},{6,4},{5,7},{7,5},{8,10},{10,8},{9,1... | collective-permute-start | bytes 2359304 | tf_op jit(solution)/shard_map/ppermute | solution.py:335
  6.0 10.6 %copy-start.4 = (bf16[128,256]{1,0:T(8,128)(2,1)S(1)}, bf16[128,256]{1,0:T(8,128)(2,1)}, u32[]{:S(2)}) copy-start(bf16[128,256]{1,0:T(8,128)(2,1)} %get-tuple-element.20.refs_0_) | copy-start | bytes 196612
  6.0 8.0 %collective-permute-start = (bf16[128,256]{1,0:T(8,128)(2,1)}, bf16[128,256]{1,0:T(8,128)(2,1)S(1)}, u32[]{:S(2)}, u32[]{:S(2)}) collective-permute-start(bf16[128,256]{1,0:T(8,128)(2,1)} %get-tuple-element.21), channel_id=1, source_target_pairs={{0,12},{4,8},{8,4},{12,0},{1,13},{5,9},{9,5},{13,1},{2,14},{6,10},... | collective-permute-start | bytes 196616 | tf_op jit(solution)/shard_map/ppermute | solution.py:332
  11.1 5.5 %collective-permute-start.1 = (bf16[128,256]{1,0:T(8,128)(2,1)}, bf16[128,256]{1,0:T(8,128)(2,1)S(1)}, u32[]{:S(2)}, u32[]{:S(2)}) collective-permute-start(bf16[128,256]{1,0:T(8,128)(2,1)} %get-tuple-element.22), channel_id=1, source_target_pairs={{0,8},{4,12},{8,0},{12,4},{1,9},{5,13},{9,1},{13,5},{2,10},{6,14},... | collective-permute-start | bytes 196616 | tf_op jit(solution)/shard_map/ppermute | solution.py:332
  11.1 5.5 %collective-permute-start.2 = (bf16[128,256]{1,0:T(8,128)(2,1)}, bf16[128,256]{1,0:T(8,128)(2,1)S(1)}, u32[]{:S(2)}, u32[]{:S(2)}) collective-permute-start(bf16[128,256]{1,0:T(8,128)(2,1)} %get-tuple-element.23), channel_id=1, source_target_pairs={{0,4},{4,0},{8,12},{12,8},{1,5},{5,1},{9,13},{13,9},{2,6},{6,2},{1... | collective-permute-start | bytes 196616 | tf_op jit(solution)/shard_map/ppermute | solution.py:332
  11.8 9.4 %copy-start.2 = (bf16[512,256]{1,0:T(8,128)(2,1)S(1)}, bf16[512,256]{1,0:T(8,128)(2,1)}, u32[]{:S(2)}) copy-start(bf16[512,256]{1,0:T(8,128)(2,1)} %cache_in.3) | copy-start | bytes 786436
  16.7 20.4 %copy-start = (bf16[256,1536]{1,0:T(8,128)(2,1)S(1)}, bf16[256,1536]{1,0:T(8,128)(2,1)}, u32[]{:S(2)}) copy-start(bf16[256,1536]{1,0:T(8,128)(2,1)} %refs_2_.1) | copy-start | bytes 2359300
  16.7 7.6 %collective-permute-start.3 = (bf16[128,256]{1,0:T(8,128)(2,1)S(1)}, bf16[128,256]{1,0:T(8,128)(2,1)S(1)}, u32[]{:S(2)}, u32[]{:S(2)}) collective-permute-start(bf16[128,256]{1,0:T(8,128)(2,1)S(1)} %collect.1._.refs_0_), channel_id=1, source_target_pairs={{0,12},{4,8},{8,4},{12,0},{1,13},{5,9},{9,5},{13,1},{2,14},{6,10},... | collective-permute-start | bytes 196616 | tf_op jit(solution)/shard_map/ppermute | solution.py:332
  18.9 5.6 %collective-permute-start.4 = (bf16[128,256]{1,0:T(8,128)(2,1)S(1)}, bf16[128,256]{1,0:T(8,128)(2,1)S(1)}, u32[]{:S(2)}, u32[]{:S(2)}) collective-permute-start(bf16[128,256]{1,0:T(8,128)(2,1)S(1)} %collect.1._.refs_0_), channel_id=1, source_target_pairs={{0,8},{4,12},{8,0},{12,4},{1,9},{5,13},{9,1},{13,5},{2,10},{6,14},... | collective-permute-start | bytes 196616 | tf_op jit(solution)/shard_map/ppermute | solution.py:332
  19.3 5.3 %collective-permute-start.5 = (bf16[128,256]{1,0:T(8,128)(2,1)S(1)}, bf16[128,256]{1,0:T(8,128)(2,1)S(1)}, u32[]{:S(2)}, u32[]{:S(2)}) collective-permute-start(bf16[128,256]{1,0:T(8,128)(2,1)S(1)} %collect.1._.refs_0_), channel_id=1, source_target_pairs={{0,4},{4,0},{8,12},{12,8},{1,5},{5,1},{9,13},{13,9},{2,6},{6,2},{1... | collective-permute-start | bytes 196616 | tf_op jit(solution)/shard_map/ppermute | solution.py:332
  25.6 6.2 %collective-permute-start.6 = (bf16[272,128]{1,0:T(8,128)(2,1)S(1)}, bf16[272,128]{1,0:T(8,128)(2,1)S(1)}, u32[]{:S(2)}, u32[]{:S(2)}) collective-permute-start(bf16[272,128]{1,0:T(8,128)(2,1)S(1)} %get-tuple-element.26), channel_id=1, source_target_pairs={{0,12},{4,8},{8,4},{12,0},{1,13},{5,9},{9,5},{13,1},{2,14},{6,10},... | collective-permute-start | bytes 208904 | tf_op jit(solution)/shard_map/ppermute | solution.py:332
  27.7 5.6 %collective-permute-start.7 = (bf16[272,128]{1,0:T(8,128)(2,1)S(1)}, bf16[272,128]{1,0:T(8,128)(2,1)S(1)}, u32[]{:S(2)}, u32[]{:S(2)}) collective-permute-start(bf16[272,128]{1,0:T(8,128)(2,1)S(1)} %get-tuple-element.27), channel_id=1, source_target_pairs={{0,8},{4,12},{8,0},{12,4},{1,9},{5,13},{9,1},{13,5},{2,10},{6,14},... | collective-permute-start | bytes 208904 | tf_op jit(solution)/shard_map/ppermute | solution.py:332
  28.0 5.3 %collective-permute-start.8 = (bf16[272,128]{1,0:T(8,128)(2,1)S(1)}, bf16[272,128]{1,0:T(8,128)(2,1)S(1)}, u32[]{:S(2)}, u32[]{:S(2)}) collective-permute-start(bf16[272,128]{1,0:T(8,128)(2,1)S(1)} %get-tuple-element.28), channel_id=1, source_target_pairs={{0,4},{4,0},{8,12},{12,8},{1,5},{5,1},{9,13},{13,9},{2,6},{6,2},{1... | collective-permute-start | bytes 208904 | tf_op jit(solution)/shard_map/ppermute | solution.py:332
  33.5 5.2 %collective-permute-start.10 = (bf16[128,256]{1,0:T(8,128)(2,1)S(1)}, bf16[128,256]{1,0:T(8,128)(2,1)S(1)}, u32[]{:S(2)}, u32[]{:S(2)}) collective-permute-start(bf16[128,256]{1,0:T(8,128)(2,1)S(1)} %combine.1.refs_0_), channel_id=1, source_target_pairs={{0,8},{4,12},{8,0},{12,4},{1,9},{5,13},{9,1},{13,5},{2,10},{6,14},... | collective-permute-start | bytes 196616 | tf_op jit(solution)/shard_map/ppermute | solution.py:332
  35.1 6.1 %collective-permute-start.11 = (bf16[128,256]{1,0:T(8,128)(2,1)S(1)}, bf16[128,256]{1,0:T(8,128)(2,1)S(1)}, u32[]{:S(2)}, u32[]{:S(2)}) collective-permute-start(bf16[128,256]{1,0:T(8,128)(2,1)S(1)} %combine.1.refs_0_), channel_id=1, source_target_pairs={{0,12},{4,8},{8,4},{12,0},{1,13},{5,9},{9,5},{13,1},{2,14},{6,10},... | collective-permute-start | bytes 196616 | tf_op jit(solution)/shard_map/ppermute | solution.py:332
  37.1 4.8 %collective-permute-start.9 = (bf16[128,256]{1,0:T(8,128)(2,1)S(1)}, bf16[128,256]{1,0:T(8,128)(2,1)S(1)}, u32[]{:S(2)}, u32[]{:S(2)}) collective-permute-start(bf16[128,256]{1,0:T(8,128)(2,1)S(1)} %combine.1.refs_0_), channel_id=1, source_target_pairs={{0,4},{4,0},{8,12},{12,8},{1,5},{5,1},{9,13},{13,9},{2,6},{6,2},{1... | collective-permute-start | bytes 196616 | tf_op jit(solution)/shard_map/ppermute | solution.py:332
  37.1 6.9 %collective-permute-start.14 = (bf16[256,1536]{1,0:T(8,128)(2,1)S(1)}, bf16[256,1536]{1,0:T(8,128)(2,1)S(1)}, u32[]{:S(2)}, u32[]{:S(2)}) collective-permute-start(bf16[256,1536]{1,0:T(8,128)(2,1)S(1)} %copy-done), channel_id=1, source_target_pairs={{0,1},{1,0},{2,3},{3,2},{4,5},{5,4},{6,7},{7,6},{8,9},{9,8},{10,11... | collective-permute-start | bytes 2359304 | tf_op jit(solution)/shard_map/ppermute | solution.py:338
  41.9 5.7 %copy-start.3 = (f32[3,1536]{1,0:T(4,128)S(1)}, f32[3,1536]{1,0:T(4,128)}, u32[]{:S(2)}) copy-start(f32[3,1536]{1,0:T(4,128)} %modulation_ref.1) | copy-start | bytes 55300
  42.1 5.5 %collective-permute-start.17 = (bf16[256,1536]{1,0:T(8,128)(2,1)S(1)}, bf16[256,1536]{1,0:T(8,128)(2,1)S(1)}, u32[]{:S(2)}, u32[]{:S(2)}) collective-permute-start(bf16[256,1536]{1,0:T(8,128)(2,1)S(1)} %get-tuple-element.34.refs_2_), channel_id=1, source_target_pairs={{0,1},{1,0},{2,3},{3,2},{4,5},{5,4},{6,7},{7,6},{8,9},{9,8},{10,11... | collective-permute-start | bytes 2359304 | tf_op jit(solution)/shard_map/ppermute | solution.py:338
  42.2 2.4 %collective-permute-start.13 = (bf16[128,256]{1,0:T(8,128)(2,1)S(1)}, bf16[128,256]{1,0:T(8,128)(2,1)S(1)}, u32[]{:S(2)}, u32[]{:S(2)}) collective-permute-start(bf16[128,256]{1,0:T(8,128)(2,1)S(1)} %get-tuple-element.31), channel_id=1, source_target_pairs={{0,1},{1,0},{2,3},{3,2},{4,5},{5,4},{6,7},{7,6},{8,9},{9,8},{10,11... | collective-permute-start | bytes 196616 | tf_op jit(solution)/shard_map/ppermute | solution.py:346
  42.7 4.9 %collective-permute-start.15 = (bf16[128,256]{1,0:T(8,128)(2,1)S(1)}, bf16[128,256]{1,0:T(8,128)(2,1)S(1)}, u32[]{:S(2)}, u32[]{:S(2)}) collective-permute-start(bf16[128,256]{1,0:T(8,128)(2,1)S(1)} %get-tuple-element.32), channel_id=1, source_target_pairs={{0,2},{1,3},{2,0},{3,1},{4,6},{5,7},{6,4},{7,5},{8,10},{9,11},{10,... | collective-permute-start | bytes 196616 | tf_op jit(solution)/shard_map/ppermute | solution.py:346
  43.2 4.4 %collective-permute-start.16 = (bf16[128,256]{1,0:T(8,128)(2,1)S(1)}, bf16[128,256]{1,0:T(8,128)(2,1)S(1)}, u32[]{:S(2)}, u32[]{:S(2)}) collective-permute-start(bf16[128,256]{1,0:T(8,128)(2,1)S(1)} %get-tuple-element.33), channel_id=1, source_target_pairs={{0,3},{1,2},{2,1},{3,0},{4,7},{5,6},{6,5},{7,4},{8,11},{9,10},{10,... | collective-permute-start | bytes 196616 | tf_op jit(solution)/shard_map/ppermute | solution.py:346

commit v7 on v6

--- a/solution.py
+++ b/solution.py
@@ -366,7 +366,7 @@
         cost_estimate=cost(2 * tokens * model * width, 2 * tokens * model + 2 * model * width),
         name="queries",
     )(block_worker, latents, modulation, query_weight)
-    arrived = [along_frame(slots[s], s) for s in range(n_frame - 1, 0, -1)]
+    arrived = [along_frame(slots[s], s) for s in range(1, n_frame)]
 
     keys = pl.pallas_call(
         key_kernel,
@@ -430,13 +430,13 @@
             name="attend",
         )(*queries, keys, values_t, *after)
 
-    far_first = list(range(n_frame - 1, 0, -1))
-    shared = [along_frame(mine, s) for s in far_first]
+    near_first = list(range(1, n_frame))
+    shared = [along_frame(mine, s) for s in near_first]
     own = list(attend([mine]))
     partial = []
     for start in range(0, n_frame - 1, SLOTS):
         partial += attend(shared[start : start + SLOTS], own)
-    sent = [along_frame(x, s) for s, x in zip(far_first, partial)]
+    sent = [along_frame(x, s) for s, x in zip(near_first, partial)]
     attended = pl.pallas_call(
         combine_kernel,
         out_shape=jax.ShapeDtypeStruct((block_rows, width), half),
@@ -446,7 +446,7 @@
         cost_estimate=cost(4 * n_frame * block_rows * width, 2 * n_frame * block_rows * width),
         name="combine",
     )(*own, *sent)
-    copies = {s: along_frame(attended, s) for s in far_first}
+    copies = {s: along_frame(attended, s) for s in near_first}
     copies = [attended] + [copies[s] for s in range(1, n_frame)]
     pieces = pl.pallas_call(
         functools.partial(select_kernel, n_frame, n_head, n_rep),

time: 49.5 us -> 51.6 us (1.042)
  waiting for transfers between devices: 13.9 us -> 16.8 us
    ppermute x12, waiting for transfers between devices: 10.8 us -> 13.7 us  [along_frame(): return lax.ppermute(x, 'frame', [(i, i ^ s) for i in range(n_frame)])]
  transfers between devices with their start and end apart: 18 -> 18, of which waited for: 9 -> 11; matrix products, arithmetic and copies ran while one was open for 0% -> 0% of each run, Pallas kernels for 21% -> 20%
where the time goes in v7:
time: 51.6 us; the launch traced here: 51.3 us
  starting transfers between devices  22.9 us (44%)
  waiting for transfers between devices  16.8 us (33%)
  Pallas kernels  11.4 us (22%)
    ppermute x12, starting transfers between devices, along_frame(): return lax.ppermute(x, 'frame', [(i, i ^ s) for i in range(n_frame)])  18 us
    ppermute x12, waiting for transfers between devices, along_frame(): return lax.ppermute(x, 'frame', [(i, i ^ s) for i in range(n_frame)])  13.7 us
    ppermute x3, waiting for transfers between devices, in_frame(): return lax.ppermute(x, ('head', 'rep'), pairs)  3.12 us
    pallas_call x1, Pallas kernels, per_device(): pl.pallas_call(functools.partial(query_kernel, n_frame), out_shape=[jax.S...  3.07 us
    ppermute x1, starting transfers between devices, along_head(): lax.ppermute(x, 'head', [(i, (i + shift) % n_head) for i in range(n_head)])  2.94 us
    pallas_call x1, Pallas kernels, per_device(): pl.pallas_call(functools.partial(value_kernel, n_frame, n_head, n_rep), o...  2.36 us
    pallas_call x1, Pallas kernels, per_device(): pl.pallas_call(key_kernel, out_shape=jax.ShapeDtypeStruct((tokens, width)...  2.28 us
    ppermute x3, starting transfers between devices, in_frame(): return lax.ppermute(x, ('head', 'rep'), pairs)  1.93 us
  transfers between devices with their start and end apart: 18, of which 11 were waited for; matrix products, arithmetic and copies ran while one was open for 0% of the time, Pallas kernels for 20%

profile of v7, /device:TPU:0, one launch (start us, length us, event | category | flops | bytes accessed | tf_op | source)
XLA Modules:
  0.0 51.3 jit_solution(16828931355813980868)
XLA Ops:
  0.0 2.9 %collective-permute-start.12 = (bf16[256,1536]{1,0:T(8,128)(2,1)}, bf16[256,1536]{1,0:T(8,128)(2,1)S(1)}, u32[]{:S(2)}, u32[]{:S(2)}) collective-permute-start(bf16[256,1536]{1,0:T(8,128)(2,1)} %refs_2_.1), channel_id=1, source_target_pairs={{0,2},{2,0},{1,3},{3,1},{4,6},{6,4},{5,7},{7,5},{8,10},{10,8},{9,1... | collective-permute-start | bytes 2359304 | tf_op jit(solution)/shard_map/ppermute | solution.py:335
  2.9 3.1 %queries.1 = (bf16[128,256]{1,0:T(8,128)(2,1)}, bf16[128,256]{1,0:T(8,128)(2,1)}, bf16[128,256]{1,0:T(8,128)(2,1)}, bf16[128,256]{1,0:T(8,128)(2,1)}, bf16[512,1536]{1,0:T(8,128)(2,1)}) custom-call(s32[4]{0:T(128)} %worker_in.5, bf16[512,1536]{1,0:T(8,128)(2,1)} %latents_in.1, f32[3,1536]{1,0:T(4,128)} %modulation_ref.1, bf16[1536,256]{1,0:T(8,128)(2,1)} %weight_in.3), custom_call_target="tpu_custom_call" | custom-call | flops 402653184 | bytes 2359296 | tf_op jit(solution)/shard_map/queries/pallas_call | solution.py:350
  6.0 1.6 %collective-permute-start = (bf16[128,256]{1,0:T(8,128)(2,1)}, bf16[128,256]{1,0:T(8,128)(2,1)S(1)}, u32[]{:S(2)}, u32[]{:S(2)}) collective-permute-start(bf16[128,256]{1,0:T(8,128)(2,1)} %get-tuple-element.21), channel_id=1, source_target_pairs={{0,4},{4,0},{8,12},{12,8},{1,5},{5,1},{9,13},{13,9},{2,6},{6,2},{1... | collective-permute-start | bytes 196616 | tf_op jit(solution)/shard_map/ppermute | solution.py:332
  7.7 2.6 %collective-permute-start.1 = (bf16[128,256]{1,0:T(8,128)(2,1)}, bf16[128,256]{1,0:T(8,128)(2,1)S(1)}, u32[]{:S(2)}, u32[]{:S(2)}) collective-permute-start(bf16[128,256]{1,0:T(8,128)(2,1)} %get-tuple-element.22), channel_id=1, source_target_pairs={{0,8},{4,12},{8,0},{12,4},{1,9},{5,13},{9,1},{13,5},{2,10},{6,14},... | collective-permute-start | bytes 196616 | tf_op jit(solution)/shard_map/ppermute | solution.py:332
  10.3 1.3 %collective-permute-start.2 = (bf16[128,256]{1,0:T(8,128)(2,1)}, bf16[128,256]{1,0:T(8,128)(2,1)S(1)}, u32[]{:S(2)}, u32[]{:S(2)}) collective-permute-start(bf16[128,256]{1,0:T(8,128)(2,1)} %get-tuple-element.23), channel_id=1, source_target_pairs={{0,12},{4,8},{8,4},{12,0},{1,13},{5,9},{9,5},{13,1},{2,14},{6,10},... | collective-permute-start | bytes 196616 | tf_op jit(solution)/shard_map/ppermute | solution.py:332
  11.6 2.3 %keys.1.refs_4_.refs_1_.refs_3_ = bf16[512,256]{1,0:T(8,128)(2,1)S(1)} custom-call(s32[4]{0:T(128)S(1)} %copy-done.5, bf16[512,1536]{1,0:T(8,128)(2,1)} %get-tuple-element.24.normed_in, bf16[1536,256]{1,0:T(8,128)(2,1)} %weight_in.4, bf16[512,256]{1,0:T(8,128)(2,1)S(1)} %copy-done.1), custom_call_target="tpu_custom_call" | custom-call | flops 402653184 | bytes 4718592 | tf_op jit(solution)/shard_map/keys/pallas_call | solution.py:371
  14.1 2.5 %collective-permute-done.2.refs_3_ = bf16[128,256]{1,0:T(8,128)(2,1)S(1)} collective-permute-done((bf16[128,256]{1,0:T(8,128)(2,1)}, bf16[128,256]{1,0:T(8,128)(2,1)S(1)}, u32[]{:S(2)}, u32[]{:S(2)}) %collective-permute-start.2) | collective-permute-done | bytes 65568 | tf_op jit(solution)/shard_map/ppermute | solution.py:332
  16.6 1.3 %collective-permute-start.3 = (bf16[128,256]{1,0:T(8,128)(2,1)S(1)}, bf16[128,256]{1,0:T(8,128)(2,1)S(1)}, u32[]{:S(2)}, u32[]{:S(2)}) collective-permute-start(bf16[128,256]{1,0:T(8,128)(2,1)S(1)} %collect.1._.refs_0_), channel_id=1, source_target_pairs={{0,4},{4,0},{8,12},{12,8},{1,5},{5,1},{9,13},{13,9},{2,6},{6,2},{1... | collective-permute-start | bytes 196616 | tf_op jit(solution)/shard_map/ppermute | solution.py:332
  17.9 1.8 %collective-permute-start.4 = (bf16[128,256]{1,0:T(8,128)(2,1)S(1)}, bf16[128,256]{1,0:T(8,128)(2,1)S(1)}, u32[]{:S(2)}, u32[]{:S(2)}) collective-permute-start(bf16[128,256]{1,0:T(8,128)(2,1)S(1)} %collect.1._.refs_0_), channel_id=1, source_target_pairs={{0,8},{4,12},{8,0},{12,4},{1,9},{5,13},{9,1},{13,5},{2,10},{6,14},... | collective-permute-start | bytes 196616 | tf_op jit(solution)/shard_map/ppermute | solution.py:332
  19.7 1.4 %collective-permute-start.5 = (bf16[128,256]{1,0:T(8,128)(2,1)S(1)}, bf16[128,256]{1,0:T(8,128)(2,1)S(1)}, u32[]{:S(2)}, u32[]{:S(2)}) collective-permute-start(bf16[128,256]{1,0:T(8,128)(2,1)S(1)} %collect.1._.refs_0_), channel_id=1, source_target_pairs={{0,12},{4,8},{8,4},{12,0},{1,13},{5,9},{9,5},{13,1},{2,14},{6,10},... | collective-permute-start | bytes 196616 | tf_op jit(solution)/shard_map/ppermute | solution.py:332
  21.1 2.4 %values.1 = (bf16[256,512]{1,0:T(8,128)(2,1)S(1)}, f32[16,128]{1,0:T(8,128)S(1)}) custom-call(s32[4]{0:T(128)S(1)} %copy-done.5, bf16[512,1536]{1,0:T(8,128)(2,1)} %get-tuple-element.24.normed_in, bf16[1536,256]{1,0:T(8,128)(2,1)} %weight_in.5, bf16[512,256]{1,0:T(8,128)(2,1)S(1)} %copy-done.2, bf16[128,256]{1,0:T(8,128)(2,1)S(1)} %collect.1._.refs_0_), custom_call_target="tpu_custom_call" | custom-call | flops 402653184 | bytes 4718592 | tf_op jit(solution)/shard_map/values/pallas_call | solution.py:397
  23.5 0.7 %attend.2.refs_5_.refs_0_ = bf16[272,128]{1,0:T(8,128)(2,1)S(1)} custom-call(bf16[128,256]{1,0:T(8,128)(2,1)S(1)} %collect.1._.refs_0_, bf16[512,256]{1,0:T(8,128)(2,1)S(1)} %keys.1.refs_4_.refs_1_.refs_3_, bf16[256,512]{1,0:T(8,128)(2,1)S(1)} %get-tuple-element.25.refs_2_.refs_4_), custom_call_target="tpu_custom_call" | custom-call | flops 67108864 | bytes 2621440 | tf_op jit(solution)/shard_map/attend/pallas_call | solution.py:419
  24.2 0.9 %collective-permute-done.4.refs_1_ = bf16[128,256]{1,0:T(8,128)(2,1)S(1)} collective-permute-done((bf16[128,256]{1,0:T(8,128)(2,1)S(1)}, bf16[128,256]{1,0:T(8,128)(2,1)S(1)}, u32[]{:S(2)}, u32[]{:S(2)}) %collective-permute-start.4) | collective-permute-done | bytes 65568 | tf_op jit(solution)/shard_map/ppermute | solution.py:332
  25.1 0.7 %collective-permute-done.5.refs_2_ = bf16[128,256]{1,0:T(8,128)(2,1)S(1)} collective-permute-done((bf16[128,256]{1,0:T(8,128)(2,1)S(1)}, bf16[128,256]{1,0:T(8,128)(2,1)S(1)}, u32[]{:S(2)}, u32[]{:S(2)}) %collective-permute-start.5) | collective-permute-done | bytes 65568 | tf_op jit(solution)/shard_map/ppermute | solution.py:332
  25.9 1.1 %attend.3 = (bf16[272,128]{1,0:T(8,128)(2,1)S(1)}, bf16[272,128]{1,0:T(8,128)(2,1)S(1)}, bf16[272,128]{1,0:T(8,128)(2,1)S(1)}) custom-call(bf16[128,256]{1,0:T(8,128)(2,1)S(1)} %collective-permute-done.3.refs_0_, bf16[128,256]{1,0:T(8,128)(2,1)S(1)} %collective-permute-done.4.refs_1_, bf16[128,256]{1,0:T(8,128)(2,1)S(1)} %collective-permute-done.5.refs_2_, ...), custom_call_target="tpu_custom_call" | custom-call | flops 201326592 | bytes 2621440 | tf_op jit(solution)/shard_map/attend/pallas_call | solution.py:419
  27.0 1.3 %collective-permute-start.6 = (bf16[272,128]{1,0:T(8,128)(2,1)S(1)}, bf16[272,128]{1,0:T(8,128)(2,1)S(1)}, u32[]{:S(2)}, u32[]{:S(2)}) collective-permute-start(bf16[272,128]{1,0:T(8,128)(2,1)S(1)} %get-tuple-element.26), channel_id=1, source_target_pairs={{0,4},{4,0},{8,12},{12,8},{1,5},{5,1},{9,13},{13,9},{2,6},{6,2},{1... | collective-permute-start | bytes 208904 | tf_op jit(solution)/shard_map/ppermute | solution.py:332
  28.2 1.8 %collective-permute-start.7 = (bf16[272,128]{1,0:T(8,128)(2,1)S(1)}, bf16[272,128]{1,0:T(8,128)(2,1)S(1)}, u32[]{:S(2)}, u32[]{:S(2)}) collective-permute-start(bf16[272,128]{1,0:T(8,128)(2,1)S(1)} %get-tuple-element.27), channel_id=1, source_target_pairs={{0,8},{4,12},{8,0},{12,4},{1,9},{5,13},{9,1},{13,5},{2,10},{6,14},... | collective-permute-start | bytes 208904 | tf_op jit(solution)/shard_map/ppermute | solution.py:332
  30.0 1.4 %collective-permute-start.8 = (bf16[272,128]{1,0:T(8,128)(2,1)S(1)}, bf16[272,128]{1,0:T(8,128)(2,1)S(1)}, u32[]{:S(2)}, u32[]{:S(2)}) collective-permute-start(bf16[272,128]{1,0:T(8,128)(2,1)S(1)} %get-tuple-element.28), channel_id=1, source_target_pairs={{0,12},{4,8},{8,4},{12,0},{1,13},{5,9},{9,5},{13,1},{2,14},{6,10},... | collective-permute-start | bytes 208904 | tf_op jit(solution)/shard_map/ppermute | solution.py:332
  31.4 3.4 %collective-permute-done.7.refs_2_ = bf16[272,128]{1,0:T(8,128)(2,1)S(1)} collective-permute-done((bf16[272,128]{1,0:T(8,128)(2,1)S(1)}, bf16[272,128]{1,0:T(8,128)(2,1)S(1)}, u32[]{:S(2)}, u32[]{:S(2)}) %collective-permute-start.7) | collective-permute-done | bytes 69664 | tf_op jit(solution)/shard_map/ppermute | solution.py:332
  34.8 1.4 %collective-permute-done.8.refs_3_ = bf16[272,128]{1,0:T(8,128)(2,1)S(1)} collective-permute-done((bf16[272,128]{1,0:T(8,128)(2,1)S(1)}, bf16[272,128]{1,0:T(8,128)(2,1)S(1)}, u32[]{:S(2)}, u32[]{:S(2)}) %collective-permute-start.8) | collective-permute-done | bytes 69664 | tf_op jit(solution)/shard_map/ppermute | solution.py:332
  36.4 1.8 %collective-permute-start.10 = (bf16[128,256]{1,0:T(8,128)(2,1)S(1)}, bf16[128,256]{1,0:T(8,128)(2,1)S(1)}, u32[]{:S(2)}, u32[]{:S(2)}) collective-permute-start(bf16[128,256]{1,0:T(8,128)(2,1)S(1)} %combine.1.refs_0_), channel_id=1, source_target_pairs={{0,8},{4,12},{8,0},{12,4},{1,9},{5,13},{9,1},{13,5},{2,10},{6,14},... | collective-permute-start | bytes 196616 | tf_op jit(solution)/shard_map/ppermute | solution.py:332
  38.2 1.3 %collective-permute-start.11 = (bf16[128,256]{1,0:T(8,128)(2,1)S(1)}, bf16[128,256]{1,0:T(8,128)(2,1)S(1)}, u32[]{:S(2)}, u32[]{:S(2)}) collective-permute-start(bf16[128,256]{1,0:T(8,128)(2,1)S(1)} %combine.1.refs_0_), channel_id=1, source_target_pairs={{0,12},{4,8},{8,4},{12,0},{1,13},{5,9},{9,5},{13,1},{2,14},{6,10},... | collective-permute-start | bytes 196616 | tf_op jit(solution)/shard_map/ppermute | solution.py:332
  39.5 0.5 collective-permute-start.9
  39.9 3.1 %collective-permute-done.10.refs_2_ = bf16[128,256]{1,0:T(8,128)(2,1)S(1)} collective-permute-done((bf16[128,256]{1,0:T(8,128)(2,1)S(1)}, bf16[128,256]{1,0:T(8,128)(2,1)S(1)}, u32[]{:S(2)}, u32[]{:S(2)}) %collective-permute-start.10) | collective-permute-done | bytes 65568 | tf_op jit(solution)/shard_map/ppermute | solution.py:332
  43.0 1.4 %collective-permute-done.11.refs_3_ = bf16[128,256]{1,0:T(8,128)(2,1)S(1)} collective-permute-done((bf16[128,256]{1,0:T(8,128)(2,1)S(1)}, bf16[128,256]{1,0:T(8,128)(2,1)S(1)}, u32[]{:S(2)}, u32[]{:S(2)}) %collective-permute-start.11) | collective-permute-done | bytes 65568 | tf_op jit(solution)/shard_map/ppermute | solution.py:332
  44.7 0.5 collective-permute-start.13
  45.2 0.5 %collective-permute-start.15 = (bf16[128,256]{1,0:T(8,128)(2,1)S(1)}, bf16[128,256]{1,0:T(8,128)(2,1)S(1)}, u32[]{:S(2)}, u32[]{:S(2)}) collective-permute-start(bf16[128,256]{1,0:T(8,128)(2,1)S(1)} %get-tuple-element.32), channel_id=1, source_target_pairs={{0,2},{1,3},{2,0},{3,1},{4,6},{5,7},{6,4},{7,5},{8,10},{9,11},{10,... | collective-permute-start | bytes 196616 | tf_op jit(solution)/shard_map/ppermute | solution.py:346
  45.7 0.9 %collective-permute-start.16 = (bf16[128,256]{1,0:T(8,128)(2,1)S(1)}, bf16[128,256]{1,0:T(8,128)(2,1)S(1)}, u32[]{:S(2)}, u32[]{:S(2)}) collective-permute-start(bf16[128,256]{1,0:T(8,128)(2,1)S(1)} %get-tuple-element.33), channel_id=1, source_target_pairs={{0,3},{1,2},{2,1},{3,0},{4,7},{5,6},{6,5},{7,4},{8,11},{9,10},{10,... | collective-permute-start | bytes 196616 | tf_op jit(solution)/shard_map/ppermute | solution.py:346
  46.6 0.4 collective-permute-done.13.refs_1_
  47.1 0.4 project_near.1.near_ref
  47.5 2.7 %collective-permute-done.15.refs_0_ = bf16[128,256]{1,0:T(8,128)(2,1)S(1)} collective-permute-done((bf16[128,256]{1,0:T(8,128)(2,1)S(1)}, bf16[128,256]{1,0:T(8,128)(2,1)S(1)}, u32[]{:S(2)}, u32[]{:S(2)}) %collective-permute-start.15) | collective-permute-done | bytes 65568 | tf_op jit(solution)/shard_map/ppermute | solution.py:346
  50.2 1.1 %project.1 = f32[128,1536]{1,0:T(8,128)} custom-call(f32[3,1536]{1,0:T(4,128)S(1)} %copy-done.3, f32[128,1536]{1,0:T(8,128)S(1)} %project_near.1.near_ref, bf16[128,256]{1,0:T(8,128)(2,1)S(1)} %collective-permute-done.15.refs_0_, bf16[128,256]{1,0:T(8,128)(2,1)S(1)} %collective-permute-done.16.refs_1_, bf16[256,1536]{1,0:T(8,128)(2,1)S(1)} %get-tuple-element.34.refs_2_, ...), custom_call_target="tpu_custom_call" | custom-call | flops 201326592 | bytes 3145728 | tf_op jit(solution)/shard_map/project/pallas_call | solution.py:478
  (26 shorter events, 0.8 us)
Async XLA Ops:
  0.0 11.6 %copy-start.5 = (s32[4]{0:T(128)S(1)}, s32[4]{0:T(128)}, u32[]{:S(2)}) copy-start(s32[4]{0:T(128)} %worker_in.5) | copy-start | bytes 52
  0.0 11.6 %copy-start.1 = (bf16[512,256]{1,0:T(8,128)(2,1)S(1)}, bf16[512,256]{1,0:T(8,128)(2,1)}, u32[]{:S(2)}) copy-start(bf16[512,256]{1,0:T(8,128)(2,1)} %cache_in.2) | copy-start | bytes 786436
  0.0 44.4 %collective-permute-start.12 = (bf16[256,1536]{1,0:T(8,128)(2,1)}, bf16[256,1536]{1,0:T(8,128)(2,1)S(1)}, u32[]{:S(2)}, u32[]{:S(2)}) collective-permute-start(bf16[256,1536]{1,0:T(8,128)(2,1)} %refs_2_.1), channel_id=1, source_target_pairs={{0,2},{2,0},{1,3},{3,1},{4,6},{6,4},{5,7},{7,5},{8,10},{10,8},{9,1... | collective-permute-start | bytes 2359304 | tf_op jit(solution)/shard_map/ppermute | solution.py:335
  6.0 10.6 %copy-start.4 = (bf16[128,256]{1,0:T(8,128)(2,1)S(1)}, bf16[128,256]{1,0:T(8,128)(2,1)}, u32[]{:S(2)}) copy-start(bf16[128,256]{1,0:T(8,128)(2,1)} %get-tuple-element.20.refs_0_) | copy-start | bytes 196612
  6.0 7.8 %collective-permute-start = (bf16[128,256]{1,0:T(8,128)(2,1)}, bf16[128,256]{1,0:T(8,128)(2,1)S(1)}, u32[]{:S(2)}, u32[]{:S(2)}) collective-permute-start(bf16[128,256]{1,0:T(8,128)(2,1)} %get-tuple-element.21), channel_id=1, source_target_pairs={{0,4},{4,0},{8,12},{12,8},{1,5},{5,1},{9,13},{13,9},{2,6},{6,2},{1... | collective-permute-start | bytes 196616 | tf_op jit(solution)/shard_map/ppermute | solution.py:332
  7.7 6.4 %collective-permute-start.1 = (bf16[128,256]{1,0:T(8,128)(2,1)}, bf16[128,256]{1,0:T(8,128)(2,1)S(1)}, u32[]{:S(2)}, u32[]{:S(2)}) collective-permute-start(bf16[128,256]{1,0:T(8,128)(2,1)} %get-tuple-element.22), channel_id=1, source_target_pairs={{0,8},{4,12},{8,0},{12,4},{1,9},{5,13},{9,1},{13,5},{2,10},{6,14},... | collective-permute-start | bytes 196616 | tf_op jit(solution)/shard_map/ppermute | solution.py:332
  10.3 6.3 %collective-permute-start.2 = (bf16[128,256]{1,0:T(8,128)(2,1)}, bf16[128,256]{1,0:T(8,128)(2,1)S(1)}, u32[]{:S(2)}, u32[]{:S(2)}) collective-permute-start(bf16[128,256]{1,0:T(8,128)(2,1)} %get-tuple-element.23), channel_id=1, source_target_pairs={{0,12},{4,8},{8,4},{12,0},{1,13},{5,9},{9,5},{13,1},{2,14},{6,10},... | collective-permute-start | bytes 196616 | tf_op jit(solution)/shard_map/ppermute | solution.py:332
  11.6 9.5 %copy-start.2 = (bf16[512,256]{1,0:T(8,128)(2,1)S(1)}, bf16[512,256]{1,0:T(8,128)(2,1)}, u32[]{:S(2)}) copy-start(bf16[512,256]{1,0:T(8,128)(2,1)} %cache_in.3) | copy-start | bytes 786436
  16.6 23.3 %copy-start = (bf16[256,1536]{1,0:T(8,128)(2,1)S(1)}, bf16[256,1536]{1,0:T(8,128)(2,1)}, u32[]{:S(2)}) copy-start(bf16[256,1536]{1,0:T(8,128)(2,1)} %refs_2_.1) | copy-start | bytes 2359300
  16.6 7.6 %collective-permute-start.3 = (bf16[128,256]{1,0:T(8,128)(2,1)S(1)}, bf16[128,256]{1,0:T(8,128)(2,1)S(1)}, u32[]{:S(2)}, u32[]{:S(2)}) collective-permute-start(bf16[128,256]{1,0:T(8,128)(2,1)S(1)} %collect.1._.refs_0_), channel_id=1, source_target_pairs={{0,4},{4,0},{8,12},{12,8},{1,5},{5,1},{9,13},{13,9},{2,6},{6,2},{1... | collective-permute-start | bytes 196616 | tf_op jit(solution)/shard_map/ppermute | solution.py:332
  17.9 7.2 %collective-permute-start.4 = (bf16[128,256]{1,0:T(8,128)(2,1)S(1)}, bf16[128,256]{1,0:T(8,128)(2,1)S(1)}, u32[]{:S(2)}, u32[]{:S(2)}) collective-permute-start(bf16[128,256]{1,0:T(8,128)(2,1)S(1)} %collect.1._.refs_0_), channel_id=1, source_target_pairs={{0,8},{4,12},{8,0},{12,4},{1,9},{5,13},{9,1},{13,5},{2,10},{6,14},... | collective-permute-start | bytes 196616 | tf_op jit(solution)/shard_map/ppermute | solution.py:332
  19.7 6.2 %collective-permute-start.5 = (bf16[128,256]{1,0:T(8,128)(2,1)S(1)}, bf16[128,256]{1,0:T(8,128)(2,1)S(1)}, u32[]{:S(2)}, u32[]{:S(2)}) collective-permute-start(bf16[128,256]{1,0:T(8,128)(2,1)S(1)} %collect.1._.refs_0_), channel_id=1, source_target_pairs={{0,12},{4,8},{8,4},{12,0},{1,13},{5,9},{9,5},{13,1},{2,14},{6,10},... | collective-permute-start | bytes 196616 | tf_op jit(solution)/shard_map/ppermute | solution.py:332
  27.0 4.5 %collective-permute-start.6 = (bf16[272,128]{1,0:T(8,128)(2,1)S(1)}, bf16[272,128]{1,0:T(8,128)(2,1)S(1)}, u32[]{:S(2)}, u32[]{:S(2)}) collective-permute-start(bf16[272,128]{1,0:T(8,128)(2,1)S(1)} %get-tuple-element.26), channel_id=1, source_target_pairs={{0,4},{4,0},{8,12},{12,8},{1,5},{5,1},{9,13},{13,9},{2,6},{6,2},{1... | collective-permute-start | bytes 208904 | tf_op jit(solution)/shard_map/ppermute | solution.py:332
  28.2 6.6 %collective-permute-start.7 = (bf16[272,128]{1,0:T(8,128)(2,1)S(1)}, bf16[272,128]{1,0:T(8,128)(2,1)S(1)}, u32[]{:S(2)}, u32[]{:S(2)}) collective-permute-start(bf16[272,128]{1,0:T(8,128)(2,1)S(1)} %get-tuple-element.27), channel_id=1, source_target_pairs={{0,8},{4,12},{8,0},{12,4},{1,9},{5,13},{9,1},{13,5},{2,10},{6,14},... | collective-permute-start | bytes 208904 | tf_op jit(solution)/shard_map/ppermute | solution.py:332
  30.0 6.2 %collective-permute-start.8 = (bf16[272,128]{1,0:T(8,128)(2,1)S(1)}, bf16[272,128]{1,0:T(8,128)(2,1)S(1)}, u32[]{:S(2)}, u32[]{:S(2)}) collective-permute-start(bf16[272,128]{1,0:T(8,128)(2,1)S(1)} %get-tuple-element.28), channel_id=1, source_target_pairs={{0,12},{4,8},{8,4},{12,0},{1,13},{5,9},{9,5},{13,1},{2,14},{6,10},... | collective-permute-start | bytes 208904 | tf_op jit(solution)/shard_map/ppermute | solution.py:332
  36.4 6.6 %collective-permute-start.10 = (bf16[128,256]{1,0:T(8,128)(2,1)S(1)}, bf16[128,256]{1,0:T(8,128)(2,1)S(1)}, u32[]{:S(2)}, u32[]{:S(2)}) collective-permute-start(bf16[128,256]{1,0:T(8,128)(2,1)S(1)} %combine.1.refs_0_), channel_id=1, source_target_pairs={{0,8},{4,12},{8,0},{12,4},{1,9},{5,13},{9,1},{13,5},{2,10},{6,14},... | collective-permute-start | bytes 196616 | tf_op jit(solution)/shard_map/ppermute | solution.py:332
  38.2 6.2 %collective-permute-start.11 = (bf16[128,256]{1,0:T(8,128)(2,1)S(1)}, bf16[128,256]{1,0:T(8,128)(2,1)S(1)}, u32[]{:S(2)}, u32[]{:S(2)}) collective-permute-start(bf16[128,256]{1,0:T(8,128)(2,1)S(1)} %combine.1.refs_0_), channel_id=1, source_target_pairs={{0,12},{4,8},{8,4},{12,0},{1,13},{5,9},{9,5},{13,1},{2,14},{6,10},... | collective-permute-start | bytes 196616 | tf_op jit(solution)/shard_map/ppermute | solution.py:332
  39.5 5.0 %collective-permute-start.9 = (bf16[128,256]{1,0:T(8,128)(2,1)S(1)}, bf16[128,256]{1,0:T(8,128)(2,1)S(1)}, u32[]{:S(2)}, u32[]{:S(2)}) collective-permute-start(bf16[128,256]{1,0:T(8,128)(2,1)S(1)} %combine.1.refs_0_), channel_id=1, source_target_pairs={{0,4},{4,0},{8,12},{12,8},{1,5},{5,1},{9,13},{13,9},{2,6},{6,2},{1... | collective-permute-start | bytes 196616 | tf_op jit(solution)/shard_map/ppermute | solution.py:332
  39.9 6.7 %collective-permute-start.14 = (bf16[256,1536]{1,0:T(8,128)(2,1)S(1)}, bf16[256,1536]{1,0:T(8,128)(2,1)S(1)}, u32[]{:S(2)}, u32[]{:S(2)}) collective-permute-start(bf16[256,1536]{1,0:T(8,128)(2,1)S(1)} %copy-done), channel_id=1, source_target_pairs={{0,1},{1,0},{2,3},{3,2},{4,5},{5,4},{6,7},{7,6},{8,9},{9,8},{10,11... | collective-permute-start | bytes 2359304 | tf_op jit(solution)/shard_map/ppermute | solution.py:338
  44.4 5.7 %copy-start.3 = (f32[3,1536]{1,0:T(4,128)S(1)}, f32[3,1536]{1,0:T(4,128)}, u32[]{:S(2)}) copy-start(f32[3,1536]{1,0:T(4,128)} %modulation_ref.1) | copy-start | bytes 55300
  44.6 5.5 %collective-permute-start.17 = (bf16[256,1536]{1,0:T(8,128)(2,1)S(1)}, bf16[256,1536]{1,0:T(8,128)(2,1)S(1)}, u32[]{:S(2)}, u32[]{:S(2)}) collective-permute-start(bf16[256,1536]{1,0:T(8,128)(2,1)S(1)} %get-tuple-element.34.refs_2_), channel_id=1, source_target_pairs={{0,1},{1,0},{2,3},{3,2},{4,5},{5,4},{6,7},{7,6},{8,9},{9,8},{10,11... | collective-permute-start | bytes 2359304 | tf_op jit(solution)/shard_map/ppermute | solution.py:338
  44.7 2.4 %collective-permute-start.13 = (bf16[128,256]{1,0:T(8,128)(2,1)S(1)}, bf16[128,256]{1,0:T(8,128)(2,1)S(1)}, u32[]{:S(2)}, u32[]{:S(2)}) collective-permute-start(bf16[128,256]{1,0:T(8,128)(2,1)S(1)} %get-tuple-element.31), channel_id=1, source_target_pairs={{0,1},{1,0},{2,3},{3,2},{4,5},{5,4},{6,7},{7,6},{8,9},{9,8},{10,11... | collective-permute-start | bytes 196616 | tf_op jit(solution)/shard_map/ppermute | solution.py:346
  45.2 4.9 %collective-permute-start.15 = (bf16[128,256]{1,0:T(8,128)(2,1)S(1)}, bf16[128,256]{1,0:T(8,128)(2,1)S(1)}, u32[]{:S(2)}, u32[]{:S(2)}) collective-permute-start(bf16[128,256]{1,0:T(8,128)(2,1)S(1)} %get-tuple-element.32), channel_id=1, source_target_pairs={{0,2},{1,3},{2,0},{3,1},{4,6},{5,7},{6,4},{7,5},{8,10},{9,11},{10,... | collective-permute-start | bytes 196616 | tf_op jit(solution)/shard_map/ppermute | solution.py:346
  45.7 4.4 %collective-permute-start.16 = (bf16[128,256]{1,0:T(8,128)(2,1)S(1)}, bf16[128,256]{1,0:T(8,128)(2,1)S(1)}, u32[]{:S(2)}, u32[]{:S(2)}) collective-permute-start(bf16[128,256]{1,0:T(8,128)(2,1)S(1)} %get-tuple-element.33), channel_id=1, source_target_pairs={{0,3},{1,2},{2,1},{3,0},{4,7},{5,6},{6,5},{7,4},{8,11},{9,10},{10,... | collective-permute-start | bytes 196616 | tf_op jit(solution)/shard_map/ppermute | solution.py:346

commit v8 on v6

--- a/solution.py
+++ b/solution.py
@@ -10,6 +10,7 @@
 HD = 128
 EPS = 1e-06
 CHUNK = 16
+UNROLL = 4
 COLUMNS = 512
 SLOTS = 3
 TAIL = 16
@@ -20,26 +21,33 @@
 ANY = pl.BlockSpec(memory_space=pl.ANY)
 
 
-def normalize_block(latents_ref, modulation_ref, normed_ref, start, block_rows):
+def normalize_block(latents_ref, gain_ref, shift_ref, normed_ref, start, block_rows):
     def one_chunk(c, carry):
         at = pl.multiple_of(start + c * CHUNK, CHUNK)
         floats = latents_ref[pl.ds(at, CHUNK), :].astype(jnp.float32)
         center = floats - jnp.mean(floats, axis=-1, keepdims=True)
         spread = jnp.mean(center * center, axis=-1, keepdims=True)
         normed_ref[pl.ds(at, CHUNK), :] = (
-            center * lax.rsqrt(spread + EPS) * (1.0 + modulation_ref[1:2, :])
-            + modulation_ref[0:1, :]
+            center * lax.rsqrt(spread + EPS) * gain_ref[...] + shift_ref[...]
         ).astype(jnp.bfloat16)
         return carry
 
-    lax.fori_loop(0, block_rows // CHUNK, one_chunk, 0, unroll=4)
+    lax.fori_loop(0, block_rows // CHUNK, one_chunk, 0, unroll=UNROLL)
 
 
 def query_kernel(n_frame, worker_in, latents_in, modulation_in, weight_in, *rest):
     outs, normed_out = rest[:n_frame], rest[n_frame]
-    worker_ref, latents_ref, modulation_ref, weight_ref, normed_ref, queries_ref, sems = rest[
-        n_frame + 1 :
-    ]
+    (
+        worker_ref,
+        latents_ref,
+        modulation_ref,
+        weight_ref,
+        normed_ref,
+        queries_ref,
+        gain_ref,
+        shift_ref,
+        sems,
+    ) = rest[n_frame + 1 :]
     n_local = worker_ref.shape[0]
     block_rows = latents_ref.shape[0] // n_local
     frame = lax.axis_index("frame")
@@ -65,12 +73,16 @@
         outs[s][...] = jnp.zeros_like(outs[s])
     for copy in first:
         copy.wait()
+    gain_ref[...] = jnp.broadcast_to(1.0 + modulation_ref[1:2, :], gain_ref.shape)
+    shift_ref[...] = jnp.broadcast_to(modulation_ref[0:1, :], shift_ref.shape)
     for j in range(n_local):
         each[j].wait()
 
         @pl.when(worker_ref[j] >= 0)
         def _():
-            normalize_block(latents_ref, modulation_ref, normed_ref, j * block_rows, block_rows)
+            normalize_block(
+                latents_ref, gain_ref, shift_ref, normed_ref, j * block_rows, block_rows
+            )
             back[j].start()
 
     weight.wait()
@@ -360,6 +372,8 @@
             pltpu.VMEM(query_weight.shape, half),
             pltpu.VMEM(latents.shape, half),
             pltpu.VMEM((tokens, width), half),
+            pltpu.VMEM((CHUNK, model), jnp.float32),
+            pltpu.VMEM((CHUNK, model), jnp.float32),
             pltpu.SemaphoreType.DMA((3 + 2 * n_local,)),
         ],
         compiler_params=params(60),

time: 49.5 us -> 49.8 us (level)
  waiting for transfers between devices: 13.9 us -> 15.4 us
  starting transfers between devices: 23.3 us -> 22.1 us
    ppermute x12, waiting for transfers between devices: 10.8 us -> 12.3 us  [along_frame(): return lax.ppermute(x, 'frame', [(i, i ^ s) for i in range(n_frame)])]
    ppermute x12, starting transfers between devices: 18.3 us -> 17.1 us  [along_frame(): return lax.ppermute(x, 'frame', [(i, i ^ s) for i in range(n_frame)])]
  transfers between devices with their start and end apart: 18 -> 18, of which waited for: 9 -> 10; matrix products, arithmetic and copies ran while one was open for 0% -> 0% of each run, Pallas kernels for 21% -> 21%
where the time goes in v8:
time: 49.8 us; the launch traced here: 49 us
  starting transfers between devices  22.1 us (44%)
  waiting for transfers between devices  15.4 us (31%)
  Pallas kernels  11.4 us (23%)
    ppermute x12, starting transfers between devices, along_frame(): return lax.ppermute(x, 'frame', [(i, i ^ s) for i in range(n_frame)])  17.1 us
    ppermute x12, waiting for transfers between devices, along_frame(): return lax.ppermute(x, 'frame', [(i, i ^ s) for i in range(n_frame)])  12.3 us
    ppermute x3, waiting for transfers between devices, in_frame(): return lax.ppermute(x, ('head', 'rep'), pairs)  3.13 us
    pallas_call x1, Pallas kernels, per_device(): pl.pallas_call(functools.partial(query_kernel, n_frame), out_shape=[jax.S...  3.07 us
    ppermute x1, starting transfers between devices, along_head(): lax.ppermute(x, 'head', [(i, (i + shift) % n_head) for i in range(n_head)])  2.94 us
    pallas_call x1, Pallas kernels, per_device(): pl.pallas_call(functools.partial(value_kernel, n_frame, n_head, n_rep), o...  2.36 us
    pallas_call x1, Pallas kernels, per_device(): pl.pallas_call(key_kernel, out_shape=jax.ShapeDtypeStruct((tokens, width)...  2.28 us
    ppermute x3, starting transfers between devices, in_frame(): return lax.ppermute(x, ('head', 'rep'), pairs)  1.93 us
  transfers between devices with their start and end apart: 18, of which 10 were waited for; matrix products, arithmetic and copies ran while one was open for 0% of the time, Pallas kernels for 21%

profile of v8, /device:TPU:0, one launch (start us, length us, event | category | flops | bytes accessed | tf_op | source)
XLA Modules:
  0.0 49.0 jit_solution(10766389883228385603)
XLA Ops:
  0.0 2.9 %collective-permute-start.12 = (bf16[256,1536]{1,0:T(8,128)(2,1)}, bf16[256,1536]{1,0:T(8,128)(2,1)S(1)}, u32[]{:S(2)}, u32[]{:S(2)}) collective-permute-start(bf16[256,1536]{1,0:T(8,128)(2,1)} %refs_2_.1), channel_id=1, source_target_pairs={{0,2},{2,0},{1,3},{3,1},{4,6},{6,4},{5,7},{7,5},{8,10},{10,8},{9,1... | collective-permute-start | bytes 2359304 | tf_op jit(solution)/shard_map/ppermute | solution.py:347
  2.9 3.1 %queries.1 = (bf16[128,256]{1,0:T(8,128)(2,1)}, bf16[128,256]{1,0:T(8,128)(2,1)}, bf16[128,256]{1,0:T(8,128)(2,1)}, bf16[128,256]{1,0:T(8,128)(2,1)}, bf16[512,1536]{1,0:T(8,128)(2,1)}) custom-call(s32[4]{0:T(128)} %worker_in.5, bf16[512,1536]{1,0:T(8,128)(2,1)} %latents_in.1, f32[3,1536]{1,0:T(4,128)} %modulation_ref.1, bf16[1536,256]{1,0:T(8,128)(2,1)} %weight_in.3), custom_call_target="tpu_custom_call" | custom-call | flops 402653184 | bytes 2359296 | tf_op jit(solution)/shard_map/queries/pallas_call | solution.py:362
  6.0 3.7 %collective-permute-start = (bf16[128,256]{1,0:T(8,128)(2,1)}, bf16[128,256]{1,0:T(8,128)(2,1)S(1)}, u32[]{:S(2)}, u32[]{:S(2)}) collective-permute-start(bf16[128,256]{1,0:T(8,128)(2,1)} %get-tuple-element.21), channel_id=1, source_target_pairs={{0,12},{4,8},{8,4},{12,0},{1,13},{5,9},{9,5},{13,1},{2,14},{6,10},... | collective-permute-start | bytes 196616 | tf_op jit(solution)/shard_map/ppermute | solution.py:344
  9.7 0.5 %collective-permute-start.1 = (bf16[128,256]{1,0:T(8,128)(2,1)}, bf16[128,256]{1,0:T(8,128)(2,1)S(1)}, u32[]{:S(2)}, u32[]{:S(2)}) collective-permute-start(bf16[128,256]{1,0:T(8,128)(2,1)} %get-tuple-element.22), channel_id=1, source_target_pairs={{0,8},{4,12},{8,0},{12,4},{1,9},{5,13},{9,1},{13,5},{2,10},{6,14},... | collective-permute-start | bytes 196616 | tf_op jit(solution)/shard_map/ppermute | solution.py:344
  10.2 0.5 collective-permute-start.2
  10.7 2.3 %keys.1.refs_4_.refs_1_.refs_3_ = bf16[512,256]{1,0:T(8,128)(2,1)S(1)} custom-call(s32[4]{0:T(128)S(1)} %copy-done.5, bf16[512,1536]{1,0:T(8,128)(2,1)} %get-tuple-element.24.normed_in, bf16[1536,256]{1,0:T(8,128)(2,1)} %weight_in.4, bf16[512,256]{1,0:T(8,128)(2,1)S(1)} %copy-done.1), custom_call_target="tpu_custom_call" | custom-call | flops 402653184 | bytes 4718592 | tf_op jit(solution)/shard_map/keys/pallas_call | solution.py:385
  13.0 2.9 %collective-permute-done.1.refs_2_ = bf16[128,256]{1,0:T(8,128)(2,1)S(1)} collective-permute-done((bf16[128,256]{1,0:T(8,128)(2,1)}, bf16[128,256]{1,0:T(8,128)(2,1)S(1)}, u32[]{:S(2)}, u32[]{:S(2)}) %collective-permute-start.1) | collective-permute-done | bytes 65568 | tf_op jit(solution)/shard_map/ppermute | solution.py:344
  16.0 3.1 %collective-permute-start.3 = (bf16[128,256]{1,0:T(8,128)(2,1)S(1)}, bf16[128,256]{1,0:T(8,128)(2,1)S(1)}, u32[]{:S(2)}, u32[]{:S(2)}) collective-permute-start(bf16[128,256]{1,0:T(8,128)(2,1)S(1)} %collect.1._.refs_0_), channel_id=1, source_target_pairs={{0,12},{4,8},{8,4},{12,0},{1,13},{5,9},{9,5},{13,1},{2,14},{6,10},... | collective-permute-start | bytes 196616 | tf_op jit(solution)/shard_map/ppermute | solution.py:344
  19.1 1.3 %collective-permute-start.5 = (bf16[128,256]{1,0:T(8,128)(2,1)S(1)}, bf16[128,256]{1,0:T(8,128)(2,1)S(1)}, u32[]{:S(2)}, u32[]{:S(2)}) collective-permute-start(bf16[128,256]{1,0:T(8,128)(2,1)S(1)} %collect.1._.refs_0_), channel_id=1, source_target_pairs={{0,4},{4,0},{8,12},{12,8},{1,5},{5,1},{9,13},{13,9},{2,6},{6,2},{1... | collective-permute-start | bytes 196616 | tf_op jit(solution)/shard_map/ppermute | solution.py:344
  20.4 2.4 %values.1 = (bf16[256,512]{1,0:T(8,128)(2,1)S(1)}, f32[16,128]{1,0:T(8,128)S(1)}) custom-call(s32[4]{0:T(128)S(1)} %copy-done.5, bf16[512,1536]{1,0:T(8,128)(2,1)} %get-tuple-element.24.normed_in, bf16[1536,256]{1,0:T(8,128)(2,1)} %weight_in.5, bf16[512,256]{1,0:T(8,128)(2,1)S(1)} %copy-done.2, bf16[128,256]{1,0:T(8,128)(2,1)S(1)} %collect.1._.refs_0_), custom_call_target="tpu_custom_call" | custom-call | flops 402653184 | bytes 4718592 | tf_op jit(solution)/shard_map/values/pallas_call | solution.py:411
  22.8 0.7 %attend.2.refs_5_.refs_0_ = bf16[272,128]{1,0:T(8,128)(2,1)S(1)} custom-call(bf16[128,256]{1,0:T(8,128)(2,1)S(1)} %collect.1._.refs_0_, bf16[512,256]{1,0:T(8,128)(2,1)S(1)} %keys.1.refs_4_.refs_1_.refs_3_, bf16[256,512]{1,0:T(8,128)(2,1)S(1)} %get-tuple-element.25.refs_2_.refs_4_), custom_call_target="tpu_custom_call" | custom-call | flops 67108864 | bytes 2621440 | tf_op jit(solution)/shard_map/attend/pallas_call | solution.py:433
  23.6 0.9 %collective-permute-done.4.refs_1_ = bf16[128,256]{1,0:T(8,128)(2,1)S(1)} collective-permute-done((bf16[128,256]{1,0:T(8,128)(2,1)S(1)}, bf16[128,256]{1,0:T(8,128)(2,1)S(1)}, u32[]{:S(2)}, u32[]{:S(2)}) %collective-permute-start.4) | collective-permute-done | bytes 65568 | tf_op jit(solution)/shard_map/ppermute | solution.py:344
  24.5 0.3 collective-permute-done.5.refs_2_
  24.8 1.1 %attend.3 = (bf16[272,128]{1,0:T(8,128)(2,1)S(1)}, bf16[272,128]{1,0:T(8,128)(2,1)S(1)}, bf16[272,128]{1,0:T(8,128)(2,1)S(1)}) custom-call(bf16[128,256]{1,0:T(8,128)(2,1)S(1)} %collective-permute-done.3.refs_0_, bf16[128,256]{1,0:T(8,128)(2,1)S(1)} %collective-permute-done.4.refs_1_, bf16[128,256]{1,0:T(8,128)(2,1)S(1)} %collective-permute-done.5.refs_2_, ...), custom_call_target="tpu_custom_call" | custom-call | flops 201326592 | bytes 2621440 | tf_op jit(solution)/shard_map/attend/pallas_call | solution.py:433
  25.9 2.1 %collective-permute-start.6 = (bf16[272,128]{1,0:T(8,128)(2,1)S(1)}, bf16[272,128]{1,0:T(8,128)(2,1)S(1)}, u32[]{:S(2)}, u32[]{:S(2)}) collective-permute-start(bf16[272,128]{1,0:T(8,128)(2,1)S(1)} %get-tuple-element.26), channel_id=1, source_target_pairs={{0,12},{4,8},{8,4},{12,0},{1,13},{5,9},{9,5},{13,1},{2,14},{6,10},... | collective-permute-start | bytes 208904 | tf_op jit(solution)/shard_map/ppermute | solution.py:344
  28.1 2.3 %collective-permute-start.8 = (bf16[272,128]{1,0:T(8,128)(2,1)S(1)}, bf16[272,128]{1,0:T(8,128)(2,1)S(1)}, u32[]{:S(2)}, u32[]{:S(2)}) collective-permute-start(bf16[272,128]{1,0:T(8,128)(2,1)S(1)} %get-tuple-element.28), channel_id=1, source_target_pairs={{0,4},{4,0},{8,12},{12,8},{1,5},{5,1},{9,13},{13,9},{2,6},{6,2},{1... | collective-permute-start | bytes 208904 | tf_op jit(solution)/shard_map/ppermute | solution.py:344
  30.3 2.1 %collective-permute-done.6.refs_1_ = bf16[272,128]{1,0:T(8,128)(2,1)S(1)} collective-permute-done((bf16[272,128]{1,0:T(8,128)(2,1)S(1)}, bf16[272,128]{1,0:T(8,128)(2,1)S(1)}, u32[]{:S(2)}, u32[]{:S(2)}) %collective-permute-start.6) | collective-permute-done | bytes 69664 | tf_op jit(solution)/shard_map/ppermute | solution.py:344
  32.4 1.9 %collective-permute-done.7.refs_2_ = bf16[272,128]{1,0:T(8,128)(2,1)S(1)} collective-permute-done((bf16[272,128]{1,0:T(8,128)(2,1)S(1)}, bf16[272,128]{1,0:T(8,128)(2,1)S(1)}, u32[]{:S(2)}, u32[]{:S(2)}) %collective-permute-start.7) | collective-permute-done | bytes 69664 | tf_op jit(solution)/shard_map/ppermute | solution.py:344
  34.5 0.9 %collective-permute-start.10 = (bf16[128,256]{1,0:T(8,128)(2,1)S(1)}, bf16[128,256]{1,0:T(8,128)(2,1)S(1)}, u32[]{:S(2)}, u32[]{:S(2)}) collective-permute-start(bf16[128,256]{1,0:T(8,128)(2,1)S(1)} %combine.1.refs_0_), channel_id=1, source_target_pairs={{0,8},{4,12},{8,0},{12,4},{1,9},{5,13},{9,1},{13,5},{2,10},{6,14},... | collective-permute-start | bytes 196616 | tf_op jit(solution)/shard_map/ppermute | solution.py:344
  35.4 1.8 %collective-permute-start.11 = (bf16[128,256]{1,0:T(8,128)(2,1)S(1)}, bf16[128,256]{1,0:T(8,128)(2,1)S(1)}, u32[]{:S(2)}, u32[]{:S(2)}) collective-permute-start(bf16[128,256]{1,0:T(8,128)(2,1)S(1)} %combine.1.refs_0_), channel_id=1, source_target_pairs={{0,12},{4,8},{8,4},{12,0},{1,13},{5,9},{9,5},{13,1},{2,14},{6,10},... | collective-permute-start | bytes 196616 | tf_op jit(solution)/shard_map/ppermute | solution.py:344
  37.2 0.8 %collective-permute-start.9 = (bf16[128,256]{1,0:T(8,128)(2,1)S(1)}, bf16[128,256]{1,0:T(8,128)(2,1)S(1)}, u32[]{:S(2)}, u32[]{:S(2)}) collective-permute-start(bf16[128,256]{1,0:T(8,128)(2,1)S(1)} %combine.1.refs_0_), channel_id=1, source_target_pairs={{0,4},{4,0},{8,12},{12,8},{1,5},{5,1},{9,13},{13,9},{2,6},{6,2},{1... | collective-permute-start | bytes 196616 | tf_op jit(solution)/shard_map/ppermute | solution.py:344
  38.0 2.6 %collective-permute-done.10.refs_2_ = bf16[128,256]{1,0:T(8,128)(2,1)S(1)} collective-permute-done((bf16[128,256]{1,0:T(8,128)(2,1)S(1)}, bf16[128,256]{1,0:T(8,128)(2,1)S(1)}, u32[]{:S(2)}, u32[]{:S(2)}) %collective-permute-start.10) | collective-permute-done | bytes 65568 | tf_op jit(solution)/shard_map/ppermute | solution.py:344
  40.6 1.0 %collective-permute-done.11.refs_3_ = bf16[128,256]{1,0:T(8,128)(2,1)S(1)} collective-permute-done((bf16[128,256]{1,0:T(8,128)(2,1)S(1)}, bf16[128,256]{1,0:T(8,128)(2,1)S(1)}, u32[]{:S(2)}, u32[]{:S(2)}) %collective-permute-start.11) | collective-permute-done | bytes 65568 | tf_op jit(solution)/shard_map/ppermute | solution.py:344
  41.7 0.5 %collective-permute-done.9.refs_1_ = bf16[128,256]{1,0:T(8,128)(2,1)S(1)} collective-permute-done((bf16[128,256]{1,0:T(8,128)(2,1)S(1)}, bf16[128,256]{1,0:T(8,128)(2,1)S(1)}, u32[]{:S(2)}, u32[]{:S(2)}) %collective-permute-start.9) | collective-permute-done | bytes 65568 | tf_op jit(solution)/shard_map/ppermute | solution.py:344
  42.2 0.2 select.1
  42.5 0.5 %collective-permute-start.13 = (bf16[128,256]{1,0:T(8,128)(2,1)S(1)}, bf16[128,256]{1,0:T(8,128)(2,1)S(1)}, u32[]{:S(2)}, u32[]{:S(2)}) collective-permute-start(bf16[128,256]{1,0:T(8,128)(2,1)S(1)} %get-tuple-element.31), channel_id=1, source_target_pairs={{0,1},{1,0},{2,3},{3,2},{4,5},{5,4},{6,7},{7,6},{8,9},{9,8},{10,11... | collective-permute-start | bytes 196616 | tf_op jit(solution)/shard_map/ppermute | solution.py:358
  43.0 0.5 %collective-permute-start.15 = (bf16[128,256]{1,0:T(8,128)(2,1)S(1)}, bf16[128,256]{1,0:T(8,128)(2,1)S(1)}, u32[]{:S(2)}, u32[]{:S(2)}) collective-permute-start(bf16[128,256]{1,0:T(8,128)(2,1)S(1)} %get-tuple-element.32), channel_id=1, source_target_pairs={{0,2},{1,3},{2,0},{3,1},{4,6},{5,7},{6,4},{7,5},{8,10},{9,11},{10,... | collective-permute-start | bytes 196616 | tf_op jit(solution)/shard_map/ppermute | solution.py:358
  43.5 0.9 %collective-permute-start.16 = (bf16[128,256]{1,0:T(8,128)(2,1)S(1)}, bf16[128,256]{1,0:T(8,128)(2,1)S(1)}, u32[]{:S(2)}, u32[]{:S(2)}) collective-permute-start(bf16[128,256]{1,0:T(8,128)(2,1)S(1)} %get-tuple-element.33), channel_id=1, source_target_pairs={{0,3},{1,2},{2,1},{3,0},{4,7},{5,6},{6,5},{7,4},{8,11},{9,10},{10,... | collective-permute-start | bytes 196616 | tf_op jit(solution)/shard_map/ppermute | solution.py:358
  44.4 0.4 collective-permute-done.13.refs_1_
  44.8 0.4 project_near.1.near_ref
  45.2 2.7 %collective-permute-done.15.refs_0_ = bf16[128,256]{1,0:T(8,128)(2,1)S(1)} collective-permute-done((bf16[128,256]{1,0:T(8,128)(2,1)S(1)}, bf16[128,256]{1,0:T(8,128)(2,1)S(1)}, u32[]{:S(2)}, u32[]{:S(2)}) %collective-permute-start.15) | collective-permute-done | bytes 65568 | tf_op jit(solution)/shard_map/ppermute | solution.py:358
  47.9 1.1 %project.1 = f32[128,1536]{1,0:T(8,128)} custom-call(f32[3,1536]{1,0:T(4,128)S(1)} %copy-done.3, f32[128,1536]{1,0:T(8,128)S(1)} %project_near.1.near_ref, bf16[128,256]{1,0:T(8,128)(2,1)S(1)} %collective-permute-done.15.refs_0_, bf16[128,256]{1,0:T(8,128)(2,1)S(1)} %collective-permute-done.16.refs_1_, bf16[256,1536]{1,0:T(8,128)(2,1)S(1)} %get-tuple-element.34.refs_2_, ...), custom_call_target="tpu_custom_call" | custom-call | flops 201326592 | bytes 3145728 | tf_op jit(solution)/shard_map/project/pallas_call | solution.py:492
  (26 shorter events, 0.4 us)
Async XLA Ops:
  0.0 10.7 %copy-start.5 = (s32[4]{0:T(128)S(1)}, s32[4]{0:T(128)}, u32[]{:S(2)}) copy-start(s32[4]{0:T(128)} %worker_in.5) | copy-start | bytes 52
  0.0 10.7 %copy-start.1 = (bf16[512,256]{1,0:T(8,128)(2,1)S(1)}, bf16[512,256]{1,0:T(8,128)(2,1)}, u32[]{:S(2)}) copy-start(bf16[512,256]{1,0:T(8,128)(2,1)} %cache_in.2) | copy-start | bytes 786436
  0.0 42.2 %collective-permute-start.12 = (bf16[256,1536]{1,0:T(8,128)(2,1)}, bf16[256,1536]{1,0:T(8,128)(2,1)S(1)}, u32[]{:S(2)}, u32[]{:S(2)}) collective-permute-start(bf16[256,1536]{1,0:T(8,128)(2,1)} %refs_2_.1), channel_id=1, source_target_pairs={{0,2},{2,0},{1,3},{3,1},{4,6},{6,4},{5,7},{7,5},{8,10},{10,8},{9,1... | collective-permute-start | bytes 2359304 | tf_op jit(solution)/shard_map/ppermute | solution.py:347
  6.0 9.9 %copy-start.4 = (bf16[128,256]{1,0:T(8,128)(2,1)S(1)}, bf16[128,256]{1,0:T(8,128)(2,1)}, u32[]{:S(2)}) copy-start(bf16[128,256]{1,0:T(8,128)(2,1)} %get-tuple-element.20.refs_0_) | copy-start | bytes 196612
  6.0 7.0 %collective-permute-start = (bf16[128,256]{1,0:T(8,128)(2,1)}, bf16[128,256]{1,0:T(8,128)(2,1)S(1)}, u32[]{:S(2)}, u32[]{:S(2)}) collective-permute-start(bf16[128,256]{1,0:T(8,128)(2,1)} %get-tuple-element.21), channel_id=1, source_target_pairs={{0,12},{4,8},{8,4},{12,0},{1,13},{5,9},{9,5},{13,1},{2,14},{6,10},... | collective-permute-start | bytes 196616 | tf_op jit(solution)/shard_map/ppermute | solution.py:344
  9.7 6.2 %collective-permute-start.1 = (bf16[128,256]{1,0:T(8,128)(2,1)}, bf16[128,256]{1,0:T(8,128)(2,1)S(1)}, u32[]{:S(2)}, u32[]{:S(2)}) collective-permute-start(bf16[128,256]{1,0:T(8,128)(2,1)} %get-tuple-element.22), channel_id=1, source_target_pairs={{0,8},{4,12},{8,0},{12,4},{1,9},{5,13},{9,1},{13,5},{2,10},{6,14},... | collective-permute-start | bytes 196616 | tf_op jit(solution)/shard_map/ppermute | solution.py:344
  10.2 5.7 %collective-permute-start.2 = (bf16[128,256]{1,0:T(8,128)(2,1)}, bf16[128,256]{1,0:T(8,128)(2,1)S(1)}, u32[]{:S(2)}, u32[]{:S(2)}) collective-permute-start(bf16[128,256]{1,0:T(8,128)(2,1)} %get-tuple-element.23), channel_id=1, source_target_pairs={{0,4},{4,0},{8,12},{12,8},{1,5},{5,1},{9,13},{13,9},{2,6},{6,2},{1... | collective-permute-start | bytes 196616 | tf_op jit(solution)/shard_map/ppermute | solution.py:344
  10.7 9.8 %copy-start.2 = (bf16[512,256]{1,0:T(8,128)(2,1)S(1)}, bf16[512,256]{1,0:T(8,128)(2,1)}, u32[]{:S(2)}) copy-start(bf16[512,256]{1,0:T(8,128)(2,1)} %cache_in.3) | copy-start | bytes 786436
  16.0 22.1 %copy-start = (bf16[256,1536]{1,0:T(8,128)(2,1)S(1)}, bf16[256,1536]{1,0:T(8,128)(2,1)}, u32[]{:S(2)}) copy-start(bf16[256,1536]{1,0:T(8,128)(2,1)} %refs_2_.1) | copy-start | bytes 2359300
  16.0 7.6 %collective-permute-start.3 = (bf16[128,256]{1,0:T(8,128)(2,1)S(1)}, bf16[128,256]{1,0:T(8,128)(2,1)S(1)}, u32[]{:S(2)}, u32[]{:S(2)}) collective-permute-start(bf16[128,256]{1,0:T(8,128)(2,1)S(1)} %collect.1._.refs_0_), channel_id=1, source_target_pairs={{0,12},{4,8},{8,4},{12,0},{1,13},{5,9},{9,5},{13,1},{2,14},{6,10},... | collective-permute-start | bytes 196616 | tf_op jit(solution)/shard_map/ppermute | solution.py:344
  19.1 5.3 %collective-permute-start.4 = (bf16[128,256]{1,0:T(8,128)(2,1)S(1)}, bf16[128,256]{1,0:T(8,128)(2,1)S(1)}, u32[]{:S(2)}, u32[]{:S(2)}) collective-permute-start(bf16[128,256]{1,0:T(8,128)(2,1)S(1)} %collect.1._.refs_0_), channel_id=1, source_target_pairs={{0,8},{4,12},{8,0},{12,4},{1,9},{5,13},{9,1},{13,5},{2,10},{6,14},... | collective-permute-start | bytes 196616 | tf_op jit(solution)/shard_map/ppermute | solution.py:344
  19.1 5.7 %collective-permute-start.5 = (bf16[128,256]{1,0:T(8,128)(2,1)S(1)}, bf16[128,256]{1,0:T(8,128)(2,1)S(1)}, u32[]{:S(2)}, u32[]{:S(2)}) collective-permute-start(bf16[128,256]{1,0:T(8,128)(2,1)S(1)} %collect.1._.refs_0_), channel_id=1, source_target_pairs={{0,4},{4,0},{8,12},{12,8},{1,5},{5,1},{9,13},{13,9},{2,6},{6,2},{1... | collective-permute-start | bytes 196616 | tf_op jit(solution)/shard_map/ppermute | solution.py:344
  25.9 6.5 %collective-permute-start.6 = (bf16[272,128]{1,0:T(8,128)(2,1)S(1)}, bf16[272,128]{1,0:T(8,128)(2,1)S(1)}, u32[]{:S(2)}, u32[]{:S(2)}) collective-permute-start(bf16[272,128]{1,0:T(8,128)(2,1)S(1)} %get-tuple-element.26), channel_id=1, source_target_pairs={{0,12},{4,8},{8,4},{12,0},{1,13},{5,9},{9,5},{13,1},{2,14},{6,10},... | collective-permute-start | bytes 208904 | tf_op jit(solution)/shard_map/ppermute | solution.py:344
  28.0 6.3 %collective-permute-start.7 = (bf16[272,128]{1,0:T(8,128)(2,1)S(1)}, bf16[272,128]{1,0:T(8,128)(2,1)S(1)}, u32[]{:S(2)}, u32[]{:S(2)}) collective-permute-start(bf16[272,128]{1,0:T(8,128)(2,1)S(1)} %get-tuple-element.27), channel_id=1, source_target_pairs={{0,8},{4,12},{8,0},{12,4},{1,9},{5,13},{9,1},{13,5},{2,10},{6,14},... | collective-permute-start | bytes 208904 | tf_op jit(solution)/shard_map/ppermute | solution.py:344
  28.1 6.3 %collective-permute-start.8 = (bf16[272,128]{1,0:T(8,128)(2,1)S(1)}, bf16[272,128]{1,0:T(8,128)(2,1)S(1)}, u32[]{:S(2)}, u32[]{:S(2)}) collective-permute-start(bf16[272,128]{1,0:T(8,128)(2,1)S(1)} %get-tuple-element.28), channel_id=1, source_target_pairs={{0,4},{4,0},{8,12},{12,8},{1,5},{5,1},{9,13},{13,9},{2,6},{6,2},{1... | collective-permute-start | bytes 208904 | tf_op jit(solution)/shard_map/ppermute | solution.py:344
  34.5 6.1 %collective-permute-start.10 = (bf16[128,256]{1,0:T(8,128)(2,1)S(1)}, bf16[128,256]{1,0:T(8,128)(2,1)S(1)}, u32[]{:S(2)}, u32[]{:S(2)}) collective-permute-start(bf16[128,256]{1,0:T(8,128)(2,1)S(1)} %combine.1.refs_0_), channel_id=1, source_target_pairs={{0,8},{4,12},{8,0},{12,4},{1,9},{5,13},{9,1},{13,5},{2,10},{6,14},... | collective-permute-start | bytes 196616 | tf_op jit(solution)/shard_map/ppermute | solution.py:344
  35.4 6.2 %collective-permute-start.11 = (bf16[128,256]{1,0:T(8,128)(2,1)S(1)}, bf16[128,256]{1,0:T(8,128)(2,1)S(1)}, u32[]{:S(2)}, u32[]{:S(2)}) collective-permute-start(bf16[128,256]{1,0:T(8,128)(2,1)S(1)} %combine.1.refs_0_), channel_id=1, source_target_pairs={{0,12},{4,8},{8,4},{12,0},{1,13},{5,9},{9,5},{13,1},{2,14},{6,10},... | collective-permute-start | bytes 196616 | tf_op jit(solution)/shard_map/ppermute | solution.py:344
  37.2 5.0 %collective-permute-start.9 = (bf16[128,256]{1,0:T(8,128)(2,1)S(1)}, bf16[128,256]{1,0:T(8,128)(2,1)S(1)}, u32[]{:S(2)}, u32[]{:S(2)}) collective-permute-start(bf16[128,256]{1,0:T(8,128)(2,1)S(1)} %combine.1.refs_0_), channel_id=1, source_target_pairs={{0,4},{4,0},{8,12},{12,8},{1,5},{5,1},{9,13},{13,9},{2,6},{6,2},{1... | collective-permute-start | bytes 196616 | tf_op jit(solution)/shard_map/ppermute | solution.py:344
  38.0 6.3 %collective-permute-start.14 = (bf16[256,1536]{1,0:T(8,128)(2,1)S(1)}, bf16[256,1536]{1,0:T(8,128)(2,1)S(1)}, u32[]{:S(2)}, u32[]{:S(2)}) collective-permute-start(bf16[256,1536]{1,0:T(8,128)(2,1)S(1)} %copy-done), channel_id=1, source_target_pairs={{0,1},{1,0},{2,3},{3,2},{4,5},{5,4},{6,7},{7,6},{8,9},{9,8},{10,11... | collective-permute-start | bytes 2359304 | tf_op jit(solution)/shard_map/ppermute | solution.py:350
  42.2 5.7 %copy-start.3 = (f32[3,1536]{1,0:T(4,128)S(1)}, f32[3,1536]{1,0:T(4,128)}, u32[]{:S(2)}) copy-start(f32[3,1536]{1,0:T(4,128)} %modulation_ref.1) | copy-start | bytes 55300
  42.4 5.5 %collective-permute-start.17 = (bf16[256,1536]{1,0:T(8,128)(2,1)S(1)}, bf16[256,1536]{1,0:T(8,128)(2,1)S(1)}, u32[]{:S(2)}, u32[]{:S(2)}) collective-permute-start(bf16[256,1536]{1,0:T(8,128)(2,1)S(1)} %get-tuple-element.34.refs_2_), channel_id=1, source_target_pairs={{0,1},{1,0},{2,3},{3,2},{4,5},{5,4},{6,7},{7,6},{8,9},{9,8},{10,11... | collective-permute-start | bytes 2359304 | tf_op jit(solution)/shard_map/ppermute | solution.py:350
  42.5 2.4 %collective-permute-start.13 = (bf16[128,256]{1,0:T(8,128)(2,1)S(1)}, bf16[128,256]{1,0:T(8,128)(2,1)S(1)}, u32[]{:S(2)}, u32[]{:S(2)}) collective-permute-start(bf16[128,256]{1,0:T(8,128)(2,1)S(1)} %get-tuple-element.31), channel_id=1, source_target_pairs={{0,1},{1,0},{2,3},{3,2},{4,5},{5,4},{6,7},{7,6},{8,9},{9,8},{10,11... | collective-permute-start | bytes 196616 | tf_op jit(solution)/shard_map/ppermute | solution.py:358
  43.0 4.9 %collective-permute-start.15 = (bf16[128,256]{1,0:T(8,128)(2,1)S(1)}, bf16[128,256]{1,0:T(8,128)(2,1)S(1)}, u32[]{:S(2)}, u32[]{:S(2)}) collective-permute-start(bf16[128,256]{1,0:T(8,128)(2,1)S(1)} %get-tuple-element.32), channel_id=1, source_target_pairs={{0,2},{1,3},{2,0},{3,1},{4,6},{5,7},{6,4},{7,5},{8,10},{9,11},{10,... | collective-permute-start | bytes 196616 | tf_op jit(solution)/shard_map/ppermute | solution.py:358
  43.5 4.4 %collective-permute-start.16 = (bf16[128,256]{1,0:T(8,128)(2,1)S(1)}, bf16[128,256]{1,0:T(8,128)(2,1)S(1)}, u32[]{:S(2)}, u32[]{:S(2)}) collective-permute-start(bf16[128,256]{1,0:T(8,128)(2,1)S(1)} %get-tuple-element.33), channel_id=1, source_target_pairs={{0,3},{1,2},{2,1},{3,0},{4,7},{5,6},{6,5},{7,4},{8,11},{9,10},{10,... | collective-permute-start | bytes 196616 | tf_op jit(solution)/shard_map/ppermute | solution.py:358

commit v9 on v8

--- a/solution.py
+++ b/solution.py
@@ -10,7 +10,7 @@
 HD = 128
 EPS = 1e-06
 CHUNK = 16
-UNROLL = 4
+UNROLL = 8
 COLUMNS = 512
 SLOTS = 3
 TAIL = 16

time: 49.8 us -> 48.3 us (0.970); the launches traced: 49 us -> 48.1 us
  waiting for transfers between devices: 15.4 us -> 14.3 us
    ppermute x12, waiting for transfers between devices: 12.3 us -> 11.2 us  [along_frame(): return lax.ppermute(x, 'frame', [(i, i ^ s) for i in range(n_frame)])]
where the time goes in v9:
time: 48.3 us; the launch traced here: 48.1 us
  starting transfers between devices  22.2 us (46%)
  waiting for transfers between devices  14.3 us (30%)
  Pallas kernels  11.4 us (24%)
    ppermute x12, starting transfers between devices, along_frame(): return lax.ppermute(x, 'frame', [(i, i ^ s) for i in range(n_frame)])  17.3 us
    ppermute x12, waiting for transfers between devices, along_frame(): return lax.ppermute(x, 'frame', [(i, i ^ s) for i in range(n_frame)])  11.2 us
    ppermute x3, waiting for transfers between devices, in_frame(): return lax.ppermute(x, ('head', 'rep'), pairs)  3.13 us
    pallas_call x1, Pallas kernels, per_device(): pl.pallas_call(functools.partial(query_kernel, n_frame), out_shape=[jax.S...  3.07 us
    ppermute x1, starting transfers between devices, along_head(): lax.ppermute(x, 'head', [(i, (i + shift) % n_head) for i in range(n_head)])  2.94 us
    pallas_call x1, Pallas kernels, per_device(): pl.pallas_call(functools.partial(value_kernel, n_frame, n_head, n_rep), o...  2.36 us
    pallas_call x1, Pallas kernels, per_device(): pl.pallas_call(key_kernel, out_shape=jax.ShapeDtypeStruct((tokens, width)...  2.28 us
    ppermute x3, starting transfers between devices, in_frame(): return lax.ppermute(x, ('head', 'rep'), pairs)  1.93 us
  transfers between devices with their start and end apart: 18, of which 10 were waited for; matrix products, arithmetic and copies ran while one was open for 0% of the time, Pallas kernels for 21%

profile of v9, /device:TPU:0, one launch (start us, length us, event | category | flops | bytes accessed | tf_op | source)
XLA Modules:
  0.0 48.1 jit_solution(8359269148777352980)
XLA Ops:
  0.0 2.9 %collective-permute-start.12 = (bf16[256,1536]{1,0:T(8,128)(2,1)}, bf16[256,1536]{1,0:T(8,128)(2,1)S(1)}, u32[]{:S(2)}, u32[]{:S(2)}) collective-permute-start(bf16[256,1536]{1,0:T(8,128)(2,1)} %refs_2_.1), channel_id=1, source_target_pairs={{0,2},{2,0},{1,3},{3,1},{4,6},{6,4},{5,7},{7,5},{8,10},{10,8},{9,1... | collective-permute-start | bytes 2359304 | tf_op jit(solution)/shard_map/ppermute | solution.py:347
  2.9 3.1 %queries.1 = (bf16[128,256]{1,0:T(8,128)(2,1)}, bf16[128,256]{1,0:T(8,128)(2,1)}, bf16[128,256]{1,0:T(8,128)(2,1)}, bf16[128,256]{1,0:T(8,128)(2,1)}, bf16[512,1536]{1,0:T(8,128)(2,1)}) custom-call(s32[4]{0:T(128)} %worker_in.5, bf16[512,1536]{1,0:T(8,128)(2,1)} %latents_in.1, f32[3,1536]{1,0:T(4,128)} %modulation_ref.1, bf16[1536,256]{1,0:T(8,128)(2,1)} %weight_in.3), custom_call_target="tpu_custom_call" | custom-call | flops 402653184 | bytes 2359296 | tf_op jit(solution)/shard_map/queries/pallas_call | solution.py:362
  6.0 3.7 %collective-permute-start = (bf16[128,256]{1,0:T(8,128)(2,1)}, bf16[128,256]{1,0:T(8,128)(2,1)S(1)}, u32[]{:S(2)}, u32[]{:S(2)}) collective-permute-start(bf16[128,256]{1,0:T(8,128)(2,1)} %get-tuple-element.21), channel_id=1, source_target_pairs={{0,12},{4,8},{8,4},{12,0},{1,13},{5,9},{9,5},{13,1},{2,14},{6,10},... | collective-permute-start | bytes 196616 | tf_op jit(solution)/shard_map/ppermute | solution.py:344
  9.8 0.6 %collective-permute-start.2 = (bf16[128,256]{1,0:T(8,128)(2,1)}, bf16[128,256]{1,0:T(8,128)(2,1)S(1)}, u32[]{:S(2)}, u32[]{:S(2)}) collective-permute-start(bf16[128,256]{1,0:T(8,128)(2,1)} %get-tuple-element.23), channel_id=1, source_target_pairs={{0,4},{4,0},{8,12},{12,8},{1,5},{5,1},{9,13},{13,9},{2,6},{6,2},{1... | collective-permute-start | bytes 196616 | tf_op jit(solution)/shard_map/ppermute | solution.py:344
  10.5 2.3 %keys.1.refs_4_.refs_1_.refs_3_ = bf16[512,256]{1,0:T(8,128)(2,1)S(1)} custom-call(s32[4]{0:T(128)S(1)} %copy-done.5, bf16[512,1536]{1,0:T(8,128)(2,1)} %get-tuple-element.24.normed_in, bf16[1536,256]{1,0:T(8,128)(2,1)} %weight_in.4, bf16[512,256]{1,0:T(8,128)(2,1)S(1)} %copy-done.1), custom_call_target="tpu_custom_call" | custom-call | flops 402653184 | bytes 4718592 | tf_op jit(solution)/shard_map/keys/pallas_call | solution.py:385
  12.8 0.4 collective-permute-done.refs_1_
  13.2 2.6 %collective-permute-done.1.refs_2_ = bf16[128,256]{1,0:T(8,128)(2,1)S(1)} collective-permute-done((bf16[128,256]{1,0:T(8,128)(2,1)}, bf16[128,256]{1,0:T(8,128)(2,1)S(1)}, u32[]{:S(2)}, u32[]{:S(2)}) %collective-permute-start.1) | collective-permute-done | bytes 65568 | tf_op jit(solution)/shard_map/ppermute | solution.py:344
  15.9 2.2 %collective-permute-start.3 = (bf16[128,256]{1,0:T(8,128)(2,1)S(1)}, bf16[128,256]{1,0:T(8,128)(2,1)S(1)}, u32[]{:S(2)}, u32[]{:S(2)}) collective-permute-start(bf16[128,256]{1,0:T(8,128)(2,1)S(1)} %collect.1._.refs_0_), channel_id=1, source_target_pairs={{0,12},{4,8},{8,4},{12,0},{1,13},{5,9},{9,5},{13,1},{2,14},{6,10},... | collective-permute-start | bytes 196616 | tf_op jit(solution)/shard_map/ppermute | solution.py:344
  18.1 2.2 %collective-permute-start.5 = (bf16[128,256]{1,0:T(8,128)(2,1)S(1)}, bf16[128,256]{1,0:T(8,128)(2,1)S(1)}, u32[]{:S(2)}, u32[]{:S(2)}) collective-permute-start(bf16[128,256]{1,0:T(8,128)(2,1)S(1)} %collect.1._.refs_0_), channel_id=1, source_target_pairs={{0,4},{4,0},{8,12},{12,8},{1,5},{5,1},{9,13},{13,9},{2,6},{6,2},{1... | collective-permute-start | bytes 196616 | tf_op jit(solution)/shard_map/ppermute | solution.py:344
  20.3 2.4 %values.1 = (bf16[256,512]{1,0:T(8,128)(2,1)S(1)}, f32[16,128]{1,0:T(8,128)S(1)}) custom-call(s32[4]{0:T(128)S(1)} %copy-done.5, bf16[512,1536]{1,0:T(8,128)(2,1)} %get-tuple-element.24.normed_in, bf16[1536,256]{1,0:T(8,128)(2,1)} %weight_in.5, bf16[512,256]{1,0:T(8,128)(2,1)S(1)} %copy-done.2, bf16[128,256]{1,0:T(8,128)(2,1)S(1)} %collect.1._.refs_0_), custom_call_target="tpu_custom_call" | custom-call | flops 402653184 | bytes 4718592 | tf_op jit(solution)/shard_map/values/pallas_call | solution.py:411
  22.7 0.7 %attend.2.refs_5_.refs_0_ = bf16[272,128]{1,0:T(8,128)(2,1)S(1)} custom-call(bf16[128,256]{1,0:T(8,128)(2,1)S(1)} %collect.1._.refs_0_, bf16[512,256]{1,0:T(8,128)(2,1)S(1)} %keys.1.refs_4_.refs_1_.refs_3_, bf16[256,512]{1,0:T(8,128)(2,1)S(1)} %get-tuple-element.25.refs_2_.refs_4_), custom_call_target="tpu_custom_call" | custom-call | flops 67108864 | bytes 2621440 | tf_op jit(solution)/shard_map/attend/pallas_call | solution.py:433
  23.4 0.6 %collective-permute-done.4.refs_1_ = bf16[128,256]{1,0:T(8,128)(2,1)S(1)} collective-permute-done((bf16[128,256]{1,0:T(8,128)(2,1)S(1)}, bf16[128,256]{1,0:T(8,128)(2,1)S(1)}, u32[]{:S(2)}, u32[]{:S(2)}) %collective-permute-start.4) | collective-permute-done | bytes 65568 | tf_op jit(solution)/shard_map/ppermute | solution.py:344
  24.1 1.1 %attend.3 = (bf16[272,128]{1,0:T(8,128)(2,1)S(1)}, bf16[272,128]{1,0:T(8,128)(2,1)S(1)}, bf16[272,128]{1,0:T(8,128)(2,1)S(1)}) custom-call(bf16[128,256]{1,0:T(8,128)(2,1)S(1)} %collective-permute-done.3.refs_0_, bf16[128,256]{1,0:T(8,128)(2,1)S(1)} %collective-permute-done.4.refs_1_, bf16[128,256]{1,0:T(8,128)(2,1)S(1)} %collective-permute-done.5.refs_2_, ...), custom_call_target="tpu_custom_call" | custom-call | flops 201326592 | bytes 2621440 | tf_op jit(solution)/shard_map/attend/pallas_call | solution.py:433
  25.2 1.8 %collective-permute-start.6 = (bf16[272,128]{1,0:T(8,128)(2,1)S(1)}, bf16[272,128]{1,0:T(8,128)(2,1)S(1)}, u32[]{:S(2)}, u32[]{:S(2)}) collective-permute-start(bf16[272,128]{1,0:T(8,128)(2,1)S(1)} %get-tuple-element.26), channel_id=1, source_target_pairs={{0,12},{4,8},{8,4},{12,0},{1,13},{5,9},{9,5},{13,1},{2,14},{6,10},... | collective-permute-start | bytes 208904 | tf_op jit(solution)/shard_map/ppermute | solution.py:344
  26.9 0.3 collective-permute-start.7
  27.2 2.4 %collective-permute-start.8 = (bf16[272,128]{1,0:T(8,128)(2,1)S(1)}, bf16[272,128]{1,0:T(8,128)(2,1)S(1)}, u32[]{:S(2)}, u32[]{:S(2)}) collective-permute-start(bf16[272,128]{1,0:T(8,128)(2,1)S(1)} %get-tuple-element.28), channel_id=1, source_target_pairs={{0,4},{4,0},{8,12},{12,8},{1,5},{5,1},{9,13},{13,9},{2,6},{6,2},{1... | collective-permute-start | bytes 208904 | tf_op jit(solution)/shard_map/ppermute | solution.py:344
  29.6 1.7 %collective-permute-done.6.refs_1_ = bf16[272,128]{1,0:T(8,128)(2,1)S(1)} collective-permute-done((bf16[272,128]{1,0:T(8,128)(2,1)S(1)}, bf16[272,128]{1,0:T(8,128)(2,1)S(1)}, u32[]{:S(2)}, u32[]{:S(2)}) %collective-permute-start.6) | collective-permute-done | bytes 69664 | tf_op jit(solution)/shard_map/ppermute | solution.py:344
  31.3 1.5 %collective-permute-done.7.refs_2_ = bf16[272,128]{1,0:T(8,128)(2,1)S(1)} collective-permute-done((bf16[272,128]{1,0:T(8,128)(2,1)S(1)}, bf16[272,128]{1,0:T(8,128)(2,1)S(1)}, u32[]{:S(2)}, u32[]{:S(2)}) %collective-permute-start.7) | collective-permute-done | bytes 69664 | tf_op jit(solution)/shard_map/ppermute | solution.py:344
  32.8 0.1 combine.1.refs_0_
  33.0 1.4 %collective-permute-start.10 = (bf16[128,256]{1,0:T(8,128)(2,1)S(1)}, bf16[128,256]{1,0:T(8,128)(2,1)S(1)}, u32[]{:S(2)}, u32[]{:S(2)}) collective-permute-start(bf16[128,256]{1,0:T(8,128)(2,1)S(1)} %combine.1.refs_0_), channel_id=1, source_target_pairs={{0,8},{4,12},{8,0},{12,4},{1,9},{5,13},{9,1},{13,5},{2,10},{6,14},... | collective-permute-start | bytes 196616 | tf_op jit(solution)/shard_map/ppermute | solution.py:344
  34.4 2.5 %collective-permute-start.11 = (bf16[128,256]{1,0:T(8,128)(2,1)S(1)}, bf16[128,256]{1,0:T(8,128)(2,1)S(1)}, u32[]{:S(2)}, u32[]{:S(2)}) collective-permute-start(bf16[128,256]{1,0:T(8,128)(2,1)S(1)} %combine.1.refs_0_), channel_id=1, source_target_pairs={{0,12},{4,8},{8,4},{12,0},{1,13},{5,9},{9,5},{13,1},{2,14},{6,10},... | collective-permute-start | bytes 196616 | tf_op jit(solution)/shard_map/ppermute | solution.py:344
  36.9 1.3 %collective-permute-done.10.refs_2_ = bf16[128,256]{1,0:T(8,128)(2,1)S(1)} collective-permute-done((bf16[128,256]{1,0:T(8,128)(2,1)S(1)}, bf16[128,256]{1,0:T(8,128)(2,1)S(1)}, u32[]{:S(2)}, u32[]{:S(2)}) %collective-permute-start.10) | collective-permute-done | bytes 65568 | tf_op jit(solution)/shard_map/ppermute | solution.py:344
  38.2 2.3 %collective-permute-done.11.refs_3_ = bf16[128,256]{1,0:T(8,128)(2,1)S(1)} collective-permute-done((bf16[128,256]{1,0:T(8,128)(2,1)S(1)}, bf16[128,256]{1,0:T(8,128)(2,1)S(1)}, u32[]{:S(2)}, u32[]{:S(2)}) %collective-permute-start.11) | collective-permute-done | bytes 65568 | tf_op jit(solution)/shard_map/ppermute | solution.py:344
  40.5 0.7 %collective-permute-done.9.refs_1_ = bf16[128,256]{1,0:T(8,128)(2,1)S(1)} collective-permute-done((bf16[128,256]{1,0:T(8,128)(2,1)S(1)}, bf16[128,256]{1,0:T(8,128)(2,1)S(1)}, u32[]{:S(2)}, u32[]{:S(2)}) %collective-permute-start.9) | collective-permute-done | bytes 65568 | tf_op jit(solution)/shard_map/ppermute | solution.py:344
  41.2 0.2 select.1
  41.5 0.5 %collective-permute-start.13 = (bf16[128,256]{1,0:T(8,128)(2,1)S(1)}, bf16[128,256]{1,0:T(8,128)(2,1)S(1)}, u32[]{:S(2)}, u32[]{:S(2)}) collective-permute-start(bf16[128,256]{1,0:T(8,128)(2,1)S(1)} %get-tuple-element.31), channel_id=1, source_target_pairs={{0,1},{1,0},{2,3},{3,2},{4,5},{5,4},{6,7},{7,6},{8,9},{9,8},{10,11... | collective-permute-start | bytes 196616 | tf_op jit(solution)/shard_map/ppermute | solution.py:358
  42.0 0.5 %collective-permute-start.15 = (bf16[128,256]{1,0:T(8,128)(2,1)S(1)}, bf16[128,256]{1,0:T(8,128)(2,1)S(1)}, u32[]{:S(2)}, u32[]{:S(2)}) collective-permute-start(bf16[128,256]{1,0:T(8,128)(2,1)S(1)} %get-tuple-element.32), channel_id=1, source_target_pairs={{0,2},{1,3},{2,0},{3,1},{4,6},{5,7},{6,4},{7,5},{8,10},{9,11},{10,... | collective-permute-start | bytes 196616 | tf_op jit(solution)/shard_map/ppermute | solution.py:358
  42.5 0.9 %collective-permute-start.16 = (bf16[128,256]{1,0:T(8,128)(2,1)S(1)}, bf16[128,256]{1,0:T(8,128)(2,1)S(1)}, u32[]{:S(2)}, u32[]{:S(2)}) collective-permute-start(bf16[128,256]{1,0:T(8,128)(2,1)S(1)} %get-tuple-element.33), channel_id=1, source_target_pairs={{0,3},{1,2},{2,1},{3,0},{4,7},{5,6},{6,5},{7,4},{8,11},{9,10},{10,... | collective-permute-start | bytes 196616 | tf_op jit(solution)/shard_map/ppermute | solution.py:358
  43.4 0.4 collective-permute-done.13.refs_1_
  43.9 0.4 project_near.1.near_ref
  44.2 2.7 %collective-permute-done.15.refs_0_ = bf16[128,256]{1,0:T(8,128)(2,1)S(1)} collective-permute-done((bf16[128,256]{1,0:T(8,128)(2,1)S(1)}, bf16[128,256]{1,0:T(8,128)(2,1)S(1)}, u32[]{:S(2)}, u32[]{:S(2)}) %collective-permute-start.15) | collective-permute-done | bytes 65568 | tf_op jit(solution)/shard_map/ppermute | solution.py:358
  47.0 1.1 %project.1 = f32[128,1536]{1,0:T(8,128)} custom-call(f32[3,1536]{1,0:T(4,128)S(1)} %copy-done.3, f32[128,1536]{1,0:T(8,128)S(1)} %project_near.1.near_ref, bf16[128,256]{1,0:T(8,128)(2,1)S(1)} %collective-permute-done.15.refs_0_, bf16[128,256]{1,0:T(8,128)(2,1)S(1)} %collective-permute-done.16.refs_1_, bf16[256,1536]{1,0:T(8,128)(2,1)S(1)} %get-tuple-element.34.refs_2_, ...), custom_call_target="tpu_custom_call" | custom-call | flops 201326592 | bytes 3145728 | tf_op jit(solution)/shard_map/project/pallas_call | solution.py:492
  (26 shorter events, 0.3 us)
Async XLA Ops:
  0.0 10.5 %copy-start.5 = (s32[4]{0:T(128)S(1)}, s32[4]{0:T(128)}, u32[]{:S(2)}) copy-start(s32[4]{0:T(128)} %worker_in.5) | copy-start | bytes 52
  0.0 10.5 %copy-start.1 = (bf16[512,256]{1,0:T(8,128)(2,1)S(1)}, bf16[512,256]{1,0:T(8,128)(2,1)}, u32[]{:S(2)}) copy-start(bf16[512,256]{1,0:T(8,128)(2,1)} %cache_in.2) | copy-start | bytes 786436
  0.0 41.2 %collective-permute-start.12 = (bf16[256,1536]{1,0:T(8,128)(2,1)}, bf16[256,1536]{1,0:T(8,128)(2,1)S(1)}, u32[]{:S(2)}, u32[]{:S(2)}) collective-permute-start(bf16[256,1536]{1,0:T(8,128)(2,1)} %refs_2_.1), channel_id=1, source_target_pairs={{0,2},{2,0},{1,3},{3,1},{4,6},{6,4},{5,7},{7,5},{8,10},{10,8},{9,1... | collective-permute-start | bytes 2359304 | tf_op jit(solution)/shard_map/ppermute | solution.py:347
  6.0 9.8 %copy-start.4 = (bf16[128,256]{1,0:T(8,128)(2,1)S(1)}, bf16[128,256]{1,0:T(8,128)(2,1)}, u32[]{:S(2)}) copy-start(bf16[128,256]{1,0:T(8,128)(2,1)} %get-tuple-element.20.refs_0_) | copy-start | bytes 196612
  6.0 7.1 %collective-permute-start = (bf16[128,256]{1,0:T(8,128)(2,1)}, bf16[128,256]{1,0:T(8,128)(2,1)S(1)}, u32[]{:S(2)}, u32[]{:S(2)}) collective-permute-start(bf16[128,256]{1,0:T(8,128)(2,1)} %get-tuple-element.21), channel_id=1, source_target_pairs={{0,12},{4,8},{8,4},{12,0},{1,13},{5,9},{9,5},{13,1},{2,14},{6,10},... | collective-permute-start | bytes 196616 | tf_op jit(solution)/shard_map/ppermute | solution.py:344
  9.7 6.1 %collective-permute-start.1 = (bf16[128,256]{1,0:T(8,128)(2,1)}, bf16[128,256]{1,0:T(8,128)(2,1)S(1)}, u32[]{:S(2)}, u32[]{:S(2)}) collective-permute-start(bf16[128,256]{1,0:T(8,128)(2,1)} %get-tuple-element.22), channel_id=1, source_target_pairs={{0,8},{4,12},{8,0},{12,4},{1,9},{5,13},{9,1},{13,5},{2,10},{6,14},... | collective-permute-start | bytes 196616 | tf_op jit(solution)/shard_map/ppermute | solution.py:344
  9.8 6.0 %collective-permute-start.2 = (bf16[128,256]{1,0:T(8,128)(2,1)}, bf16[128,256]{1,0:T(8,128)(2,1)S(1)}, u32[]{:S(2)}, u32[]{:S(2)}) collective-permute-start(bf16[128,256]{1,0:T(8,128)(2,1)} %get-tuple-element.23), channel_id=1, source_target_pairs={{0,4},{4,0},{8,12},{12,8},{1,5},{5,1},{9,13},{13,9},{2,6},{6,2},{1... | collective-permute-start | bytes 196616 | tf_op jit(solution)/shard_map/ppermute | solution.py:344
  10.5 9.8 %copy-start.2 = (bf16[512,256]{1,0:T(8,128)(2,1)S(1)}, bf16[512,256]{1,0:T(8,128)(2,1)}, u32[]{:S(2)}) copy-start(bf16[512,256]{1,0:T(8,128)(2,1)} %cache_in.3) | copy-start | bytes 786436
  15.8 21.1 %copy-start = (bf16[256,1536]{1,0:T(8,128)(2,1)S(1)}, bf16[256,1536]{1,0:T(8,128)(2,1)}, u32[]{:S(2)}) copy-start(bf16[256,1536]{1,0:T(8,128)(2,1)} %refs_2_.1) | copy-start | bytes 2359300
  15.9 7.6 %collective-permute-start.3 = (bf16[128,256]{1,0:T(8,128)(2,1)S(1)}, bf16[128,256]{1,0:T(8,128)(2,1)S(1)}, u32[]{:S(2)}, u32[]{:S(2)}) collective-permute-start(bf16[128,256]{1,0:T(8,128)(2,1)S(1)} %collect.1._.refs_0_), channel_id=1, source_target_pairs={{0,12},{4,8},{8,4},{12,0},{1,13},{5,9},{9,5},{13,1},{2,14},{6,10},... | collective-permute-start | bytes 196616 | tf_op jit(solution)/shard_map/ppermute | solution.py:344
  18.1 6.0 %collective-permute-start.4 = (bf16[128,256]{1,0:T(8,128)(2,1)S(1)}, bf16[128,256]{1,0:T(8,128)(2,1)S(1)}, u32[]{:S(2)}, u32[]{:S(2)}) collective-permute-start(bf16[128,256]{1,0:T(8,128)(2,1)S(1)} %collect.1._.refs_0_), channel_id=1, source_target_pairs={{0,8},{4,12},{8,0},{12,4},{1,9},{5,13},{9,1},{13,5},{2,10},{6,14},... | collective-permute-start | bytes 196616 | tf_op jit(solution)/shard_map/ppermute | solution.py:344
  18.1 6.0 %collective-permute-start.5 = (bf16[128,256]{1,0:T(8,128)(2,1)S(1)}, bf16[128,256]{1,0:T(8,128)(2,1)S(1)}, u32[]{:S(2)}, u32[]{:S(2)}) collective-permute-start(bf16[128,256]{1,0:T(8,128)(2,1)S(1)} %collect.1._.refs_0_), channel_id=1, source_target_pairs={{0,4},{4,0},{8,12},{12,8},{1,5},{5,1},{9,13},{13,9},{2,6},{6,2},{1... | collective-permute-start | bytes 196616 | tf_op jit(solution)/shard_map/ppermute | solution.py:344
  25.2 6.2 %collective-permute-start.6 = (bf16[272,128]{1,0:T(8,128)(2,1)S(1)}, bf16[272,128]{1,0:T(8,128)(2,1)S(1)}, u32[]{:S(2)}, u32[]{:S(2)}) collective-permute-start(bf16[272,128]{1,0:T(8,128)(2,1)S(1)} %get-tuple-element.26), channel_id=1, source_target_pairs={{0,12},{4,8},{8,4},{12,0},{1,13},{5,9},{9,5},{13,1},{2,14},{6,10},... | collective-permute-start | bytes 208904 | tf_op jit(solution)/shard_map/ppermute | solution.py:344
  26.9 5.9 %collective-permute-start.7 = (bf16[272,128]{1,0:T(8,128)(2,1)S(1)}, bf16[272,128]{1,0:T(8,128)(2,1)S(1)}, u32[]{:S(2)}, u32[]{:S(2)}) collective-permute-start(bf16[272,128]{1,0:T(8,128)(2,1)S(1)} %get-tuple-element.27), channel_id=1, source_target_pairs={{0,8},{4,12},{8,0},{12,4},{1,9},{5,13},{9,1},{13,5},{2,10},{6,14},... | collective-permute-start | bytes 208904 | tf_op jit(solution)/shard_map/ppermute | solution.py:344
  27.2 5.6 %collective-permute-start.8 = (bf16[272,128]{1,0:T(8,128)(2,1)S(1)}, bf16[272,128]{1,0:T(8,128)(2,1)S(1)}, u32[]{:S(2)}, u32[]{:S(2)}) collective-permute-start(bf16[272,128]{1,0:T(8,128)(2,1)S(1)} %get-tuple-element.28), channel_id=1, source_target_pairs={{0,4},{4,0},{8,12},{12,8},{1,5},{5,1},{9,13},{13,9},{2,6},{6,2},{1... | collective-permute-start | bytes 208904 | tf_op jit(solution)/shard_map/ppermute | solution.py:344
  33.0 5.2 %collective-permute-start.10 = (bf16[128,256]{1,0:T(8,128)(2,1)S(1)}, bf16[128,256]{1,0:T(8,128)(2,1)S(1)}, u32[]{:S(2)}, u32[]{:S(2)}) collective-permute-start(bf16[128,256]{1,0:T(8,128)(2,1)S(1)} %combine.1.refs_0_), channel_id=1, source_target_pairs={{0,8},{4,12},{8,0},{12,4},{1,9},{5,13},{9,1},{13,5},{2,10},{6,14},... | collective-permute-start | bytes 196616 | tf_op jit(solution)/shard_map/ppermute | solution.py:344
  34.4 6.2 %collective-permute-start.11 = (bf16[128,256]{1,0:T(8,128)(2,1)S(1)}, bf16[128,256]{1,0:T(8,128)(2,1)S(1)}, u32[]{:S(2)}, u32[]{:S(2)}) collective-permute-start(bf16[128,256]{1,0:T(8,128)(2,1)S(1)} %combine.1.refs_0_), channel_id=1, source_target_pairs={{0,12},{4,8},{8,4},{12,0},{1,13},{5,9},{9,5},{13,1},{2,14},{6,10},... | collective-permute-start | bytes 196616 | tf_op jit(solution)/shard_map/ppermute | solution.py:344
  36.9 4.3 %collective-permute-start.9 = (bf16[128,256]{1,0:T(8,128)(2,1)S(1)}, bf16[128,256]{1,0:T(8,128)(2,1)S(1)}, u32[]{:S(2)}, u32[]{:S(2)}) collective-permute-start(bf16[128,256]{1,0:T(8,128)(2,1)S(1)} %combine.1.refs_0_), channel_id=1, source_target_pairs={{0,4},{4,0},{8,12},{12,8},{1,5},{5,1},{9,13},{13,9},{2,6},{6,2},{1... | collective-permute-start | bytes 196616 | tf_op jit(solution)/shard_map/ppermute | solution.py:344
  36.9 6.5 %collective-permute-start.14 = (bf16[256,1536]{1,0:T(8,128)(2,1)S(1)}, bf16[256,1536]{1,0:T(8,128)(2,1)S(1)}, u32[]{:S(2)}, u32[]{:S(2)}) collective-permute-start(bf16[256,1536]{1,0:T(8,128)(2,1)S(1)} %copy-done), channel_id=1, source_target_pairs={{0,1},{1,0},{2,3},{3,2},{4,5},{5,4},{6,7},{7,6},{8,9},{9,8},{10,11... | collective-permute-start | bytes 2359304 | tf_op jit(solution)/shard_map/ppermute | solution.py:350
  41.2 5.7 %copy-start.3 = (f32[3,1536]{1,0:T(4,128)S(1)}, f32[3,1536]{1,0:T(4,128)}, u32[]{:S(2)}) copy-start(f32[3,1536]{1,0:T(4,128)} %modulation_ref.1) | copy-start | bytes 55300
  41.4 5.5 %collective-permute-start.17 = (bf16[256,1536]{1,0:T(8,128)(2,1)S(1)}, bf16[256,1536]{1,0:T(8,128)(2,1)S(1)}, u32[]{:S(2)}, u32[]{:S(2)}) collective-permute-start(bf16[256,1536]{1,0:T(8,128)(2,1)S(1)} %get-tuple-element.34.refs_2_), channel_id=1, source_target_pairs={{0,1},{1,0},{2,3},{3,2},{4,5},{5,4},{6,7},{7,6},{8,9},{9,8},{10,11... | collective-permute-start | bytes 2359304 | tf_op jit(solution)/shard_map/ppermute | solution.py:350
  41.5 2.4 %collective-permute-start.13 = (bf16[128,256]{1,0:T(8,128)(2,1)S(1)}, bf16[128,256]{1,0:T(8,128)(2,1)S(1)}, u32[]{:S(2)}, u32[]{:S(2)}) collective-permute-start(bf16[128,256]{1,0:T(8,128)(2,1)S(1)} %get-tuple-element.31), channel_id=1, source_target_pairs={{0,1},{1,0},{2,3},{3,2},{4,5},{5,4},{6,7},{7,6},{8,9},{9,8},{10,11... | collective-permute-start | bytes 196616 | tf_op jit(solution)/shard_map/ppermute | solution.py:358
  42.0 4.9 %collective-permute-start.15 = (bf16[128,256]{1,0:T(8,128)(2,1)S(1)}, bf16[128,256]{1,0:T(8,128)(2,1)S(1)}, u32[]{:S(2)}, u32[]{:S(2)}) collective-permute-start(bf16[128,256]{1,0:T(8,128)(2,1)S(1)} %get-tuple-element.32), channel_id=1, source_target_pairs={{0,2},{1,3},{2,0},{3,1},{4,6},{5,7},{6,4},{7,5},{8,10},{9,11},{10,... | collective-permute-start | bytes 196616 | tf_op jit(solution)/shard_map/ppermute | solution.py:358
  42.5 4.4 %collective-permute-start.16 = (bf16[128,256]{1,0:T(8,128)(2,1)S(1)}, bf16[128,256]{1,0:T(8,128)(2,1)S(1)}, u32[]{:S(2)}, u32[]{:S(2)}) collective-permute-start(bf16[128,256]{1,0:T(8,128)(2,1)S(1)} %get-tuple-element.33), channel_id=1, source_target_pairs={{0,3},{1,2},{2,1},{3,0},{4,7},{5,6},{6,5},{7,4},{8,11},{9,10},{10,... | collective-permute-start | bytes 196616 | tf_op jit(solution)/shard_map/ppermute | solution.py:358
